TPU v7x, 128 devices: a whole 4x4x4 slice. The times are simulated.
128 devices in a mesh: rep: 4 (over y), shard: 32 (over x, z, core).
Axes of the slice: x: 4, y: 4, z: 4, core: 2. Of those that a mesh axis runs over, the one named last changes fastest.
Arguments:
- embed_table: bfloat16 [262144, 128], P('shard'), may hold values from -6 to 6
- row_ids: int32 [128, 8192], P(('rep', 'shard')), may hold values from 0 to 1023
- row_owner: int32 [128, 8192, 1], P(('rep', 'shard')), may hold values from 0 to 31; in each aligned block of 8192 rows (0 to 8191, 8192 to 16383, ..., all dimensions but the last counted through in order) at most 512 rows name the same one
- lengths: int32 [128, 1024], P(('rep', 'shard')), may hold values from 1 to 200, 8192 in all within a row
- feature_slot: int32 [32, 8], replicated, may hold values from 0 to 7, each once within a row
- labels: int32 [16384], P(('rep', 'shard')), may hold values 0 or 1
- norm_gain: float32 [1024], replicated, may hold values from 0.1 to 1.9
- cross_weight: bfloat16 [3, 1024, 1024], replicated, may hold values from -0.1875 to 0.1875
- cross_bias: float32 [3, 1024], replicated, may hold values from -3 to 3
- deep_weight: bfloat16 [3, 1024, 1024], replicated, may hold values from -0.1875 to 0.1875
- deep_bias: float32 [3, 1024], replicated, may hold values from -3 to 3
- out_weight: float32 [1024], replicated, may hold values from -0.1875 to 0.1875
Outputs:
- row_grad: float32 [262144, 128], P('shard')
- first_grad: float32 [1024, 1024], replicated
- logits: float32 [16384], P(('rep', 'shard'))
Inputs may be any that keep to these rules, and one draw needn't show every extreme that they name: `row_owner`: among one device's ids, at most 512 have the same owner, and in every draw some device sends exactly 512 to some owner. Each device's 1024 lengths sum to 8192; the largest is 200. `feature_slot`: each row holds each of 0 to 7 once.
All inputs are finite; a program needn't handle non-finite values. No bound on the sum of `labels` on one device may be relied on, other than what follows from the above.
Results may differ from a plain program's by a relative error of at most 0.035.
Values may be sent and summed in bfloat16 or wider, within the bound.
No kernel may reach another device: no remote copies, remote signals or barrier semaphores. Data moves between devices by JAX's collectives and lax.ppermute only.
A program may use at most 128 MiB of HBM per device.

v0:
```python
import functools

import jax
import jax.numpy as jnp
import numpy as np
from jax import lax
from jax.experimental import pallas as pl
from jax.experimental.pallas import tpu as pltpu
from jax.sharding import PartitionSpec as P

BF = jnp.bfloat16
F32 = jnp.float32
I32 = jnp.int32
OWNERS = 32
FEATS = 8
KEYS = OWNERS * FEATS
CAP = 512
VOC = 1024
ROWS = FEATS * VOC
EMB = 128
BAGS = 1024
SAMPLES = 128
WIDTH = FEATS * EMB
IDS = 8192
REPS = 4
PAIR = FEATS // REPS
LANES = 256
IDROWS = IDS // LANES
ACCS = 16
POOLED = 8
GROUP = 8
SOURCES = GROUP * REPS * PAIR * SAMPLES
SHIFT = 13
EARLY = 256
VMEM = 56 * 1024 * 1024

NT = (((1,), (1,)), ((), ()))
TN = (((0,), (0,)), ((), ()))


def dot(a, b, dims=(((1,), (0,)), ((), ()))):
    return lax.dot_general(a, b, dims, preferred_element_type=F32)


def iota(shape, dim):
    return lax.broadcasted_iota(I32, shape, dim)


def onehot(cond):
    return jnp.where(cond, 1.0, 0.0).astype(BF)


def index_kernel(
    ids_in, owner_in, len_in, slot_ref, out_ref, ids_ref, owner_ref, len_ref, bag_ref, key_ref
):
    for r in range(IDROWS):
        ids_ref[r : r + 1, :] = ids_in[:, r * LANES : (r + 1) * LANES]
        owner_ref[r : r + 1, :] = owner_in[:, r * LANES : (r + 1) * LANES]
    for r in range(BAGS // 128):
        len_ref[r : r + 1, :] = len_in[:, r * 128 : (r + 1) * 128]
    lens = len_ref[...].astype(F32).astype(BF)
    incl128 = onehot(iota((128, 128), 0) <= iota((128, 128), 1))
    within = dot(lens, incl128)
    total = jnp.broadcast_to(within[:, 127:128], (8, 128))
    high = jnp.floor(total * (1.0 / 256.0))
    low = total - high * 256.0
    below8 = onehot(iota((8, 8), 1) < iota((8, 8), 0))
    before = dot(below8, high.astype(BF)) * 256.0 + dot(below8, low.astype(BF))
    start = (within + before).astype(I32) - len_ref[...]
    start_hi = start >> 8
    start_lo = start & 255
    marks = jnp.zeros((IDROWS, LANES), F32)
    for r in range(8):
        a = onehot(iota((IDROWS, 128), 0) == start_hi[r : r + 1, :])
        b = onehot(iota((LANES, 128), 0) == start_lo[r : r + 1, :])
        marks = marks + dot(a, b, NT)
    marks = marks.astype(BF)
    incl = onehot(iota((LANES, LANES), 0) <= iota((LANES, LANES), 1))
    strict = onehot(iota((LANES, LANES), 0) < iota((LANES, LANES), 1))
    row_counts = dot(marks, jnp.ones((LANES, LANES), BF))
    below = onehot(iota((IDROWS, IDROWS), 1) < iota((IDROWS, IDROWS), 0))
    bag = (dot(marks, incl) + dot(below, row_counts.astype(BF))).astype(I32) - 1
    bag_ref[...] = bag
    key_ref[...] = owner_ref[...] * FEATS + (bag & (FEATS - 1))

    key_iota = iota((KEYS, LANES), 0)

    def count(r, acc):
        return acc + jnp.where(key_iota == key_ref[pl.ds(r, 1), :], 1.0, 0.0)

    counts = lax.fori_loop(0, IDROWS, count, jnp.zeros((KEYS, LANES), F32), unroll=4)
    totals = dot(counts.astype(BF), jnp.ones((LANES, LANES), BF))
    high = jnp.floor(totals * (1.0 / 256.0))
    low = totals - high * 256.0
    ki, kj = iota((KEYS, KEYS), 0), iota((KEYS, KEYS), 1)
    earlier = onehot((ki // FEATS == kj // FEATS) & (kj < ki))
    carry0 = dot(earlier, high.astype(BF)) * 256.0 + dot(earlier, low.astype(BF))

    rank_iota = iota((CAP, LANES), 0)
    owner_iota = iota((OWNERS, LANES), 0)

    of_owner = onehot(iota((KEYS, OWNERS), 0) // FEATS == iota((KEYS, OWNERS), 1))
    by_owner = dot(of_owner, slot_ref[...].astype(F32).astype(BF))
    is_feature = (iota((KEYS, FEATS), 0) & (FEATS - 1)) == iota((KEYS, FEATS), 1)
    slots = jnp.sum(jnp.where(is_feature, by_owner, 0.0), axis=1, keepdims=True)
    carry0 = carry0 + jnp.broadcast_to(slots, (KEYS, LANES)) * VOC

    def place(r, state):
        carry, acc = state
        same = key_iota == key_ref[pl.ds(r, 1), :]
        hot = jnp.where(same, 1.0, 0.0)
        prefix = dot(hot.astype(BF), strict)
        found = jnp.sum(jnp.where(same, prefix + carry, 0.0), axis=0, keepdims=True)
        found = found.astype(I32)
        rank = found & (VOC - 1)
        row = (found - rank) + ids_ref[pl.ds(r, 1), :]
        value = (1 << 23) + (row << 10) + bag_ref[pl.ds(r, 1), :]
        mine = owner_iota == owner_ref[pl.ds(r, 1), :]
        pieces = [
            jnp.where(mine, jnp.broadcast_to(p.astype(F32), (OWNERS, LANES)), 0.0)
            for p in (value & 255, (value >> 8) & 255, value >> 16)
        ]
        left = jnp.concatenate(pieces, axis=0).astype(BF)
        right = onehot(rank_iota == rank)
        acc = acc + dot(left, right, NT)
        carry = carry + (prefix + hot)[:, LANES - 1 : LANES]
        return carry, acc

    _, acc = lax.fori_loop(
        0, IDROWS, place, (carry0, jnp.zeros((3 * OWNERS, CAP), F32)), unroll=8
    )
    acc = acc.astype(I32)
    out_ref[...] = (
        acc[:OWNERS] + (acc[OWNERS : 2 * OWNERS] << 8) + (acc[2 * OWNERS :] << 16)
    )


def index_call(ids, owners, lengths, slots):
    return pl.pallas_call(
        index_kernel,
        out_shape=jax.ShapeDtypeStruct((OWNERS, CAP), I32),
        scratch_shapes=[
            pltpu.VMEM((IDROWS, LANES), I32),
            pltpu.VMEM((IDROWS, LANES), I32),
            pltpu.VMEM((BAGS // 128, 128), I32),
            pltpu.VMEM((IDROWS, LANES), I32),
            pltpu.VMEM((IDROWS, LANES), I32),
        ],
        compiler_params=pltpu.CompilerParams(vmem_limit_bytes=VMEM),
        name="index",
    )(ids, owners, lengths, slots)


def gather_kernel(row_ref, table_ref, out_ref, wide, picked):
    step = pl.program_id(0)
    depth = out_ref.shape[1]

    @pl.when(step == 0)
    def _():
        wide[...] = table_ref[...].astype(F32)

    base = step * depth

    def some(i, _):
        at = i * 32
        rows = [wide[pl.ds(row_ref[base + at + j], 1), :] for j in range(32)]
        for j in range(32):
            picked[pl.ds(at + j, 1), :] = rows[j]
        return 0

    lax.fori_loop(0, depth // 32, some, 0)
    out_ref[0] = picked[...].astype(BF)


def gather_call(rows, table):
    depth = rows.shape[1]
    return pl.pallas_call(
        gather_kernel,
        out_shape=jax.ShapeDtypeStruct((OWNERS, depth, EMB), BF),
        grid_spec=pltpu.PrefetchScalarGridSpec(
            num_scalar_prefetch=1,
            grid=(OWNERS,),
            in_specs=[pl.BlockSpec((ROWS, EMB), lambda i, r: (0, 0))],
            out_specs=pl.BlockSpec((1, depth, EMB), lambda i, r: (i, 0, 0)),
            scratch_shapes=[pltpu.VMEM((ROWS, EMB), F32), pltpu.VMEM((depth, EMB), F32)],
        ),
        compiler_params=pltpu.CompilerParams(vmem_limit_bytes=VMEM),
        name="gather",
    )(rows.reshape(-1), table)


def sums_of(packed_ref, got_ref, step, at):
    rows, masked = [], []
    depth = got_ref.shape[1]
    for i in range(POOLED):
        packed = packed_ref[pl.ds(step * POOLED + i, 1), at : at + depth]
        bag = packed & (BAGS - 1)
        sample = jnp.where(packed > 0, bag >> 3, -1)
        rows.append(onehot(iota((SAMPLES, depth), 0) == sample))
        feature = jnp.broadcast_to((bag & (FEATS - 1)).astype(F32), (EMB, depth)).T.astype(BF)
        own = got_ref[i]
        masked.append(
            jnp.concatenate(
                [jnp.where(feature == f, own, jnp.zeros((), BF)) for f in range(FEATS)], axis=1
            )
        )
    return dot(jnp.concatenate(rows, axis=1), jnp.concatenate(masked, axis=0))


def pool_kernel(at, got_ref, packed_ref, out_ref):
    step = pl.program_id(0)
    sums = sums_of(packed_ref, got_ref, step, at)

    @pl.when(step == 0)
    def _():
        out_ref[...] = sums

    @pl.when(step > 0)
    def _():
        out_ref[...] += sums


def pool_call(got, packed, at):
    depth = got.shape[1]
    return pl.pallas_call(
        functools.partial(pool_kernel, at),
        out_shape=jax.ShapeDtypeStruct((SAMPLES, WIDTH), F32),
        grid=(OWNERS // POOLED,),
        in_specs=[
            pl.BlockSpec((POOLED, depth, EMB), lambda i: (i, 0, 0)),
            pl.BlockSpec((OWNERS, CAP), lambda i: (0, 0)),
        ],
        out_specs=pl.BlockSpec((SAMPLES, WIDTH), lambda i: (0, 0)),
        compiler_params=pltpu.CompilerParams(vmem_limit_bytes=VMEM),
        name="pool",
    )(got, packed)


def sigmoid(x):
    return 1.0 / (1.0 + jnp.exp(-x))


def tower_kernel(
    at,
    got_ref,
    packed_ref,
    earlier_ref,
    labels_ref,
    gain_ref,
    cbias_ref,
    dbias_ref,
    out_w_ref,
    cross_hbm,
    deep_hbm,
    logits_ref,
    grads_ref,
    first_ref,
    pooled_ref,
    cross_w,
    deep_w,
    start_ref,
    cross_t,
    deep_t,
    gx_ref,
    sems,
):
    step = pl.program_id(0)

    def copies():
        out = []
        for layer in range(3):
            out.append(
                pltpu.make_async_copy(cross_hbm.at[layer], cross_w.at[layer], sems.at[layer])
            )
            out.append(
                pltpu.make_async_copy(deep_hbm.at[layer], deep_w.at[layer], sems.at[3 + layer])
            )
        return out

    @pl.when(step == 0)
    def _():
        for copy in copies():
            copy.start()
        pooled_ref[...] = earlier_ref[...]

    pooled_ref[...] += sums_of(packed_ref, got_ref, step, at)

    @pl.when(step == OWNERS // POOLED - 1)
    def _():
        for copy in copies():
            copy.wait()
        gain = gain_ref[...]
        pooled = pooled_ref[...]
        inverse = lax.rsqrt(jnp.mean(pooled * pooled, axis=1, keepdims=True) + 1e-06)
        start = (pooled * inverse * gain).astype(BF)
        start_ref[...] = start
        current = start
        for layer in range(3):
            product = dot(current, cross_w[layer]) + cbias_ref[layer : layer + 1, :]
            cross_t[layer] = product
            current = (start_ref[...].astype(F32) * product + current.astype(F32)).astype(BF)
        for layer in range(3):
            product = dot(current, deep_w[layer]) + dbias_ref[layer : layer + 1, :]
            deep_t[layer] = product
            current = (product * sigmoid(product)).astype(BF)
        out_w = out_w_ref[...]
        logits = jnp.sum(current.astype(F32) * out_w, axis=1, keepdims=True)
        logits_ref[...] = logits
        error = sigmoid(logits) - labels_ref[...].astype(F32)
        grad = error * out_w
        for layer in (2, 1, 0):
            product = deep_t[layer]
            sig = sigmoid(product)
            masked = (grad * sig * (1.0 + product * (1.0 - sig))).astype(BF)
            grad = dot(masked, deep_w[layer], NT)
        gx_ref[...] = jnp.zeros_like(gx_ref)
        for layer in (2, 1, 0):
            crossed = (grad * start_ref[...].astype(F32)).astype(BF)
            gx_ref[...] += grad * cross_t[layer]
            grad = grad + dot(crossed, cross_w[layer], NT)
            if layer == 0:
                first_ref[...] = dot(start_ref[...], crossed, TN).astype(BF)
        scaled = (gx_ref[...] + grad) * gain
        pooled = pooled_ref[...]
        inverse = lax.rsqrt(jnp.mean(pooled * pooled, axis=1, keepdims=True) + 1e-06)
        mean = jnp.mean(scaled * pooled, axis=1, keepdims=True)
        result = (inverse * scaled - pooled * (inverse * inverse * inverse) * mean).astype(BF)
        for r in range(REPS):
            grads_ref[r] = result[:, r * PAIR * EMB : (r + 1) * PAIR * EMB]


def tower_call(got, packed, earlier, labels, gain, cross, cbias, deep, dbias, out_w):
    def whole(shape):
        return pl.BlockSpec(shape, lambda i: (0,) * len(shape))

    return pl.pallas_call(
        functools.partial(tower_kernel, CAP - got.shape[1]),
        grid=(OWNERS // POOLED,),
        in_specs=[
            pl.BlockSpec((POOLED, got.shape[1], EMB), lambda i: (i, 0, 0)),
            whole((OWNERS, CAP)),
            whole((SAMPLES, WIDTH)),
            whole((SAMPLES, 1)),
            whole((1, WIDTH)),
            whole((3, WIDTH)),
            whole((3, WIDTH)),
            whole((1, WIDTH)),
            pl.BlockSpec(memory_space=pl.ANY),
            pl.BlockSpec(memory_space=pl.ANY),
        ],
        out_specs=[
            whole((SAMPLES, 1)),
            whole((REPS, SAMPLES, PAIR * EMB)),
            whole((WIDTH, WIDTH)),
        ],
        out_shape=[
            jax.ShapeDtypeStruct((SAMPLES, 1), F32),
            jax.ShapeDtypeStruct((REPS, SAMPLES, PAIR * EMB), BF),
            jax.ShapeDtypeStruct((WIDTH, WIDTH), BF),
        ],
        scratch_shapes=[
            pltpu.VMEM((SAMPLES, WIDTH), F32),
            pltpu.VMEM((3, WIDTH, WIDTH), BF),
            pltpu.VMEM((3, WIDTH, WIDTH), BF),
            pltpu.VMEM((SAMPLES, WIDTH), BF),
            pltpu.VMEM((3, SAMPLES, WIDTH), F32),
            pltpu.VMEM((3, SAMPLES, WIDTH), F32),
            pltpu.VMEM((SAMPLES, WIDTH), F32),
            pltpu.SemaphoreType.DMA((6,)),
        ],
        compiler_params=pltpu.CompilerParams(vmem_limit_bytes=VMEM),
        name="tower",
    )(got, packed, earlier, labels, gain, cbias, dbias, out_w, cross, deep)


def scatter_kernel(word_ref, first_ref, last_ref, grads_ref, out_ref, wide, *accs):
    step = pl.program_id(0)

    @pl.when(step == 0)
    def _():
        for acc in accs:
            acc[...] = jnp.zeros_like(acc)

    group = grads_ref.shape[0]
    for g in range(group):
        for r in range(REPS):
            block = grads_ref[g, r]
            base = (g * REPS + r) * PAIR * SAMPLES
            for f in range(PAIR):
                wide[base + f * SAMPLES : base + (f + 1) * SAMPLES, :] = block[
                    :, f * EMB : (f + 1) * EMB
                ].astype(F32)

    def device(k, _):
        listed = (k & (REPS - 1)) * OWNERS + step * group + k // REPS

        def some(i, _):
            at = listed * CAP + i * ACCS
            words = [word_ref[at + j] for j in range(ACCS)]
            rows = [wide[pl.ds(word & (SOURCES - 1), 1), :] for word in words]
            olds = [accs[j][pl.ds(words[j] >> SHIFT, 1), :] for j in range(ACCS)]
            for j in range(ACCS):
                accs[j][pl.ds(words[j] >> SHIFT, 1), :] = olds[j] + rows[j]
            return 0

        lax.fori_loop(first_ref[listed], last_ref[listed], some, 0)
        return 0

    lax.fori_loop(0, group * REPS, device, 0)

    @pl.when(step == pl.num_programs(0) - 1)
    def _():
        total = accs[0][: PAIR * VOC, :]
        for acc in accs[1:]:
            total = total + acc[: PAIR * VOC, :]
        out_ref[...] = total.astype(out_ref.dtype)


def scatter_call(words, first, last, grads, group=GROUP):
    rows = PAIR * VOC
    return pl.pallas_call(
        scatter_kernel,
        out_shape=jax.ShapeDtypeStruct((rows, EMB), BF),
        grid_spec=pltpu.PrefetchScalarGridSpec(
            num_scalar_prefetch=3,
            grid=(OWNERS // group,),
            in_specs=[
                pl.BlockSpec(
                    (group, REPS, SAMPLES, PAIR * EMB), lambda i, *_: (i, 0, 0, 0)
                )
            ],
            out_specs=pl.BlockSpec((rows, EMB), lambda i, *_: (0, 0)),
            scratch_shapes=[pltpu.VMEM((group * REPS * PAIR * SAMPLES, EMB), F32)]
            + [pltpu.VMEM((rows + 8, EMB), F32) for _ in range(ACCS)],
        ),
        compiler_params=pltpu.CompilerParams(vmem_limit_bytes=VMEM),
        name="scatter",
    )(words, first, last, grads)


def finish_kernel(order_ref, *refs):
    parts, rows_ref = refs[:REPS], refs[REPS]
    source = order_ref[pl.program_id(0)]
    for k in range(REPS):

        @pl.when(source // PAIR == k)
        def _():
            rows_ref[...] = parts[k][lax.rem(source, PAIR)].astype(F32)


def finish_call(order, parts):
    return pl.pallas_call(
        finish_kernel,
        out_shape=jax.ShapeDtypeStruct((ROWS, EMB), F32),
        grid_spec=pltpu.PrefetchScalarGridSpec(
            num_scalar_prefetch=1,
            grid=(FEATS,),
            in_specs=[pl.BlockSpec((PAIR, VOC, EMB), lambda i, o: (0, 0, 0)) for _ in parts],
            out_specs=pl.BlockSpec((VOC, EMB), lambda i, o: (i, 0)),
        ),
        compiler_params=pltpu.CompilerParams(vmem_limit_bytes=VMEM),
        name="finish",
    )(order, *parts)


def from_before(x, axis, k):
    if k == 0:
        return x
    n = lax.axis_size(axis)
    return lax.ppermute(x, axis, [(i, (i + k) % n) for i in range(n)])


def summed(x):
    return jnp.sum(x.astype(F32), axis=0).astype(BF)


def body(
    embed_table,
    row_ids,
    row_owner,
    lengths,
    feature_slot,
    labels,
    norm_gain,
    cross_weight,
    cross_bias,
    deep_weight,
    deep_bias,
    out_weight,
):
    packed = index_call(
        row_ids,
        row_owner.reshape(1, IDS),
        lengths,
        feature_slot,
    )
    asked = lax.all_to_all(
        packed.reshape(OWNERS, 4, 128), "shard", split_axis=0, concat_axis=0, tiled=True
    )
    rows = ((asked >> 10) & (ROWS - 1)).reshape(OWNERS, CAP)

    def exchange(x, axis):
        return lax.all_to_all(x, axis, split_axis=0, concat_axis=0, tiled=True)

    picked_early = gather_call(rows[:, :EARLY], embed_table)
    picked_early, lists = lax.optimization_barrier((picked_early, asked))
    got_early = exchange(picked_early, "shard")
    picked_late, lists = lax.optimization_barrier(
        (gather_call(rows[:, EARLY:], embed_table), lists)
    )
    got_late = exchange(picked_late, "shard")

    rep = lax.axis_index("rep")
    everyone = jnp.concatenate(
        [lists] + [from_before(lists, "rep", k) for k in range(1, REPS)]
    ).reshape(REPS * OWNERS, CAP)
    feature = everyone & (FEATS - 1)
    valid = everyone > 0
    within = feature - rep * PAIR
    ours = valid & (within >= 0) & (within < PAIR)
    target = jnp.where(ours, within * VOC + ((everyone >> 10) & (VOC - 1)), PAIR * VOC)
    device = lax.broadcasted_iota(I32, everyone.shape, 0)
    source = ((device & (GROUP - 1)) * REPS + device // OWNERS) * (PAIR * SAMPLES) + jnp.where(
        ours, within * SAMPLES + ((everyone >> 3) & (SAMPLES - 1)), 0
    )
    words = ((target << SHIFT) | source).reshape(-1)
    below = jnp.sum((valid & (within < 0)).astype(I32), axis=1)
    upto = jnp.sum((valid & (within < PAIR)).astype(I32), axis=1)
    first_block = below // ACCS
    last_block = (upto + ACCS - 1) // ACCS
    sums_early = pool_call(got_early, packed, 0)
    got_late, sums_early, words, first_block, last_block = lax.optimization_barrier(
        (got_late, sums_early, words, first_block, last_block)
    )

    logits, grads, first_local = tower_call(
        got_late,
        packed,
        sums_early,
        labels.reshape(SAMPLES, 1),
        norm_gain.reshape(1, WIDTH),
        cross_weight,
        cross_bias,
        deep_weight,
        deep_bias,
        out_weight.reshape(1, WIDTH),
    )
    mine = jnp.stack(
        [
            from_before(lax.dynamic_index_in_dim(grads, (rep + k) % REPS, 0, False), "rep", k)
            for k in range(REPS)
        ]
    )
    mine, first_local = lax.optimization_barrier((mine, first_local))
    all_grads = lax.all_gather(mine, "shard", axis=0)
    eight = summed(
        exchange(first_local.reshape(REPS * OWNERS, 8, WIDTH), ("rep", "shard"))
    )
    first_grad = lax.all_gather(eight, ("rep", "shard"), axis=0, tiled=True).astype(F32)

    part = scatter_call(words, first_block, last_block, all_grads).reshape(PAIR, VOC, EMB)
    parts = [part] + [from_before(part, "rep", k) for k in range(1, REPS)]
    slots = feature_slot[lax.axis_index("shard")]
    feature_of = jnp.argmax(
        slots[None, :] == jnp.arange(FEATS, dtype=I32)[:, None], axis=1
    ).astype(I32)
    order = ((rep - feature_of // PAIR) & (REPS - 1)) * PAIR + feature_of % PAIR
    row_grad = finish_call(order, parts)
    return (row_grad, first_grad, logits.reshape(SAMPLES))


def solution(mesh):
    both = ("rep", "shard")
    in_specs = (
        P("shard", None),
        P(both, None),
        P(both, None, None),
        P(both, None),
        P(),
        P(both),
        P(),
        P(),
        P(),
        P(),
        P(),
        P(),
    )
    out_specs = (P("shard", None), P(), P(both))
    return jax.shard_map(body, mesh=mesh, in_specs=in_specs, out_specs=out_specs, check_vma=False)
```

profile of v0, /device:TPU:38, one launch (start us, length us, event | category | flops | bytes accessed | tf_op | source)
XLA Modules:
  0.0 324.5 jit_solution(16648091472546023767)
XLA Ops:
  7.2 1.4 copy.21.slot_ref
  8.5 15.3 %index.1.packed_ref = s32[32,512]{1,0:T(8,128)} custom-call(s32[1,8192]{1,0:T(1,128)} %ids_in.1, s32[1,8192]{1,0:T(1,128)} %bitcast.47, s32[1,1024]{1,0:T(1,128)} %len_in.1, s32[32,8]{1,0:T(8,128)} %copy.21.slot_ref), custom_call_target="tpu_custom_call" | custom-call | tf_op jit(solution)/shard_map/index/pallas_call | solution.py:139
  24.7 12.5 %all_to_all.20 = s32[32,4,128]{2,1,0:T(4,128)S(1)} all-to-all(s32[32,4,128]{2,1,0:T(4,128)S(1)} %reshape.80), channel_id=1, replica_groups=mesh['rep'=4,'shard'=32] {'shard'}, dimensions={0} | all-to-all | bytes 131072 | tf_op jit(solution)/shard_map/all_to_all | solution.py:497
  37.9 17.3 %gather.3 = bf16[32,256,128]{2,1,0:T(8,128)(2,1)} custom-call(s32[8192]{0:T(1024)} %bitcast.42, bf16[8192,128]{1,0:T(8,128)(2,1)} %table_ref.3), custom_call_target="tpu_custom_call" | custom-call | tf_op jit(solution)/shard_map/gather/pallas_call | solution.py:177
  55.2 7.0 %all-to-all-start.2 = ((bf16[32,256,128]{2,1,0:T(8,128)(2,1)}), bf16[32,256,128]{2,1,0:T(8,128)(2,1)S(1)}, u32[]{:S(2)}, u32[]{:S(2)}) async-start(bf16[32,256,128]{2,1,0:T(8,128)(2,1)} %gather.3), calls=%async_computation.2 | async-start | bytes 4194304 | tf_op jit(solution)/shard_map/all_to_all | solution.py:503
  63.9 17.3 %gather.2 = bf16[32,256,128]{2,1,0:T(8,128)(2,1)} custom-call(s32[8192]{0:T(1024)} %bitcast.43, bf16[8192,128]{1,0:T(8,128)(2,1)} %table_ref.3), custom_call_target="tpu_custom_call" | custom-call | tf_op jit(solution)/shard_map/gather/pallas_call | solution.py:177
  81.2 3.0 collective-permute-start.2
  85.8 5.2 %collective-permute-done = s32[32,4,128]{2,1,0:T(4,128)S(1)} collective-permute-done((s32[32,4,128]{2,1,0:T(4,128)S(1)}, s32[32,4,128]{2,1,0:T(4,128)S(1)}, u32[]{:S(2)}, u32[]{:S(2)}) %collective-permute-start) | collective-permute-done | bytes 65568 | tf_op jit(solution)/shard_map/ppermute | solution.py:470
  91.0 4.8 %convert_reduce_fusion = (s32[128]{0:T(128)S(1)}, s32[128]{0:T(128)S(1)}, s32[128,4,128]{2,1,0:T(4,128)S(1)}, s32[128,4,128]{2,1,0:T(4,128)S(1)}) fusion(s32[128,4,128]{2,1,0:T(4,128)S(1)} %constant_dynamic-update-slice_fusion, s32[]{:T(128)S(6)} %mul.42), kind=kLoop, calls=%fused_computation.2 | loop fusion | flops 1638144 | bytes 787460 | tf_op jit(solution)/shard_map/reduce_sum | solution.py:528
  97.2 7.4 %all-to-all-start.1 = ((bf16[32,256,128]{2,1,0:T(8,128)(2,1)}), bf16[32,256,128]{2,1,0:T(8,128)(2,1)S(1)}, u32[]{:S(2)}, u32[]{:S(2)}) async-start(bf16[32,256,128]{2,1,0:T(8,128)(2,1)} %gather.2), calls=%async_computation.1 | async-start | bytes 4194304 | tf_op jit(solution)/shard_map/all_to_all | solution.py:503
  106.2 5.5 %pool.1.earlier_ref = f32[128,1024]{1,0:T(8,128)} custom-call(bf16[32,256,128]{2,1,0:T(8,128)(2,1)} %copy-done.1, s32[32,512]{1,0:T(8,128)} %index.1.packed_ref), custom_call_target="tpu_custom_call" | custom-call | tf_op jit(solution)/shard_map/pool/pallas_call | solution.py:225
  111.7 17.9 %all-to-all-done.1.got_ref = bf16[32,256,128]{2,1,0:T(8,128)(2,1)S(1)} async-done(((bf16[32,256,128]{2,1,0:T(8,128)(2,1)}), bf16[32,256,128]{2,1,0:T(8,128)(2,1)S(1)}, u32[]{:S(2)}, u32[]{:S(2)}) %all-to-all-start.1) | async-done | bytes 2097184 | tf_op jit(solution)/shard_map/all_to_all | solution.py:503
  129.6 1.3 copy-done
  130.9 16.7 %tower.1 = (f32[128,1]{1,0:T(8,128)}, bf16[4,128,256]{2,1,0:T(8,128)(2,1)}, bf16[1024,1024]{1,0:T(8,128)(2,1)}) custom-call(bf16[32,256,128]{2,1,0:T(8,128)(2,1)} %copy-done, s32[32,512]{1,0:T(8,128)} %index.1.packed_ref, f32[128,1024]{1,0:T(8,128)} %pool.1.earlier_ref, s32[128,1]{1,0:T(8,128)} %copy.22.labels_ref, f32[1,1024]{1,0:T(1,128)} %bitcast.48, ...), custom_call_target="tpu_custom_call" | custom-call | tf_op jit(solution)/shard_map/tower/pallas_call | solution.py:336
  151.1 2.4 collective-permute-done.5
  153.4 1.6 collective-permute-done.4
  156.7 38.7 %all_to_all.21 = bf16[128,8,1024]{2,1,0:T(8,128)(2,1)S(1)} all-to-all(bf16[128,8,1024]{2,1,0:T(8,128)(2,1)} %bitcast.36), channel_id=1, replica_groups=mesh['rep'=4,'shard'=32] {'rep','shard'}, dimensions={0} | all-to-all | bytes 4194304 | tf_op jit(solution)/shard_map/all_to_all | solution.py:503
  196.4 29.3 %all-gather.6.cloned.1.call-done = bf16[128,128,256]{2,1,0:T(8,128)(2,1)} async-done(((bf16[4,128,256]{2,1,0:T(8,128)(2,1)}), bf16[128,128,256]{2,1,0:T(8,128)(2,1)}) %all-gather.6.cloned.1.call-update) | async-done | bytes 8388624 | tf_op jit(solution)/shard_map/all_gather | solution.py:555
  225.8 25.9 %scatter.1 = bf16[2048,128]{1,0:T(8,128)(2,1)} custom-call(s32[65536]{0:T(1024)} %add_or_fusion.word_ref, s32[128]{0:T(128)} %get-tuple-element.24.first_ref, s32[128]{0:T(128)} %get-tuple-element.25.last_ref, bf16[32,4,128,256]{3,2,1,0:T(8,128)(2,1)} %bitcast.31), custom_call_target="tpu_custom_call" | custom-call | tf_op jit(solution)/shard_map/scatter/pallas_call | solution.py:421
  251.7 4.2 %collective-permute-start.8 = (bf16[2,1024,128]{2,1,0:T(8,128)(2,1)}, bf16[2,1024,128]{2,1,0:T(8,128)(2,1)S(1)}, u32[]{:S(2)}, u32[]{:S(2)}) collective-permute-start(bf16[2,1024,128]{2,1,0:T(8,128)(2,1)} %bitcast.32), channel_id=1, source_target_pairs={{0,96},{32,0},{64,32},{96,64},{1,97},{33,1},{65,33},{97,65},{2,98}... | collective-permute-start | bytes 1572872 | tf_op jit(solution)/shard_map/ppermute | solution.py:470
  257.2 1.4 collective-permute-start.6
  260.6 45.5 %all-gather.4.cloned.1.call-done = bf16[1024,1024]{1,0:T(8,128)(2,1)} async-done(((bf16[8,1024]{1,0:T(8,128)(2,1)}), bf16[1024,1024]{1,0:T(8,128)(2,1)}) %all-gather.4.cloned.1.call-update) | async-done | bytes 2097168 | tf_op jit(solution)/shard_map/all_gather | solution.py:559
  306.1 4.1 %convert_element_type.15 = f32[1024,1024]{1,0:T(8,128)} convert(bf16[1024,1024]{1,0:T(8,128)(2,1)} %all-gather.4.cloned.1.call-done) | non-fusion elementwise | flops 1048576 | bytes 6291456 | tf_op jit(solution)/shard_map/convert_element_type | solution.py:559
  311.9 5.7 %finish.1 = f32[8192,128]{1,0:T(8,128)} custom-call(s32[8]{0:T(128)} %fusion.6.order_ref, bf16[2,1024,128]{2,1,0:T(8,128)(2,1)} %bitcast.35, bf16[2,1024,128]{2,1,0:T(8,128)(2,1)} %copy-done.4, bf16[2,1024,128]{2,1,0:T(8,128)(2,1)} %copy-done.3, bf16[2,1024,128]{2,1,0:T(8,128)(2,1)} %copy-done.2), custom_call_target="tpu_custom_call" | custom-call | tf_op jit(solution)/shard_map/finish/pallas_call | solution.py:452
  (57 shorter events, 18.7 us)
Async XLA Ops:
  55.2 7.0 %copy-start.7 = (s32[128]{0:T(128)S(1)}, s32[128]{0:T(128)}, u32[]{:S(2)}) copy-start(s32[128]{0:T(128)} %param.17) | copy-start | bytes 1540
  55.2 40.7 %all-to-all-start.2 = ((bf16[32,256,128]{2,1,0:T(8,128)(2,1)}), bf16[32,256,128]{2,1,0:T(8,128)(2,1)S(1)}, u32[]{:S(2)}, u32[]{:S(2)}) async-start(bf16[32,256,128]{2,1,0:T(8,128)(2,1)} %gather.3), calls=%async_computation.2 | async-start | bytes 4194304 | tf_op jit(solution)/shard_map/all_to_all | solution.py:503
  81.2 9.8 %collective-permute-start.2 = (s32[32,4,128]{2,1,0:T(4,128)S(1)}, s32[32,4,128]{2,1,0:T(4,128)S(1)}, u32[]{:S(2)}, u32[]{:S(2)}) collective-permute-start(s32[32,4,128]{2,1,0:T(4,128)S(1)} %all_to_all.20), channel_id=1, source_target_pairs={{0,96},{32,0},{64,32},{96,64},{1,97},{33,1},{65,33},{97,65},{2,98}... | collective-permute-start | bytes 196616 | tf_op jit(solution)/shard_map/ppermute | solution.py:470
  84.2 6.8 %collective-permute-start.1 = (s32[32,4,128]{2,1,0:T(4,128)S(1)}, s32[32,4,128]{2,1,0:T(4,128)S(1)}, u32[]{:S(2)}, u32[]{:S(2)}) collective-permute-start(s32[32,4,128]{2,1,0:T(4,128)S(1)} %all_to_all.20), channel_id=1, source_target_pairs={{0,64},{32,96},{64,0},{96,32},{1,65},{33,97},{65,1},{97,33},{2,66}... | collective-permute-start | bytes 196616 | tf_op jit(solution)/shard_map/ppermute | solution.py:470
  84.8 6.1 %collective-permute-start = (s32[32,4,128]{2,1,0:T(4,128)S(1)}, s32[32,4,128]{2,1,0:T(4,128)S(1)}, u32[]{:S(2)}, u32[]{:S(2)}) collective-permute-start(s32[32,4,128]{2,1,0:T(4,128)S(1)} %all_to_all.20), channel_id=1, source_target_pairs={{0,32},{32,64},{64,96},{96,0},{1,33},{33,65},{65,97},{97,1},{2,34}... | collective-permute-start | bytes 196616 | tf_op jit(solution)/shard_map/ppermute | solution.py:470
  95.9 1.3 copy-start.1
  97.2 32.4 %all-to-all-start.1 = ((bf16[32,256,128]{2,1,0:T(8,128)(2,1)}), bf16[32,256,128]{2,1,0:T(8,128)(2,1)S(1)}, u32[]{:S(2)}, u32[]{:S(2)}) async-start(bf16[32,256,128]{2,1,0:T(8,128)(2,1)} %gather.2), calls=%async_computation.1 | async-start | bytes 4194304 | tf_op jit(solution)/shard_map/all_to_all | solution.py:503
  104.6 121.2 %all-gather.6.cloned.1.call-start = ((), (), s32[]{:S(2)}) async-start(), calls=%async_computation.5 | async-start | bytes 8650752 | tf_op jit(solution)/shard_map/all_gather | solution.py:555
  129.6 1.3 copy-start
  148.5 4.9 %collective-permute-start.5 = (bf16[128,256]{1,0:T(8,128)(2,1)S(1)}, bf16[128,256]{1,0:T(8,128)(2,1)S(1)}, u32[]{:S(2)}, u32[]{:S(2)}) collective-permute-start(bf16[128,256]{1,0:T(8,128)(2,1)S(1)} %get-tuple-element.36), channel_id=1, source_target_pairs={{0,96},{32,0},{64,32},{96,64},{1,97},{33,1},{65,33},{97,65},{2,98}... | collective-permute-start | bytes 196616 | tf_op jit(solution)/shard_map/ppermute | solution.py:470
  149.2 5.9 %collective-permute-start.4 = (bf16[128,256]{1,0:T(8,128)(2,1)S(1)}, bf16[128,256]{1,0:T(8,128)(2,1)S(1)}, u32[]{:S(2)}, u32[]{:S(2)}) collective-permute-start(bf16[128,256]{1,0:T(8,128)(2,1)S(1)} %get-tuple-element.37), channel_id=1, source_target_pairs={{0,64},{32,96},{64,0},{96,32},{1,65},{33,97},{65,1},{97,33},{2,66}... | collective-permute-start | bytes 196616 | tf_op jit(solution)/shard_map/ppermute | solution.py:470
  149.8 6.1 %collective-permute-start.3 = (bf16[128,256]{1,0:T(8,128)(2,1)S(1)}, bf16[128,256]{1,0:T(8,128)(2,1)S(1)}, u32[]{:S(2)}, u32[]{:S(2)}) collective-permute-start(bf16[128,256]{1,0:T(8,128)(2,1)S(1)} %get-tuple-element.38), channel_id=1, source_target_pairs={{0,32},{32,64},{64,96},{96,0},{1,33},{33,65},{65,97},{97,1},{2,34}... | collective-permute-start | bytes 196616 | tf_op jit(solution)/shard_map/ppermute | solution.py:470
  156.7 149.4 %all-gather.4.cloned.1.call-start = ((), (), s32[]{:S(2)}) async-start(), calls=%async_computation.4 | async-start | bytes 2113536 | tf_op jit(solution)/shard_map/all_gather | solution.py:559
  225.8 32.8 %copy-start.6 = (s32[32,8]{0,1:T(8,128)S(1)}, s32[32,8]{0,1:T(8,128)}, u32[]{:S(2)}) copy-start(s32[32,8]{0,1:T(8,128)} %param.16) | copy-start | bytes 3076
  225.8 34.2 %copy-start.5 = (f32[128,1]{1,0:T(8,128)S(1)}, f32[128,1]{1,0:T(8,128)}, u32[]{:S(2)}) copy-start(f32[128,1]{1,0:T(8,128)} %get-tuple-element.32) | copy-start | bytes 1540
  251.7 58.5 %collective-permute-start.8 = (bf16[2,1024,128]{2,1,0:T(8,128)(2,1)}, bf16[2,1024,128]{2,1,0:T(8,128)(2,1)S(1)}, u32[]{:S(2)}, u32[]{:S(2)}) collective-permute-start(bf16[2,1024,128]{2,1,0:T(8,128)(2,1)} %bitcast.32), channel_id=1, source_target_pairs={{0,96},{32,0},{64,32},{96,64},{1,97},{33,1},{65,33},{97,65},{2,98}... | collective-permute-start | bytes 1572872 | tf_op jit(solution)/shard_map/ppermute | solution.py:470
  255.9 54.2 %collective-permute-start.7 = (bf16[2,1024,128]{2,1,0:T(8,128)(2,1)}, bf16[2,1024,128]{2,1,0:T(8,128)(2,1)S(1)}, u32[]{:S(2)}, u32[]{:S(2)}) collective-permute-start(bf16[2,1024,128]{2,1,0:T(8,128)(2,1)} %bitcast.33), channel_id=1, source_target_pairs={{0,64},{32,96},{64,0},{96,32},{1,65},{33,97},{65,1},{97,33},{2,66}... | collective-permute-start | bytes 1572872 | tf_op jit(solution)/shard_map/ppermute | solution.py:470
  257.2 53.0 %collective-permute-start.6 = (bf16[2,1024,128]{2,1,0:T(8,128)(2,1)}, bf16[2,1024,128]{2,1,0:T(8,128)(2,1)S(1)}, u32[]{:S(2)}, u32[]{:S(2)}) collective-permute-start(bf16[2,1024,128]{2,1,0:T(8,128)(2,1)} %bitcast.34), channel_id=1, source_target_pairs={{0,32},{32,64},{64,96},{96,0},{1,33},{33,65},{65,97},{97,1},{2,34}... | collective-permute-start | bytes 1572872 | tf_op jit(solution)/shard_map/ppermute | solution.py:470
  310.2 0.8 copy-start.2
  310.2 1.0 copy-start.3
  311.1 0.8 copy-start.4
Sparse Core Ops, SparseCore 0:
  156.8 68.9 all-gather.5
  229.5 76.5 all-gather.3
where the time goes:
time: 329 us; the launch traced here: 324 us
  Pallas kernels  104 us (32%)
  waiting for transfers between devices  103 us (31%)
  blocking collectives  51.2 us (16%)
  starting transfers between devices  28.6 us (9%)
  between operations  14.3 us (4%)
  other arithmetic  13.9 us (4%)
  local copies, waits for them, and re-layouts  9.87 us (3%)
    all_gather x1, waiting for transfers between devices, body(): lax.all_gather(eight, ('rep', 'shard'), axis=0, tiled=True).astype(F32)  45.5 us
    all_to_all x1, blocking collectives, exchange(): return lax.all_to_all(x, axis, split_axis=0, concat_axis=0, tiled=True)  38.7 us
    pallas_call x2, Pallas kernels, gather_call(): pl.pallas_call(gather_kernel, out_shape=jax.ShapeDtypeStruct((OWNERS, dep...  34.6 us
    all_gather x1, waiting for transfers between devices, body(): all_grads = lax.all_gather(mine, 'shard', axis=0)  29.3 us
    pallas_call x1, Pallas kernels, scatter_call(): pl.pallas_call(scatter_kernel, out_shape=jax.ShapeDtypeStruct((rows, EMB)...  25.9 us
    all_to_all x2, waiting for transfers between devices, exchange(): return lax.all_to_all(x, axis, split_axis=0, concat_axis=0, tiled=True)  17.9 us
    pallas_call x1, Pallas kernels, tower_call(): pl.pallas_call(functools.partial(tower_kernel, CAP - got.shape[1]), grid=...  16.7 us
    pallas_call x1, Pallas kernels, index_call(): pl.pallas_call(index_kernel, out_shape=jax.ShapeDtypeStruct((OWNERS, CAP)...  15.3 us
  transfers between devices with their start and end apart: 13, of which 7 were waited for; matrix products, arithmetic and copies ran while one was open for 5% of the time, Pallas kernels for 15%

commit v1 on v0

--- a/solution.py
+++ b/solution.py
@@ -28,7 +28,9 @@
 IDROWS = IDS // LANES
 ACCS = 16
 POOLED = 8
-GROUP = 8
+GROUP = 4
+LISTED = CAP + 64
+LISTS = 4
 SOURCES = GROUP * REPS * PAIR * SAMPLES
 SHIFT = 13
 EARLY = 256
@@ -159,17 +161,18 @@
     def _():
         wide[...] = table_ref[...].astype(F32)
 
-    base = step * depth
-
-    def some(i, _):
-        at = i * 32
-        rows = [wide[pl.ds(row_ref[base + at + j], 1), :] for j in range(32)]
-        for j in range(32):
-            picked[pl.ds(at + j, 1), :] = rows[j]
-        return 0
-
-    lax.fori_loop(0, depth // 32, some, 0)
-    out_ref[0] = picked[...].astype(BF)
+    for part in range(LISTS):
+        base = (step * LISTS + part) * depth
+
+        def some(i, _):
+            at = i * 32
+            rows = [wide[pl.ds(row_ref[base + at + j], 1), :] for j in range(32)]
+            for j in range(32):
+                picked[pl.ds(part * depth + at + j, 1), :] = rows[j]
+            return 0
+
+        lax.fori_loop(0, depth // 32, some, 0)
+        out_ref[part] = picked[part * depth : (part + 1) * depth, :].astype(BF)
 
 
 def gather_call(rows, table):
@@ -179,10 +182,10 @@
         out_shape=jax.ShapeDtypeStruct((OWNERS, depth, EMB), BF),
         grid_spec=pltpu.PrefetchScalarGridSpec(
             num_scalar_prefetch=1,
-            grid=(OWNERS,),
+            grid=(OWNERS // LISTS,),
             in_specs=[pl.BlockSpec((ROWS, EMB), lambda i, r: (0, 0))],
-            out_specs=pl.BlockSpec((1, depth, EMB), lambda i, r: (i, 0, 0)),
-            scratch_shapes=[pltpu.VMEM((ROWS, EMB), F32), pltpu.VMEM((depth, EMB), F32)],
+            out_specs=pl.BlockSpec((LISTS, depth, EMB), lambda i, r: (i, 0, 0)),
+            scratch_shapes=[pltpu.VMEM((ROWS, EMB), F32), pltpu.VMEM((LISTS * depth, EMB), F32)],
         ),
         compiler_params=pltpu.CompilerParams(vmem_limit_bytes=VMEM),
         name="gather",
@@ -319,7 +322,9 @@
             gx_ref[...] += grad * cross_t[layer]
             grad = grad + dot(crossed, cross_w[layer], NT)
             if layer == 0:
-                first_ref[...] = dot(start_ref[...], crossed, TN).astype(BF)
+                outer = dot(start_ref[...], crossed, TN).reshape(OWNERS, REPS, 8, WIDTH)
+                for r in range(REPS):
+                    first_ref[r] = outer[:, r].reshape(OWNERS * 8, WIDTH).astype(BF)
         scaled = (gx_ref[...] + grad) * gain
         pooled = pooled_ref[...]
         inverse = lax.rsqrt(jnp.mean(pooled * pooled, axis=1, keepdims=True) + 1e-06)
@@ -351,12 +356,12 @@
         out_specs=[
             whole((SAMPLES, 1)),
             whole((REPS, SAMPLES, PAIR * EMB)),
-            whole((WIDTH, WIDTH)),
+            whole((REPS, OWNERS * 8, WIDTH)),
         ],
         out_shape=[
             jax.ShapeDtypeStruct((SAMPLES, 1), F32),
             jax.ShapeDtypeStruct((REPS, SAMPLES, PAIR * EMB), BF),
-            jax.ShapeDtypeStruct((WIDTH, WIDTH), BF),
+            jax.ShapeDtypeStruct((REPS, OWNERS * 8, WIDTH), BF),
         ],
         scratch_shapes=[
             pltpu.VMEM((SAMPLES, WIDTH), F32),
@@ -373,7 +378,7 @@
     )(got, packed, earlier, labels, gain, cbias, dbias, out_w, cross, deep)
 
 
-def scatter_kernel(word_ref, first_ref, last_ref, grads_ref, out_ref, wide, *accs):
+def scatter_kernel(first_ref, last_ref, word_ref, grads_ref, out_ref, wide, *accs):
     step = pl.program_id(0)
 
     @pl.when(step == 0)
@@ -392,10 +397,11 @@
                 ].astype(F32)
 
     def device(k, _):
-        listed = (k & (REPS - 1)) * OWNERS + step * group + k // REPS
+        listed = step * group * REPS + k
+        first = first_ref[listed]
 
         def some(i, _):
-            at = listed * CAP + i * ACCS
+            at = k * LISTED + first + i * ACCS
             words = [word_ref[at + j] for j in range(ACCS)]
             rows = [wide[pl.ds(word & (SOURCES - 1), 1), :] for word in words]
             olds = [accs[j][pl.ds(words[j] >> SHIFT, 1), :] for j in range(ACCS)]
@@ -403,7 +409,7 @@
                 accs[j][pl.ds(words[j] >> SHIFT, 1), :] = olds[j] + rows[j]
             return 0
 
-        lax.fori_loop(first_ref[listed], last_ref[listed], some, 0)
+        lax.fori_loop(0, (last_ref[listed] - first + ACCS - 1) // ACCS, some, 0)
         return 0
 
     lax.fori_loop(0, group * REPS, device, 0)
@@ -422,12 +428,15 @@
         scatter_kernel,
         out_shape=jax.ShapeDtypeStruct((rows, EMB), BF),
         grid_spec=pltpu.PrefetchScalarGridSpec(
-            num_scalar_prefetch=3,
+            num_scalar_prefetch=2,
             grid=(OWNERS // group,),
             in_specs=[
                 pl.BlockSpec(
+                    (group * REPS * LISTED,), lambda i, *_: (i,), memory_space=pltpu.SMEM
+                ),
+                pl.BlockSpec(
                     (group, REPS, SAMPLES, PAIR * EMB), lambda i, *_: (i, 0, 0, 0)
-                )
+                ),
             ],
             out_specs=pl.BlockSpec((rows, EMB), lambda i, *_: (0, 0)),
             scratch_shapes=[pltpu.VMEM((group * REPS * PAIR * SAMPLES, EMB), F32)]
@@ -435,7 +444,7 @@
         ),
         compiler_params=pltpu.CompilerParams(vmem_limit_bytes=VMEM),
         name="scatter",
-    )(words, first, last, grads)
+    )(first, last, words, grads)
 
 
 def finish_kernel(order_ref, *refs):
@@ -468,6 +477,13 @@
         return x
     n = lax.axis_size(axis)
     return lax.ppermute(x, axis, [(i, (i + k) % n) for i in range(n)])
+
+
+def in_order(x, axis, me):
+    n = lax.axis_size(axis)
+    back = [from_before(x, axis, k) for k in range(n)]
+    twice = jnp.concatenate([back[(n - 1 - i) % n] for i in range(2 * n - 1)])
+    return lax.dynamic_slice_in_dim(twice, (n - 1 - me) * x.shape[0], n * x.shape[0])
 
 
 def summed(x):
@@ -511,26 +527,33 @@
     got_late = exchange(picked_late, "shard")
 
     rep = lax.axis_index("rep")
-    everyone = jnp.concatenate(
-        [lists] + [from_before(lists, "rep", k) for k in range(1, REPS)]
-    ).reshape(REPS * OWNERS, CAP)
+    everyone = jnp.stack(
+        [
+            from_before(lists, "rep", k).reshape(OWNERS // GROUP, GROUP, CAP)
+            for k in range(REPS)
+        ],
+        axis=2,
+    )
     feature = everyone & (FEATS - 1)
     valid = everyone > 0
     within = feature - rep * PAIR
     ours = valid & (within >= 0) & (within < PAIR)
     target = jnp.where(ours, within * VOC + ((everyone >> 10) & (VOC - 1)), PAIR * VOC)
-    device = lax.broadcasted_iota(I32, everyone.shape, 0)
-    source = ((device & (GROUP - 1)) * REPS + device // OWNERS) * (PAIR * SAMPLES) + jnp.where(
+    group = lax.broadcasted_iota(I32, everyone.shape, 1)
+    back = lax.broadcasted_iota(I32, everyone.shape, 2)
+    source = (group * REPS + back) * (PAIR * SAMPLES) + jnp.where(
         ours, within * SAMPLES + ((everyone >> 3) & (SAMPLES - 1)), 0
     )
-    words = ((target << SHIFT) | source).reshape(-1)
-    below = jnp.sum((valid & (within < 0)).astype(I32), axis=1)
-    upto = jnp.sum((valid & (within < PAIR)).astype(I32), axis=1)
-    first_block = below // ACCS
-    last_block = (upto + ACCS - 1) // ACCS
+    words = jnp.pad(
+        (target << SHIFT) | source,
+        ((0, 0), (0, 0), (0, 0), (0, LISTED - CAP)),
+        constant_values=(PAIR * VOC) << SHIFT,
+    ).reshape(-1)
+    first_word = jnp.sum((valid & (within < 0)).astype(I32), axis=3).reshape(-1)
+    last_word = jnp.sum((valid & (within < PAIR)).astype(I32), axis=3).reshape(-1)
     sums_early = pool_call(got_early, packed, 0)
-    got_late, sums_early, words, first_block, last_block = lax.optimization_barrier(
-        (got_late, sums_early, words, first_block, last_block)
+    got_late, sums_early, words, first_word, last_word = lax.optimization_barrier(
+        (got_late, sums_early, words, first_word, last_word)
     )
 
     logits, grads, first_local = tower_call(
@@ -553,12 +576,13 @@
     )
     mine, first_local = lax.optimization_barrier((mine, first_local))
     all_grads = lax.all_gather(mine, "shard", axis=0)
-    eight = summed(
-        exchange(first_local.reshape(REPS * OWNERS, 8, WIDTH), ("rep", "shard"))
-    )
-    first_grad = lax.all_gather(eight, ("rep", "shard"), axis=0, tiled=True).astype(F32)
-
-    part = scatter_call(words, first_block, last_block, all_grads).reshape(PAIR, VOC, EMB)
+    quarter = summed(exchange(first_local, "rep"))
+    eight = summed(exchange(quarter.reshape(OWNERS, 8, WIDTH), "shard"))
+    first_grad = lax.all_gather(
+        in_order(eight, "rep", rep), "shard", axis=0, tiled=True
+    ).astype(F32)
+
+    part = scatter_call(words, first_word, last_word, all_grads).reshape(PAIR, VOC, EMB)
     parts = [part] + [from_before(part, "rep", k) for k in range(1, REPS)]
     slots = feature_slot[lax.axis_index("shard")]
     feature_of = jnp.argmax(

time: 329 us -> 287 us (0.87)
  the two profiles are of different devices: /device:TPU:38 before, /device:TPU:96 now
where the time goes in v1:
time: 287 us; the launch traced here: 284 us
  Pallas kernels  113 us (39%)
  blocking collectives  63.2 us (22%)
  waiting for transfers between devices  45 us (16%)
  starting transfers between devices  28.4 us (10%)
  between operations  14.2 us (5%)
  local copies, waits for them, and re-layouts  11.8 us (4%)
  other arithmetic  8.54 us (3%)
    all_to_all x2, blocking collectives, exchange(): return lax.all_to_all(x, axis, split_axis=0, concat_axis=0, tiled=True)  50.6 us
    pallas_call x1, Pallas kernels, scatter_call(): pl.pallas_call(scatter_kernel, out_shape=jax.ShapeDtypeStruct((rows, EMB)...  45.6 us
    ppermute x12, waiting for transfers between devices, from_before(): return lax.ppermute(x, axis, [(i, (i + k) % n) for i in range(n)])  23.9 us
    pallas_call x2, Pallas kernels, gather_call(): pl.pallas_call(gather_kernel, out_shape=jax.ShapeDtypeStruct((OWNERS, dep...  23.7 us
    all_to_all x2, waiting for transfers between devices, exchange(): return lax.all_to_all(x, axis, split_axis=0, concat_axis=0, tiled=True)  21 us
    pallas_call x1, Pallas kernels, tower_call(): pl.pallas_call(functools.partial(tower_kernel, CAP - got.shape[1]), grid=...  16.7 us
    ppermute x12, starting transfers between devices, from_before(): return lax.ppermute(x, axis, [(i, (i + k) % n) for i in range(n)])  16.4 us
    pallas_call x1, Pallas kernels, index_call(): pl.pallas_call(index_kernel, out_shape=jax.ShapeDtypeStruct((OWNERS, CAP)...  15.3 us
  transfers between devices with their start and end apart: 16, of which 12 were waited for; matrix products, arithmetic and copies ran while one was open for 4% of the time, Pallas kernels for 22%

profile of v1, /device:TPU:96, one launch (start us, length us, event | category | flops | bytes accessed | tf_op | source)
XLA Modules:
  0.0 283.8 jit_solution(2697823111470456684)
XLA Ops:
  8.5 15.3 %index.1.packed_ref = s32[32,512]{1,0:T(8,128)} custom-call(s32[1,8192]{1,0:T(1,128)} %ids_in.1, s32[1,8192]{1,0:T(1,128)} %bitcast.47, s32[1,1024]{1,0:T(1,128)} %len_in.1, s32[32,8]{1,0:T(8,128)} %copy.21.slot_ref), custom_call_target="tpu_custom_call" | custom-call | tf_op jit(solution)/shard_map/index/pallas_call | solution.py:141
  24.7 12.6 %all_to_all.25 = s32[32,4,128]{2,1,0:T(4,128)S(1)} all-to-all(s32[32,4,128]{2,1,0:T(4,128)S(1)} %reshape.49), channel_id=1, replica_groups=mesh['rep'=4,'shard'=32] {'shard'}, dimensions={0} | all-to-all | bytes 131072 | tf_op jit(solution)/shard_map/all_to_all | solution.py:513
  38.0 11.9 %gather.3 = bf16[32,256,128]{2,1,0:T(8,128)(2,1)} custom-call(s32[8192]{0:T(1024)} %bitcast.39, bf16[8192,128]{1,0:T(8,128)(2,1)} %table_ref.3), custom_call_target="tpu_custom_call" | custom-call | tf_op jit(solution)/shard_map/gather/pallas_call | solution.py:180
  49.9 5.8 %all-to-all-start.2 = ((bf16[32,256,128]{2,1,0:T(8,128)(2,1)}), bf16[32,256,128]{2,1,0:T(8,128)(2,1)S(1)}, u32[]{:S(2)}, u32[]{:S(2)}) async-start(bf16[32,256,128]{2,1,0:T(8,128)(2,1)} %gather.3), calls=%async_computation.2 | async-start | bytes 4194304 | tf_op jit(solution)/shard_map/all_to_all | solution.py:519
  56.3 11.9 %gather.2 = bf16[32,256,128]{2,1,0:T(8,128)(2,1)} custom-call(s32[8192]{0:T(1024)} %bitcast.40, bf16[8192,128]{1,0:T(8,128)(2,1)} %table_ref.3), custom_call_target="tpu_custom_call" | custom-call | tf_op jit(solution)/shard_map/gather/pallas_call | solution.py:180
  68.2 14.2 %all-to-all-done.2.got_ref = bf16[32,256,128]{2,1,0:T(8,128)(2,1)S(1)} async-done(((bf16[32,256,128]{2,1,0:T(8,128)(2,1)}), bf16[32,256,128]{2,1,0:T(8,128)(2,1)S(1)}, u32[]{:S(2)}, u32[]{:S(2)}) %all-to-all-start.2) | async-done | bytes 2097184 | tf_op jit(solution)/shard_map/all_to_all | solution.py:519
  83.7 6.2 %all-to-all-start.1 = ((bf16[32,256,128]{2,1,0:T(8,128)(2,1)}), bf16[32,256,128]{2,1,0:T(8,128)(2,1)S(1)}, u32[]{:S(2)}, u32[]{:S(2)}) async-start(bf16[32,256,128]{2,1,0:T(8,128)(2,1)} %gather.2), calls=%async_computation.1 | async-start | bytes 4194304 | tf_op jit(solution)/shard_map/all_to_all | solution.py:519
  90.8 3.0 %collective-permute-start.2 = (s32[32,4,128]{2,1,0:T(4,128)S(1)}, s32[32,4,128]{2,1,0:T(4,128)S(1)}, u32[]{:S(2)}, u32[]{:S(2)}) collective-permute-start(s32[32,4,128]{2,1,0:T(4,128)S(1)} %all_to_all.25), channel_id=1, source_target_pairs={{0,96},{32,0},{64,32},{96,64},{1,97},{33,1},{65,33},{97,65},{2,98}... | collective-permute-start | bytes 196616 | tf_op jit(solution)/shard_map/ppermute | solution.py:479
  95.4 1.6 collective-permute-done.2
  96.9 3.0 %collective-permute-done.1 = s32[32,4,128]{2,1,0:T(4,128)S(1)} collective-permute-done((s32[32,4,128]{2,1,0:T(4,128)S(1)}, s32[32,4,128]{2,1,0:T(4,128)S(1)}, u32[]{:S(2)}, u32[]{:S(2)}) %collective-permute-start.1) | collective-permute-done | bytes 65568 | tf_op jit(solution)/shard_map/ppermute | solution.py:479
  104.3 5.5 %pool.1.earlier_ref = f32[128,1024]{1,0:T(8,128)} custom-call(bf16[32,256,128]{2,1,0:T(8,128)(2,1)} %copy-done.1, s32[32,512]{1,0:T(8,128)} %index.1.packed_ref), custom_call_target="tpu_custom_call" | custom-call | tf_op jit(solution)/shard_map/pool/pallas_call | solution.py:228
  109.8 6.8 %all-to-all-done.1.got_ref = bf16[32,256,128]{2,1,0:T(8,128)(2,1)S(1)} async-done(((bf16[32,256,128]{2,1,0:T(8,128)(2,1)}), bf16[32,256,128]{2,1,0:T(8,128)(2,1)S(1)}, u32[]{:S(2)}, u32[]{:S(2)}) %all-to-all-start.1) | async-done | bytes 2097184 | tf_op jit(solution)/shard_map/all_to_all | solution.py:519
  117.9 16.7 %tower.1 = (f32[128,1]{1,0:T(8,128)}, bf16[4,128,256]{2,1,0:T(8,128)(2,1)}, bf16[4,256,1024]{2,1,0:T(8,128)(2,1)}) custom-call(bf16[32,256,128]{2,1,0:T(8,128)(2,1)} %copy-done, s32[32,512]{1,0:T(8,128)} %index.1.packed_ref, f32[128,1024]{1,0:T(8,128)} %pool.1.earlier_ref, s32[128,1]{1,0:T(8,128)} %copy.22.labels_ref, f32[1,1024]{1,0:T(1,128)} %bitcast.48, ...), custom_call_target="tpu_custom_call" | custom-call | tf_op jit(solution)/shard_map/tower/pallas_call | solution.py:341
  135.6 3.1 %collective-permute-start.5 = (bf16[128,256]{1,0:T(8,128)(2,1)S(1)}, bf16[128,256]{1,0:T(8,128)(2,1)S(1)}, u32[]{:S(2)}, u32[]{:S(2)}) collective-permute-start(bf16[128,256]{1,0:T(8,128)(2,1)S(1)} %get-tuple-element.36), channel_id=1, source_target_pairs={{0,96},{32,0},{64,32},{96,64},{1,97},{33,1},{65,33},{97,65},{2,98}... | collective-permute-start | bytes 196616 | tf_op jit(solution)/shard_map/ppermute | solution.py:479
  141.8 3.0 %collective-permute-done.4 = bf16[128,256]{1,0:T(8,128)(2,1)S(1)} collective-permute-done((bf16[128,256]{1,0:T(8,128)(2,1)S(1)}, bf16[128,256]{1,0:T(8,128)(2,1)S(1)}, u32[]{:S(2)}, u32[]{:S(2)}) %collective-permute-start.4) | collective-permute-done | bytes 65568 | tf_op jit(solution)/shard_map/ppermute | solution.py:479
  146.2 29.6 %all_to_all.26 = bf16[4,256,1024]{2,1,0:T(8,128)(2,1)S(1)} all-to-all(bf16[4,256,1024]{2,1,0:T(8,128)(2,1)} %get-tuple-element.31), channel_id=1, replica_groups=mesh['rep'=4,'shard'=32] {'rep'}, dimensions={0} | all-to-all | bytes 4194304 | tf_op jit(solution)/shard_map/all_to_all | solution.py:519
  176.3 21.0 %all_to_all.27 = bf16[32,8,1024]{2,1,0:T(8,128)(2,1)S(1)} all-to-all(bf16[32,8,1024]{2,1,0:T(8,128)(2,1)S(1)} %bitcast.35), channel_id=1, replica_groups=mesh['rep'=4,'shard'=32] {'shard'}, dimensions={0} | all-to-all | bytes 1048576 | tf_op jit(solution)/shard_map/all_to_all | solution.py:519
  201.1 3.5 %collective-permute-done.10 = bf16[8,1024]{1,0:T(8,128)(2,1)S(1)} collective-permute-done((bf16[8,1024]{1,0:T(8,128)(2,1)S(1)}, bf16[8,1024]{1,0:T(8,128)(2,1)S(1)}, u32[]{:S(2)}, u32[]{:S(2)}) %collective-permute-start.10) | collective-permute-done | bytes 16416 | tf_op jit(solution)/shard_map/ppermute | solution.py:479
  205.5 45.6 %scatter.1 = bf16[2048,128]{1,0:T(8,128)(2,1)} custom-call(s32[128]{0:T(128)} %reshape.54.first_ref, s32[128]{0:T(128)} %reshape.55.last_ref, s32[73728]{0:T(1024)} %reshape.53.word_ref, bf16[32,4,128,256]{3,2,1,0:T(8,128)(2,1)} %bitcast.30), custom_call_target="tpu_custom_call" | custom-call | tf_op jit(solution)/shard_map/scatter/pallas_call | solution.py:427
  251.1 3.2 %collective-permute-start.8 = (bf16[2,1024,128]{2,1,0:T(8,128)(2,1)}, bf16[2,1024,128]{2,1,0:T(8,128)(2,1)S(1)}, u32[]{:S(2)}, u32[]{:S(2)}) collective-permute-start(bf16[2,1024,128]{2,1,0:T(8,128)(2,1)} %bitcast.31), channel_id=1, source_target_pairs={{0,96},{32,0},{64,32},{96,64},{1,97},{33,1},{65,33},{97,65},{2,98}... | collective-permute-start | bytes 1572872 | tf_op jit(solution)/shard_map/ppermute | solution.py:479
  257.1 4.1 %convert_element_type.15 = f32[1024,1024]{1,0:T(8,128)} convert(bf16[1024,1024]{1,0:T(8,128)(2,1)} %all-gather.4.cloned.1.call-done) | non-fusion elementwise | flops 1048576 | bytes 6291456 | tf_op jit(solution)/shard_map/convert_element_type | solution.py:583
  261.2 5.7 %collective-permute-done.8.refs_3_ = bf16[2,1024,128]{2,1,0:T(8,128)(2,1)S(1)} collective-permute-done((bf16[2,1024,128]{2,1,0:T(8,128)(2,1)}, bf16[2,1024,128]{2,1,0:T(8,128)(2,1)S(1)}, u32[]{:S(2)}, u32[]{:S(2)}) %collective-permute-start.8) | collective-permute-done | bytes 524320 | tf_op jit(solution)/shard_map/ppermute | solution.py:479
  266.9 3.6 %collective-permute-done.6.refs_1_ = bf16[2,1024,128]{2,1,0:T(8,128)(2,1)S(1)} collective-permute-done((bf16[2,1024,128]{2,1,0:T(8,128)(2,1)}, bf16[2,1024,128]{2,1,0:T(8,128)(2,1)S(1)}, u32[]{:S(2)}, u32[]{:S(2)}) %collective-permute-start.6) | collective-permute-done | bytes 524320 | tf_op jit(solution)/shard_map/ppermute | solution.py:479
  271.3 5.7 %finish.1 = f32[8192,128]{1,0:T(8,128)} custom-call(s32[8]{0:T(128)} %fusion.1.order_ref, bf16[2,1024,128]{2,1,0:T(8,128)(2,1)} %bitcast.34, bf16[2,1024,128]{2,1,0:T(8,128)(2,1)} %copy-done.4, bf16[2,1024,128]{2,1,0:T(8,128)(2,1)} %copy-done.3, bf16[2,1024,128]{2,1,0:T(8,128)(2,1)} %copy-done.2), custom_call_target="tpu_custom_call" | custom-call | tf_op jit(solution)/shard_map/finish/pallas_call | solution.py:461
  (67 shorter events, 27.2 us)
Async XLA Ops:
  49.9 32.5 %all-to-all-start.2 = ((bf16[32,256,128]{2,1,0:T(8,128)(2,1)}), bf16[32,256,128]{2,1,0:T(8,128)(2,1)S(1)}, u32[]{:S(2)}, u32[]{:S(2)}) async-start(bf16[32,256,128]{2,1,0:T(8,128)(2,1)} %gather.3), calls=%async_computation.2 | async-start | bytes 4194304 | tf_op jit(solution)/shard_map/all_to_all | solution.py:519
  68.2 21.8 %copy-start.7 = (s32[128]{0:T(128)S(1)}, s32[128]{0:T(128)}, u32[]{:S(2)}) copy-start(s32[128]{0:T(128)} %param.17) | copy-start | bytes 1540
  82.4 1.3 copy-start.1
  83.7 32.9 %all-to-all-start.1 = ((bf16[32,256,128]{2,1,0:T(8,128)(2,1)}), bf16[32,256,128]{2,1,0:T(8,128)(2,1)S(1)}, u32[]{:S(2)}, u32[]{:S(2)}) async-start(bf16[32,256,128]{2,1,0:T(8,128)(2,1)} %gather.2), calls=%async_computation.1 | async-start | bytes 4194304 | tf_op jit(solution)/shard_map/all_to_all | solution.py:519
  89.9 115.5 %all-gather.6.cloned.1.call-start = ((), (), s32[]{:S(2)}) async-start(), calls=%async_computation.6 | async-start | bytes 8650752 | tf_op jit(solution)/shard_map/all_gather | solution.py:578
  90.8 6.2 %collective-permute-start.2 = (s32[32,4,128]{2,1,0:T(4,128)S(1)}, s32[32,4,128]{2,1,0:T(4,128)S(1)}, u32[]{:S(2)}, u32[]{:S(2)}) collective-permute-start(s32[32,4,128]{2,1,0:T(4,128)S(1)} %all_to_all.25), channel_id=1, source_target_pairs={{0,96},{32,0},{64,32},{96,64},{1,97},{33,1},{65,33},{97,65},{2,98}... | collective-permute-start | bytes 196616 | tf_op jit(solution)/shard_map/ppermute | solution.py:479
  93.8 6.1 %collective-permute-start.1 = (s32[32,4,128]{2,1,0:T(4,128)S(1)}, s32[32,4,128]{2,1,0:T(4,128)S(1)}, u32[]{:S(2)}, u32[]{:S(2)}) collective-permute-start(s32[32,4,128]{2,1,0:T(4,128)S(1)} %all_to_all.25), channel_id=1, source_target_pairs={{0,64},{32,96},{64,0},{96,32},{1,65},{33,97},{65,1},{97,33},{2,66}... | collective-permute-start | bytes 196616 | tf_op jit(solution)/shard_map/ppermute | solution.py:479
  94.4 6.1 %collective-permute-start = (s32[32,4,128]{2,1,0:T(4,128)S(1)}, s32[32,4,128]{2,1,0:T(4,128)S(1)}, u32[]{:S(2)}, u32[]{:S(2)}) collective-permute-start(s32[32,4,128]{2,1,0:T(4,128)S(1)} %all_to_all.25), channel_id=1, source_target_pairs={{0,32},{32,64},{64,96},{96,0},{1,33},{33,65},{65,97},{97,1},{2,34}... | collective-permute-start | bytes 196616 | tf_op jit(solution)/shard_map/ppermute | solution.py:479
  116.6 1.3 copy-start
  135.6 6.2 %collective-permute-start.5 = (bf16[128,256]{1,0:T(8,128)(2,1)S(1)}, bf16[128,256]{1,0:T(8,128)(2,1)S(1)}, u32[]{:S(2)}, u32[]{:S(2)}) collective-permute-start(bf16[128,256]{1,0:T(8,128)(2,1)S(1)} %get-tuple-element.36), channel_id=1, source_target_pairs={{0,96},{32,0},{64,32},{96,64},{1,97},{33,1},{65,33},{97,65},{2,98}... | collective-permute-start | bytes 196616 | tf_op jit(solution)/shard_map/ppermute | solution.py:479
  138.7 6.1 %collective-permute-start.4 = (bf16[128,256]{1,0:T(8,128)(2,1)S(1)}, bf16[128,256]{1,0:T(8,128)(2,1)S(1)}, u32[]{:S(2)}, u32[]{:S(2)}) collective-permute-start(bf16[128,256]{1,0:T(8,128)(2,1)S(1)} %get-tuple-element.37), channel_id=1, source_target_pairs={{0,64},{32,96},{64,0},{96,32},{1,65},{33,97},{65,1},{97,33},{2,66}... | collective-permute-start | bytes 196616 | tf_op jit(solution)/shard_map/ppermute | solution.py:479
  139.3 6.1 %collective-permute-start.3 = (bf16[128,256]{1,0:T(8,128)(2,1)S(1)}, bf16[128,256]{1,0:T(8,128)(2,1)S(1)}, u32[]{:S(2)}, u32[]{:S(2)}) collective-permute-start(bf16[128,256]{1,0:T(8,128)(2,1)S(1)} %get-tuple-element.38), channel_id=1, source_target_pairs={{0,32},{32,64},{64,96},{96,0},{1,33},{33,65},{65,97},{97,1},{2,34}... | collective-permute-start | bytes 196616 | tf_op jit(solution)/shard_map/ppermute | solution.py:479
  146.2 110.9 %all-gather.4.cloned.1.call-start = ((), (), s32[]{:S(2)}) async-start(), calls=%async_computation.5 | async-start | bytes 2162688 | tf_op jit(solution)/shard_map/all_gather | solution.py:581
  197.3 3.8 %collective-permute-start.9 = (bf16[8,1024]{1,0:T(8,128)(2,1)S(1)}, bf16[8,1024]{1,0:T(8,128)(2,1)S(1)}, u32[]{:S(2)}, u32[]{:S(2)}) collective-permute-start(bf16[8,1024]{1,0:T(8,128)(2,1)S(1)} %reduce_sum.45), channel_id=1, source_target_pairs={{0,96},{32,0},{64,32},{96,64},{1,97},{33,1},{65,33},{97,65},{2,98}... | collective-permute-start | bytes 49160 | tf_op jit(solution)/shard_map/ppermute | solution.py:479
  198.6 6.1 %collective-permute-start.11 = (bf16[8,1024]{1,0:T(8,128)(2,1)S(1)}, bf16[8,1024]{1,0:T(8,128)(2,1)S(1)}, u32[]{:S(2)}, u32[]{:S(2)}) collective-permute-start(bf16[8,1024]{1,0:T(8,128)(2,1)S(1)} %reduce_sum.45), channel_id=1, source_target_pairs={{0,32},{32,64},{64,96},{96,0},{1,33},{33,65},{65,97},{97,1},{2,34}... | collective-permute-start | bytes 49160 | tf_op jit(solution)/shard_map/ppermute | solution.py:479
  199.4 5.2 %collective-permute-start.10 = (bf16[8,1024]{1,0:T(8,128)(2,1)S(1)}, bf16[8,1024]{1,0:T(8,128)(2,1)S(1)}, u32[]{:S(2)}, u32[]{:S(2)}) collective-permute-start(bf16[8,1024]{1,0:T(8,128)(2,1)S(1)} %reduce_sum.45), channel_id=1, source_target_pairs={{0,64},{32,96},{64,0},{96,32},{1,65},{33,97},{65,1},{97,33},{2,66}... | collective-permute-start | bytes 49160 | tf_op jit(solution)/shard_map/ppermute | solution.py:479
  205.4 49.7 %copy-start.6 = (s32[32,8]{0,1:T(8,128)S(1)}, s32[32,8]{0,1:T(8,128)}, u32[]{:S(2)}) copy-start(s32[32,8]{0,1:T(8,128)} %param.16) | copy-start | bytes 3076
  205.4 51.0 %copy-start.5 = (f32[128,1]{1,0:T(8,128)S(1)}, f32[128,1]{1,0:T(8,128)}, u32[]{:S(2)}) copy-start(f32[128,1]{1,0:T(8,128)} %get-tuple-element.32) | copy-start | bytes 1540
  251.1 15.8 %collective-permute-start.8 = (bf16[2,1024,128]{2,1,0:T(8,128)(2,1)}, bf16[2,1024,128]{2,1,0:T(8,128)(2,1)S(1)}, u32[]{:S(2)}, u32[]{:S(2)}) collective-permute-start(bf16[2,1024,128]{2,1,0:T(8,128)(2,1)} %bitcast.31), channel_id=1, source_target_pairs={{0,96},{32,0},{64,32},{96,64},{1,97},{33,1},{65,33},{97,65},{2,98}... | collective-permute-start | bytes 1572872 | tf_op jit(solution)/shard_map/ppermute | solution.py:479
  254.3 12.6 %collective-permute-start.7 = (bf16[2,1024,128]{2,1,0:T(8,128)(2,1)}, bf16[2,1024,128]{2,1,0:T(8,128)(2,1)S(1)}, u32[]{:S(2)}, u32[]{:S(2)}) collective-permute-start(bf16[2,1024,128]{2,1,0:T(8,128)(2,1)} %bitcast.32), channel_id=1, source_target_pairs={{0,64},{32,96},{64,0},{96,32},{1,65},{33,97},{65,1},{97,33},{2,66}... | collective-permute-start | bytes 1572872 | tf_op jit(solution)/shard_map/ppermute | solution.py:479
  254.3 16.2 %collective-permute-start.6 = (bf16[2,1024,128]{2,1,0:T(8,128)(2,1)}, bf16[2,1024,128]{2,1,0:T(8,128)(2,1)S(1)}, u32[]{:S(2)}, u32[]{:S(2)}) collective-permute-start(bf16[2,1024,128]{2,1,0:T(8,128)(2,1)} %bitcast.33), channel_id=1, source_target_pairs={{0,32},{32,64},{64,96},{96,0},{1,33},{33,65},{65,97},{97,1},{2,34}... | collective-permute-start | bytes 1572872 | tf_op jit(solution)/shard_map/ppermute | solution.py:479
  266.9 3.6 %copy-start.2 = (bf16[2,1024,128]{2,1,0:T(8,128)(2,1)}, bf16[2,1024,128]{2,1,0:T(8,128)(2,1)S(1)}, u32[]{:S(2)}) copy-start(bf16[2,1024,128]{2,1,0:T(8,128)(2,1)S(1)} %collective-permute-done.8.refs_3_) | copy-start | bytes 1572868
  266.9 3.6 %copy-start.3 = (bf16[2,1024,128]{2,1,0:T(8,128)(2,1)}, bf16[2,1024,128]{2,1,0:T(8,128)(2,1)S(1)}, u32[]{:S(2)}) copy-start(bf16[2,1024,128]{2,1,0:T(8,128)(2,1)S(1)} %collective-permute-done.7.refs_2_) | copy-start | bytes 1572868
  270.5 0.8 copy-start.4
Sparse Core Ops, SparseCore 0:
  146.3 55.7 all-gather.5
  205.5 42.6 all-gather.3

commit v2 on v1

--- a/solution.py
+++ b/solution.py
@@ -98,7 +98,7 @@
     earlier = onehot((ki // FEATS == kj // FEATS) & (kj < ki))
     carry0 = dot(earlier, high.astype(BF)) * 256.0 + dot(earlier, low.astype(BF))
 
-    rank_iota = iota((CAP, LANES), 0)
+    rank_iota = iota((CAP // 2, LANES), 0)
     owner_iota = iota((OWNERS, LANES), 0)
 
     of_owner = onehot(iota((KEYS, OWNERS), 0) // FEATS == iota((KEYS, OWNERS), 1))
@@ -123,15 +123,17 @@
             for p in (value & 255, (value >> 8) & 255, value >> 16)
         ]
         left = jnp.concatenate(pieces, axis=0).astype(BF)
-        right = onehot(rank_iota == rank)
+        upper = rank >= CAP // 2
+        left = jnp.concatenate([left * onehot(~upper), left * onehot(upper)], axis=0)
+        right = onehot(rank_iota == (rank & (CAP // 2 - 1)))
         acc = acc + dot(left, right, NT)
         carry = carry + (prefix + hot)[:, LANES - 1 : LANES]
         return carry, acc
 
     _, acc = lax.fori_loop(
-        0, IDROWS, place, (carry0, jnp.zeros((3 * OWNERS, CAP), F32)), unroll=8
-    )
-    acc = acc.astype(I32)
+        0, IDROWS, place, (carry0, jnp.zeros((6 * OWNERS, CAP // 2), F32)), unroll=8
+    )
+    acc = jnp.concatenate([acc[: 3 * OWNERS], acc[3 * OWNERS :]], axis=1).astype(I32)
     out_ref[...] = (
         acc[:OWNERS] + (acc[OWNERS : 2 * OWNERS] << 8) + (acc[2 * OWNERS :] << 16)
     )
@@ -378,26 +380,22 @@
     )(got, packed, earlier, labels, gain, cbias, dbias, out_w, cross, deep)
 
 
-def scatter_kernel(first_ref, last_ref, word_ref, grads_ref, out_ref, wide, *accs):
+def scatter_kernel(which, first_ref, last_ref, word_ref, grads_ref, out_ref, wide, *accs):
     step = pl.program_id(0)
+    ours = slice(which * VOC, (which + 1) * VOC)
 
     @pl.when(step == 0)
     def _():
         for acc in accs:
-            acc[...] = jnp.zeros_like(acc)
-
-    group = grads_ref.shape[0]
-    for g in range(group):
+            acc[ours, :] = jnp.zeros((VOC, EMB), F32)
+
+    for g in range(GROUP):
         for r in range(REPS):
-            block = grads_ref[g, r]
-            base = (g * REPS + r) * PAIR * SAMPLES
-            for f in range(PAIR):
-                wide[base + f * SAMPLES : base + (f + 1) * SAMPLES, :] = block[
-                    :, f * EMB : (f + 1) * EMB
-                ].astype(F32)
+            base = ((g * REPS + r) * PAIR + which) * SAMPLES
+            wide[base : base + SAMPLES, :] = grads_ref[g, r].astype(F32)
 
     def device(k, _):
-        listed = step * group * REPS + k
+        listed = step * GROUP * REPS + k
         first = first_ref[listed]
 
         def some(i, _):
@@ -412,64 +410,67 @@
         lax.fori_loop(0, (last_ref[listed] - first + ACCS - 1) // ACCS, some, 0)
         return 0
 
-    lax.fori_loop(0, group * REPS, device, 0)
+    lax.fori_loop(0, GROUP * REPS, device, 0)
 
     @pl.when(step == pl.num_programs(0) - 1)
     def _():
-        total = accs[0][: PAIR * VOC, :]
+        total = accs[0][ours, :]
         for acc in accs[1:]:
-            total = total + acc[: PAIR * VOC, :]
+            total = total + acc[ours, :]
         out_ref[...] = total.astype(out_ref.dtype)
 
 
-def scatter_call(words, first, last, grads, group=GROUP):
-    rows = PAIR * VOC
+def scatter_call(which, words, first, last, grads):
     return pl.pallas_call(
-        scatter_kernel,
-        out_shape=jax.ShapeDtypeStruct((rows, EMB), BF),
+        functools.partial(scatter_kernel, which),
+        out_shape=jax.ShapeDtypeStruct((VOC, EMB), BF),
         grid_spec=pltpu.PrefetchScalarGridSpec(
             num_scalar_prefetch=2,
-            grid=(OWNERS // group,),
+            grid=(OWNERS // GROUP,),
             in_specs=[
                 pl.BlockSpec(
-                    (group * REPS * LISTED,), lambda i, *_: (i,), memory_space=pltpu.SMEM
+                    (GROUP * REPS * LISTED,), lambda i, *_: (i,), memory_space=pltpu.SMEM
                 ),
-                pl.BlockSpec(
-                    (group, REPS, SAMPLES, PAIR * EMB), lambda i, *_: (i, 0, 0, 0)
-                ),
+                pl.BlockSpec((GROUP, REPS, SAMPLES, EMB), lambda i, *_: (i, 0, 0, which)),
             ],
-            out_specs=pl.BlockSpec((rows, EMB), lambda i, *_: (0, 0)),
-            scratch_shapes=[pltpu.VMEM((group * REPS * PAIR * SAMPLES, EMB), F32)]
-            + [pltpu.VMEM((rows + 8, EMB), F32) for _ in range(ACCS)],
+            out_specs=pl.BlockSpec((VOC, EMB), lambda i, *_: (0, 0)),
+            scratch_shapes=[pltpu.VMEM((SOURCES, EMB), F32)]
+            + [pltpu.VMEM((PAIR * VOC + 8, EMB), F32) for _ in range(ACCS)],
         ),
         compiler_params=pltpu.CompilerParams(vmem_limit_bytes=VMEM),
+        cost_estimate=pl.CostEstimate(
+            flops=IDS * EMB, bytes_accessed=60_000_000, transcendentals=0
+        ),
         name="scatter",
     )(first, last, words, grads)
 
 
-def finish_kernel(order_ref, *refs):
-    parts, rows_ref = refs[:REPS], refs[REPS]
-    source = order_ref[pl.program_id(0)]
+def finish_kernel(place_ref, *refs):
+    parts, rows_ref = refs[:REPS], refs[-1]
+    step = pl.program_id(0)
     for k in range(REPS):
 
-        @pl.when(source // PAIR == k)
+        @pl.when(step == k)
         def _():
-            rows_ref[...] = parts[k][lax.rem(source, PAIR)].astype(F32)
-
-
-def finish_call(order, parts):
+            rows_ref[...] = parts[k][...].astype(F32)
+
+
+def finish_call(places, parts, earlier):
+    whole = pl.BlockSpec((VOC, EMB), lambda i, p: (0, 0))
+    more = [] if earlier is None else [earlier]
     return pl.pallas_call(
         finish_kernel,
         out_shape=jax.ShapeDtypeStruct((ROWS, EMB), F32),
         grid_spec=pltpu.PrefetchScalarGridSpec(
             num_scalar_prefetch=1,
-            grid=(FEATS,),
-            in_specs=[pl.BlockSpec((PAIR, VOC, EMB), lambda i, o: (0, 0, 0)) for _ in parts],
-            out_specs=pl.BlockSpec((VOC, EMB), lambda i, o: (i, 0)),
+            grid=(REPS,),
+            in_specs=[whole] * REPS + [pl.BlockSpec(memory_space=pl.ANY)] * len(more),
+            out_specs=pl.BlockSpec((VOC, EMB), lambda i, p: (p[i], 0)),
         ),
+        input_output_aliases={1 + REPS: 0} if more else {},
         compiler_params=pltpu.CompilerParams(vmem_limit_bytes=VMEM),
         name="finish",
-    )(order, *parts)
+    )(places, *parts, *more)
 
 
 def from_before(x, axis, k):
@@ -549,11 +550,12 @@
         ((0, 0), (0, 0), (0, 0), (0, LISTED - CAP)),
         constant_values=(PAIR * VOC) << SHIFT,
     ).reshape(-1)
-    first_word = jnp.sum((valid & (within < 0)).astype(I32), axis=3).reshape(-1)
-    last_word = jnp.sum((valid & (within < PAIR)).astype(I32), axis=3).reshape(-1)
+    bounds = [
+        jnp.sum((valid & (within < f)).astype(I32), axis=3).reshape(-1) for f in range(PAIR + 1)
+    ]
     sums_early = pool_call(got_early, packed, 0)
-    got_late, sums_early, words, first_word, last_word = lax.optimization_barrier(
-        (got_late, sums_early, words, first_word, last_word)
+    got_late, sums_early, words, bounds = lax.optimization_barrier(
+        (got_late, sums_early, words, bounds)
     )
 
     logits, grads, first_local = tower_call(
@@ -582,14 +584,13 @@
         in_order(eight, "rep", rep), "shard", axis=0, tiled=True
     ).astype(F32)
 
-    part = scatter_call(words, first_word, last_word, all_grads).reshape(PAIR, VOC, EMB)
-    parts = [part] + [from_before(part, "rep", k) for k in range(1, REPS)]
     slots = feature_slot[lax.axis_index("shard")]
-    feature_of = jnp.argmax(
-        slots[None, :] == jnp.arange(FEATS, dtype=I32)[:, None], axis=1
-    ).astype(I32)
-    order = ((rep - feature_of // PAIR) & (REPS - 1)) * PAIR + feature_of % PAIR
-    row_grad = finish_call(order, parts)
+    row_grad = None
+    for f in range(PAIR):
+        part = scatter_call(f, words, bounds[f], bounds[f + 1], all_grads)
+        parts = [from_before(part, "rep", k) for k in range(REPS)]
+        holder = (rep - jnp.arange(REPS, dtype=I32)) % REPS
+        row_grad = finish_call(slots[holder * PAIR + f], parts, row_grad)
     return (row_grad, first_grad, logits.reshape(SAMPLES))
 
 

time: 287 us -> 293 us (1.021)
  the two profiles are of different devices: /device:TPU:96 before, /device:TPU:75 now
where the time goes in v2:
time: 293 us; the launch traced here: 291 us
  Pallas kernels  114 us (39%)
  blocking collectives  65.5 us (22%)
  waiting for transfers between devices  40.2 us (14%)
  starting transfers between devices  33.2 us (11%)
  local copies, waits for them, and re-layouts  16.2 us (6%)
  between operations  14.3 us (5%)
  other arithmetic  7.97 us (3%)
    all_to_all x2, blocking collectives, exchange(): return lax.all_to_all(x, axis, split_axis=0, concat_axis=0, tiled=True)  53.4 us
    pallas_call x2, Pallas kernels, scatter_call(): pl.pallas_call(functools.partial(scatter_kernel, which), out_shape=jax.Sh...  50.5 us
    pallas_call x2, Pallas kernels, gather_call(): pl.pallas_call(gather_kernel, out_shape=jax.ShapeDtypeStruct((OWNERS, dep...  23.7 us
    all_to_all x2, waiting for transfers between devices, exchange(): return lax.all_to_all(x, axis, split_axis=0, concat_axis=0, tiled=True)  20.6 us
    ppermute x15, waiting for transfers between devices, from_before(): return lax.ppermute(x, axis, [(i, (i + k) % n) for i in range(n)])  19.5 us
    ppermute x15, starting transfers between devices, from_before(): return lax.ppermute(x, axis, [(i, (i + k) % n) for i in range(n)])  18.5 us
    pallas_call x1, Pallas kernels, tower_call(): pl.pallas_call(functools.partial(tower_kernel, CAP - got.shape[1]), grid=...  16.7 us
    all_to_all x2, starting transfers between devices, exchange(): return lax.all_to_all(x, axis, split_axis=0, concat_axis=0, tiled=True)  14.6 us
  transfers between devices with their start and end apart: 19, of which 9 were waited for; matrix products, arithmetic and copies ran while one was open for 5% of the time, Pallas kernels for 25%

profile of v2, /device:TPU:75, one launch (start us, length us, event | category | flops | bytes accessed | tf_op | source)
XLA Modules:
  0.0 291.2 jit_solution(18289882060996400257)
XLA Ops:
  8.5 10.0 %index.1.packed_ref = s32[32,512]{1,0:T(8,128)} custom-call(s32[1,8192]{1,0:T(1,128)} %ids_in.1, s32[1,8192]{1,0:T(1,128)} %bitcast.47, s32[1,1024]{1,0:T(1,128)} %len_in.1, s32[32,8]{1,0:T(8,128)} %copy.22.slot_ref), custom_call_target="tpu_custom_call" | custom-call | tf_op jit(solution)/shard_map/index/pallas_call | solution.py:143
  19.4 12.1 %all_to_all.25 = s32[32,4,128]{2,1,0:T(4,128)S(1)} all-to-all(s32[32,4,128]{2,1,0:T(4,128)S(1)} %reshape.114), channel_id=1, replica_groups=mesh['rep'=4,'shard'=32] {'shard'}, dimensions={0} | all-to-all | bytes 131072 | tf_op jit(solution)/shard_map/all_to_all | solution.py:514
  32.2 11.9 %gather.15 = bf16[32,256,128]{2,1,0:T(8,128)(2,1)} custom-call(s32[8192]{0:T(1024)} %bitcast.39, bf16[8192,128]{1,0:T(8,128)(2,1)} %table_ref.3), custom_call_target="tpu_custom_call" | custom-call | tf_op jit(solution)/shard_map/gather/pallas_call | solution.py:182
  44.1 7.1 %all-to-all-start.2 = ((bf16[32,256,128]{2,1,0:T(8,128)(2,1)}), bf16[32,256,128]{2,1,0:T(8,128)(2,1)S(1)}, u32[]{:S(2)}, u32[]{:S(2)}) async-start(bf16[32,256,128]{2,1,0:T(8,128)(2,1)} %gather.15), calls=%async_computation.2 | async-start | bytes 4194304 | tf_op jit(solution)/shard_map/all_to_all | solution.py:520
  51.8 11.9 %gather.14 = bf16[32,256,128]{2,1,0:T(8,128)(2,1)} custom-call(s32[8192]{0:T(1024)} %bitcast.40, bf16[8192,128]{1,0:T(8,128)(2,1)} %table_ref.3), custom_call_target="tpu_custom_call" | custom-call | tf_op jit(solution)/shard_map/gather/pallas_call | solution.py:182
  63.6 12.9 %all-to-all-done.2.got_ref = bf16[32,256,128]{2,1,0:T(8,128)(2,1)S(1)} async-done(((bf16[32,256,128]{2,1,0:T(8,128)(2,1)}), bf16[32,256,128]{2,1,0:T(8,128)(2,1)S(1)}, u32[]{:S(2)}, u32[]{:S(2)}) %all-to-all-start.2) | async-done | bytes 2097184 | tf_op jit(solution)/shard_map/all_to_all | solution.py:520
  77.8 7.6 %all-to-all-start.1 = ((bf16[32,256,128]{2,1,0:T(8,128)(2,1)}), bf16[32,256,128]{2,1,0:T(8,128)(2,1)S(1)}, u32[]{:S(2)}, u32[]{:S(2)}) async-start(bf16[32,256,128]{2,1,0:T(8,128)(2,1)} %gather.14), calls=%async_computation.1 | async-start | bytes 4194304 | tf_op jit(solution)/shard_map/all_to_all | solution.py:520
  86.4 2.3 collective-permute-start.1
  92.4 2.0 convert_reduce_fusion
  97.4 5.5 %pool.1.earlier_ref = f32[128,1024]{1,0:T(8,128)} custom-call(bf16[32,256,128]{2,1,0:T(8,128)(2,1)} %copy-done.1, s32[32,512]{1,0:T(8,128)} %index.1.packed_ref), custom_call_target="tpu_custom_call" | custom-call | tf_op jit(solution)/shard_map/pool/pallas_call | solution.py:230
  102.9 7.8 %all-to-all-done.1.got_ref = bf16[32,256,128]{2,1,0:T(8,128)(2,1)S(1)} async-done(((bf16[32,256,128]{2,1,0:T(8,128)(2,1)}), bf16[32,256,128]{2,1,0:T(8,128)(2,1)S(1)}, u32[]{:S(2)}, u32[]{:S(2)}) %all-to-all-start.1) | async-done | bytes 2097184 | tf_op jit(solution)/shard_map/all_to_all | solution.py:520
  112.0 16.7 %tower.1 = (f32[128,1]{1,0:T(8,128)}, bf16[4,128,256]{2,1,0:T(8,128)(2,1)}, bf16[4,256,1024]{2,1,0:T(8,128)(2,1)}) custom-call(bf16[32,256,128]{2,1,0:T(8,128)(2,1)} %copy-done, s32[32,512]{1,0:T(8,128)} %index.1.packed_ref, f32[128,1024]{1,0:T(8,128)} %pool.1.earlier_ref, s32[128,1]{1,0:T(8,128)} %copy.23.labels_ref, f32[1,1024]{1,0:T(1,128)} %bitcast.48, ...), custom_call_target="tpu_custom_call" | custom-call | tf_op jit(solution)/shard_map/tower/pallas_call | solution.py:343
  129.9 2.3 collective-permute-start.4
  136.2 29.1 %all_to_all.26 = bf16[4,256,1024]{2,1,0:T(8,128)(2,1)S(1)} all-to-all(bf16[4,256,1024]{2,1,0:T(8,128)(2,1)} %get-tuple-element.31), channel_id=1, replica_groups=mesh['rep'=4,'shard'=32] {'rep'}, dimensions={0} | all-to-all | bytes 4194304 | tf_op jit(solution)/shard_map/all_to_all | solution.py:520
  165.7 24.3 %all_to_all.27 = bf16[32,8,1024]{2,1,0:T(8,128)(2,1)S(1)} all-to-all(bf16[32,8,1024]{2,1,0:T(8,128)(2,1)S(1)} %bitcast.35), channel_id=1, replica_groups=mesh['rep'=4,'shard'=32] {'shard'}, dimensions={0} | all-to-all | bytes 1048576 | tf_op jit(solution)/shard_map/all_to_all | solution.py:520
  191.6 2.0 collective-permute-start.14
  193.6 2.0 collective-permute-done.13
  196.4 25.2 %scatter.3.refs_0_ = bf16[1024,128]{1,0:T(8,128)(2,1)} custom-call(s32[128]{0:T(128)} %reshape.119.first_ref, s32[128]{0:T(128)} %reshape.120.first_ref.last_ref, s32[73728]{0:T(1024)} %reshape.118.word_ref, bf16[32,4,128,256]{3,2,1,0:T(8,128)(2,1)} %bitcast.33), custom_call_target="tpu_custom_call" | custom-call | flops 1048576 | bytes 60000000 | tf_op jit(solution)/shard_map/scatter/pallas_call | solution.py:424
  222.5 25.4 %scatter.2.refs_0_ = bf16[1024,128]{1,0:T(8,128)(2,1)} custom-call(s32[128]{0:T(128)} %reshape.120.first_ref.last_ref, s32[128]{0:T(128)} %reshape.121.last_ref, s32[73728]{0:T(1024)} %reshape.118.word_ref, bf16[32,4,128,256]{3,2,1,0:T(8,128)(2,1)} %bitcast.34), custom_call_target="tpu_custom_call" | custom-call | flops 1048576 | bytes 60000000 | tf_op jit(solution)/shard_map/scatter/pallas_call | solution.py:424
  256.8 4.1 %convert_element_type.19 = f32[1024,1024]{1,0:T(8,128)} convert(bf16[1024,1024]{1,0:T(8,128)(2,1)} %all-gather.4.cloned.1.call-done) | non-fusion elementwise | flops 1048576 | bytes 6291456 | tf_op jit(solution)/shard_map/convert_element_type | solution.py:585
  260.9 5.5 %collective-permute-done.10.refs_2_ = bf16[1024,128]{1,0:T(8,128)(2,1)S(1)} collective-permute-done((bf16[1024,128]{1,0:T(8,128)(2,1)S(1)}, bf16[1024,128]{1,0:T(8,128)(2,1)S(1)}, u32[]{:S(2)}, u32[]{:S(2)}) %collective-permute-start.10) | collective-permute-done | bytes 262176 | tf_op jit(solution)/shard_map/ppermute | solution.py:480
  266.4 8.3 %collective-permute-done.11.refs_3_ = bf16[1024,128]{1,0:T(8,128)(2,1)S(1)} collective-permute-done((bf16[1024,128]{1,0:T(8,128)(2,1)S(1)}, bf16[1024,128]{1,0:T(8,128)(2,1)S(1)}, u32[]{:S(2)}, u32[]{:S(2)}) %collective-permute-start.11) | collective-permute-done | bytes 262176 | tf_op jit(solution)/shard_map/ppermute | solution.py:480
  275.4 3.7 %finish.2.refs_4_ = f32[8192,128]{1,0:T(8,128)} custom-call(s32[4]{0:T(128)} %gather_fusion.1, bf16[1024,128]{1,0:T(8,128)(2,1)} %scatter.3.refs_0_, bf16[1024,128]{1,0:T(8,128)(2,1)} %copy-done.6, bf16[1024,128]{1,0:T(8,128)(2,1)} %copy-done.7, bf16[1024,128]{1,0:T(8,128)(2,1)} %copy-done.8), custom_call_target="tpu_custom_call" | custom-call | tf_op jit(solution)/shard_map/finish/pallas_call | solution.py:461
  280.7 3.7 %finish.3 = f32[8192,128]{1,0:T(8,128)} custom-call(s32[4]{0:T(128)} %gather_fusion, bf16[1024,128]{1,0:T(8,128)(2,1)} %scatter.2.refs_0_, bf16[1024,128]{1,0:T(8,128)(2,1)} %copy-done.3, bf16[1024,128]{1,0:T(8,128)(2,1)} %copy-done.4, bf16[1024,128]{1,0:T(8,128)(2,1)} %copy-done.5, f32[8192,128]{1,0:T(8,128)} %finish.2.refs_4_), custom_call_target="tpu_custom_call", output_to_operand_aliasing={{}: (5, {})} | custom-call | tf_op jit(solution)/shard_map/finish/pallas_call | solution.py:461
  (87 shorter events, 33.8 us)
Async XLA Ops:
  44.1 32.4 %all-to-all-start.2 = ((bf16[32,256,128]{2,1,0:T(8,128)(2,1)}), bf16[32,256,128]{2,1,0:T(8,128)(2,1)S(1)}, u32[]{:S(2)}, u32[]{:S(2)}) async-start(bf16[32,256,128]{2,1,0:T(8,128)(2,1)} %gather.15), calls=%async_computation.2 | async-start | bytes 4194304 | tf_op jit(solution)/shard_map/all_to_all | solution.py:520
  63.6 21.8 %copy-start.11 = (s32[128]{0:T(128)S(1)}, s32[128]{0:T(128)}, u32[]{:S(2)}) copy-start(s32[128]{0:T(128)} %param.17) | copy-start | bytes 1540
  77.8 32.9 %all-to-all-start.1 = ((bf16[32,256,128]{2,1,0:T(8,128)(2,1)}), bf16[32,256,128]{2,1,0:T(8,128)(2,1)S(1)}, u32[]{:S(2)}, u32[]{:S(2)}) async-start(bf16[32,256,128]{2,1,0:T(8,128)(2,1)} %gather.14), calls=%async_computation.1 | async-start | bytes 4194304 | tf_op jit(solution)/shard_map/all_to_all | solution.py:520
  85.4 111.0 %all-gather.6.cloned.1.call-start = ((), (), s32[]{:S(2)}) async-start(), calls=%async_computation.6 | async-start | bytes 8650752 | tf_op jit(solution)/shard_map/all_gather | solution.py:580
  86.2 4.1 %collective-permute-start.2 = (s32[32,4,128]{2,1,0:T(4,128)S(1)}, s32[32,4,128]{2,1,0:T(4,128)S(1)}, u32[]{:S(2)}, u32[]{:S(2)}) collective-permute-start(s32[32,4,128]{2,1,0:T(4,128)S(1)} %all_to_all.25), channel_id=1, source_target_pairs={{0,96},{32,0},{64,32},{96,64},{1,97},{33,1},{65,33},{97,65},{2,98}... | collective-permute-start | bytes 196616 | tf_op jit(solution)/shard_map/ppermute | solution.py:480
  86.4 5.6 %collective-permute-start.1 = (s32[32,4,128]{2,1,0:T(4,128)S(1)}, s32[32,4,128]{2,1,0:T(4,128)S(1)}, u32[]{:S(2)}, u32[]{:S(2)}) collective-permute-start(s32[32,4,128]{2,1,0:T(4,128)S(1)} %all_to_all.25), channel_id=1, source_target_pairs={{0,64},{32,96},{64,0},{96,32},{1,65},{33,97},{65,1},{97,33},{2,66}... | collective-permute-start | bytes 196616 | tf_op jit(solution)/shard_map/ppermute | solution.py:480
  88.7 3.7 %collective-permute-start = (s32[32,4,128]{2,1,0:T(4,128)S(1)}, s32[32,4,128]{2,1,0:T(4,128)S(1)}, u32[]{:S(2)}, u32[]{:S(2)}) collective-permute-start(s32[32,4,128]{2,1,0:T(4,128)S(1)} %all_to_all.25), channel_id=1, source_target_pairs={{0,32},{32,64},{64,96},{96,0},{1,33},{33,65},{65,97},{97,1},{2,34}... | collective-permute-start | bytes 196616 | tf_op jit(solution)/shard_map/ppermute | solution.py:480
  129.7 4.2 %collective-permute-start.5 = (bf16[128,256]{1,0:T(8,128)(2,1)S(1)}, bf16[128,256]{1,0:T(8,128)(2,1)S(1)}, u32[]{:S(2)}, u32[]{:S(2)}) collective-permute-start(bf16[128,256]{1,0:T(8,128)(2,1)S(1)} %get-tuple-element.37), channel_id=1, source_target_pairs={{0,96},{32,0},{64,32},{96,64},{1,97},{33,1},{65,33},{97,65},{2,98}... | collective-permute-start | bytes 196616 | tf_op jit(solution)/shard_map/ppermute | solution.py:480
  129.9 4.8 %collective-permute-start.4 = (bf16[128,256]{1,0:T(8,128)(2,1)S(1)}, bf16[128,256]{1,0:T(8,128)(2,1)S(1)}, u32[]{:S(2)}, u32[]{:S(2)}) collective-permute-start(bf16[128,256]{1,0:T(8,128)(2,1)S(1)} %get-tuple-element.38), channel_id=1, source_target_pairs={{0,64},{32,96},{64,0},{96,32},{1,65},{33,97},{65,1},{97,33},{2,66}... | collective-permute-start | bytes 196616 | tf_op jit(solution)/shard_map/ppermute | solution.py:480
  132.2 3.1 %collective-permute-start.3 = (bf16[128,256]{1,0:T(8,128)(2,1)S(1)}, bf16[128,256]{1,0:T(8,128)(2,1)S(1)}, u32[]{:S(2)}, u32[]{:S(2)}) collective-permute-start(bf16[128,256]{1,0:T(8,128)(2,1)S(1)} %get-tuple-element.39), channel_id=1, source_target_pairs={{0,32},{32,64},{64,96},{96,0},{1,33},{33,65},{65,97},{97,1},{2,34}... | collective-permute-start | bytes 196616 | tf_op jit(solution)/shard_map/ppermute | solution.py:480
  136.1 120.7 %all-gather.4.cloned.1.call-start = ((), (), s32[]{:S(2)}) async-start(), calls=%async_computation.5 | async-start | bytes 2162688 | tf_op jit(solution)/shard_map/all_gather | solution.py:583
  190.1 3.5 %collective-permute-start.12 = (bf16[8,1024]{1,0:T(8,128)(2,1)S(1)}, bf16[8,1024]{1,0:T(8,128)(2,1)S(1)}, u32[]{:S(2)}, u32[]{:S(2)}) collective-permute-start(bf16[8,1024]{1,0:T(8,128)(2,1)S(1)} %reduce_sum.55), channel_id=1, source_target_pairs={{0,96},{32,0},{64,32},{96,64},{1,97},{33,1},{65,33},{97,65},{2,98}... | collective-permute-start | bytes 49160 | tf_op jit(solution)/shard_map/ppermute | solution.py:480
  191.5 4.1 %collective-permute-start.13 = (bf16[8,1024]{1,0:T(8,128)(2,1)S(1)}, bf16[8,1024]{1,0:T(8,128)(2,1)S(1)}, u32[]{:S(2)}, u32[]{:S(2)}) collective-permute-start(bf16[8,1024]{1,0:T(8,128)(2,1)S(1)} %reduce_sum.55), channel_id=1, source_target_pairs={{0,64},{32,96},{64,0},{96,32},{1,65},{33,97},{65,1},{97,33},{2,66}... | collective-permute-start | bytes 49160 | tf_op jit(solution)/shard_map/ppermute | solution.py:480
  191.6 4.0 %collective-permute-start.14 = (bf16[8,1024]{1,0:T(8,128)(2,1)S(1)}, bf16[8,1024]{1,0:T(8,128)(2,1)S(1)}, u32[]{:S(2)}, u32[]{:S(2)}) collective-permute-start(bf16[8,1024]{1,0:T(8,128)(2,1)S(1)} %reduce_sum.55), channel_id=1, source_target_pairs={{0,32},{32,64},{64,96},{96,0},{1,33},{33,65},{65,97},{97,1},{2,34}... | collective-permute-start | bytes 49160 | tf_op jit(solution)/shard_map/ppermute | solution.py:480
  221.6 30.4 %copy-start.2 = (bf16[1024,128]{1,0:T(8,128)(2,1)S(1)}, bf16[1024,128]{1,0:T(8,128)(2,1)}, u32[]{:S(2)}) copy-start(bf16[1024,128]{1,0:T(8,128)(2,1)} %scatter.3.refs_0_) | copy-start | bytes 786436
  221.6 32.1 %copy-start.10 = (s32[32,8]{0,1:T(8,128)S(1)}, s32[32,8]{0,1:T(8,128)}, u32[]{:S(2)}) copy-start(s32[32,8]{0,1:T(8,128)} %param.16) | copy-start | bytes 3076
  221.6 34.6 %copy-start.9 = (f32[128,1]{1,0:T(8,128)S(1)}, f32[128,1]{1,0:T(8,128)}, u32[]{:S(2)}) copy-start(f32[128,1]{1,0:T(8,128)} %get-tuple-element.32) | copy-start | bytes 1540
  221.6 30.5 %collective-permute-start.9 = (bf16[1024,128]{1,0:T(8,128)(2,1)}, bf16[1024,128]{1,0:T(8,128)(2,1)S(1)}, u32[]{:S(2)}, u32[]{:S(2)}) collective-permute-start(bf16[1024,128]{1,0:T(8,128)(2,1)} %scatter.3.refs_0_), channel_id=1, source_target_pairs={{0,32},{32,64},{64,96},{96,0},{1,33},{33,65},{65,97},{97,1},{2,34}... | collective-permute-start | bytes 786440 | tf_op jit(solution)/shard_map/ppermute | solution.py:480
  247.8 31.3 %collective-permute-start.6 = (bf16[1024,128]{1,0:T(8,128)(2,1)}, bf16[1024,128]{1,0:T(8,128)(2,1)S(1)}, u32[]{:S(2)}, u32[]{:S(2)}) collective-permute-start(bf16[1024,128]{1,0:T(8,128)(2,1)} %scatter.2.refs_0_), channel_id=1, source_target_pairs={{0,32},{32,64},{64,96},{96,0},{1,33},{33,65},{65,97},{97,1},{2,34}... | collective-permute-start | bytes 786440 | tf_op jit(solution)/shard_map/ppermute | solution.py:480
  249.1 30.1 %collective-permute-start.7 = (bf16[1024,128]{1,0:T(8,128)(2,1)}, bf16[1024,128]{1,0:T(8,128)(2,1)S(1)}, u32[]{:S(2)}, u32[]{:S(2)}) collective-permute-start(bf16[1024,128]{1,0:T(8,128)(2,1)} %scatter.2.refs_0_), channel_id=1, source_target_pairs={{0,64},{32,96},{64,0},{96,32},{1,65},{33,97},{65,1},{97,33},{2,66}... | collective-permute-start | bytes 786440 | tf_op jit(solution)/shard_map/ppermute | solution.py:480
  250.4 28.8 %collective-permute-start.8 = (bf16[1024,128]{1,0:T(8,128)(2,1)}, bf16[1024,128]{1,0:T(8,128)(2,1)S(1)}, u32[]{:S(2)}, u32[]{:S(2)}) collective-permute-start(bf16[1024,128]{1,0:T(8,128)(2,1)} %scatter.2.refs_0_), channel_id=1, source_target_pairs={{0,96},{32,0},{64,32},{96,64},{1,97},{33,1},{65,33},{97,65},{2,98}... | collective-permute-start | bytes 786440 | tf_op jit(solution)/shard_map/ppermute | solution.py:480
  252.0 14.4 %collective-permute-start.10 = (bf16[1024,128]{1,0:T(8,128)(2,1)S(1)}, bf16[1024,128]{1,0:T(8,128)(2,1)S(1)}, u32[]{:S(2)}, u32[]{:S(2)}) collective-permute-start(bf16[1024,128]{1,0:T(8,128)(2,1)S(1)} %copy-done.2), channel_id=1, source_target_pairs={{0,64},{32,96},{64,0},{96,32},{1,65},{33,97},{65,1},{97,33},{2,66}... | collective-permute-start | bytes 786440 | tf_op jit(solution)/shard_map/ppermute | solution.py:480
  252.0 8.9 %copy-start.6 = (bf16[1024,128]{1,0:T(8,128)(2,1)}, bf16[1024,128]{1,0:T(8,128)(2,1)S(1)}, u32[]{:S(2)}) copy-start(bf16[1024,128]{1,0:T(8,128)(2,1)S(1)} %collective-permute-done.9.refs_1_) | copy-start | bytes 786436
  252.1 22.7 %collective-permute-start.11 = (bf16[1024,128]{1,0:T(8,128)(2,1)S(1)}, bf16[1024,128]{1,0:T(8,128)(2,1)S(1)}, u32[]{:S(2)}, u32[]{:S(2)}) collective-permute-start(bf16[1024,128]{1,0:T(8,128)(2,1)S(1)} %copy-done.2), channel_id=1, source_target_pairs={{0,96},{32,0},{64,32},{96,64},{1,97},{33,1},{65,33},{97,65},{2,98}... | collective-permute-start | bytes 786440 | tf_op jit(solution)/shard_map/ppermute | solution.py:480
  (7 other events, 13.8 us)
Sparse Core Ops, SparseCore 0:
  136.2 59.7 all-gather.5
  198.9 43.1 all-gather.3

commit v3 on v1

--- a/solution.py
+++ b/solution.py
@@ -34,7 +34,7 @@
 SOURCES = GROUP * REPS * PAIR * SAMPLES
 SHIFT = 13
 EARLY = 256
-VMEM = 56 * 1024 * 1024
+VMEM = 62 * 1024 * 1024
 
 NT = (((1,), (1,)), ((), ()))
 TN = (((0,), (0,)), ((), ()))
@@ -98,7 +98,7 @@
     earlier = onehot((ki // FEATS == kj // FEATS) & (kj < ki))
     carry0 = dot(earlier, high.astype(BF)) * 256.0 + dot(earlier, low.astype(BF))
 
-    rank_iota = iota((CAP, LANES), 0)
+    rank_iota = iota((CAP // 2, LANES), 0)
     owner_iota = iota((OWNERS, LANES), 0)
 
     of_owner = onehot(iota((KEYS, OWNERS), 0) // FEATS == iota((KEYS, OWNERS), 1))
@@ -123,15 +123,17 @@
             for p in (value & 255, (value >> 8) & 255, value >> 16)
         ]
         left = jnp.concatenate(pieces, axis=0).astype(BF)
-        right = onehot(rank_iota == rank)
+        upper = rank >= CAP // 2
+        left = jnp.concatenate([left * onehot(~upper), left * onehot(upper)], axis=0)
+        right = onehot(rank_iota == (rank & (CAP // 2 - 1)))
         acc = acc + dot(left, right, NT)
         carry = carry + (prefix + hot)[:, LANES - 1 : LANES]
         return carry, acc
 
     _, acc = lax.fori_loop(
-        0, IDROWS, place, (carry0, jnp.zeros((3 * OWNERS, CAP), F32)), unroll=8
-    )
-    acc = acc.astype(I32)
+        0, IDROWS, place, (carry0, jnp.zeros((6 * OWNERS, CAP // 2), F32)), unroll=8
+    )
+    acc = jnp.concatenate([acc[: 3 * OWNERS], acc[3 * OWNERS :]], axis=1).astype(I32)
     out_ref[...] = (
         acc[:OWNERS] + (acc[OWNERS : 2 * OWNERS] << 8) + (acc[2 * OWNERS :] << 16)
     )
@@ -269,29 +271,24 @@
 ):
     step = pl.program_id(0)
 
-    def copies():
-        out = []
-        for layer in range(3):
-            out.append(
-                pltpu.make_async_copy(cross_hbm.at[layer], cross_w.at[layer], sems.at[layer])
-            )
-            out.append(
-                pltpu.make_async_copy(deep_hbm.at[layer], deep_w.at[layer], sems.at[3 + layer])
-            )
-        return out
+    def cross_copy(layer):
+        return pltpu.make_async_copy(cross_hbm.at[layer], cross_w.at[layer], sems.at[layer])
+
+    def deep_copy(layer):
+        return pltpu.make_async_copy(deep_hbm.at[layer], deep_w.at[layer], sems.at[3 + layer])
 
     @pl.when(step == 0)
     def _():
-        for copy in copies():
-            copy.start()
+        for layer in range(3):
+            cross_copy(layer).start()
+        for layer in range(3):
+            deep_copy(layer).start()
         pooled_ref[...] = earlier_ref[...]
 
     pooled_ref[...] += sums_of(packed_ref, got_ref, step, at)
 
     @pl.when(step == OWNERS // POOLED - 1)
     def _():
-        for copy in copies():
-            copy.wait()
         gain = gain_ref[...]
         pooled = pooled_ref[...]
         inverse = lax.rsqrt(jnp.mean(pooled * pooled, axis=1, keepdims=True) + 1e-06)
@@ -299,10 +296,12 @@
         start_ref[...] = start
         current = start
         for layer in range(3):
+            cross_copy(layer).wait()
             product = dot(current, cross_w[layer]) + cbias_ref[layer : layer + 1, :]
             cross_t[layer] = product
             current = (start_ref[...].astype(F32) * product + current.astype(F32)).astype(BF)
         for layer in range(3):
+            deep_copy(layer).wait()
             product = dot(current, deep_w[layer]) + dbias_ref[layer : layer + 1, :]
             deep_t[layer] = product
             current = (product * sigmoid(product)).astype(BF)
@@ -378,7 +377,7 @@
     )(got, packed, earlier, labels, gain, cbias, dbias, out_w, cross, deep)
 
 
-def scatter_kernel(first_ref, last_ref, word_ref, grads_ref, out_ref, wide, *accs):
+def scatter_kernel(first_ref, trips_ref, word_ref, grads_ref, out_ref, wide, *accs):
     step = pl.program_id(0)
 
     @pl.when(step == 0)
@@ -401,7 +400,7 @@
         first = first_ref[listed]
 
         def some(i, _):
-            at = k * LISTED + first + i * ACCS
+            at = first + i * ACCS
             words = [word_ref[at + j] for j in range(ACCS)]
             rows = [wide[pl.ds(word & (SOURCES - 1), 1), :] for word in words]
             olds = [accs[j][pl.ds(words[j] >> SHIFT, 1), :] for j in range(ACCS)]
@@ -409,7 +408,7 @@
                 accs[j][pl.ds(words[j] >> SHIFT, 1), :] = olds[j] + rows[j]
             return 0
 
-        lax.fori_loop(0, (last_ref[listed] - first + ACCS - 1) // ACCS, some, 0)
+        lax.fori_loop(0, trips_ref[listed], some, 0)
         return 0
 
     lax.fori_loop(0, group * REPS, device, 0)
@@ -422,7 +421,7 @@
         out_ref[...] = total.astype(out_ref.dtype)
 
 
-def scatter_call(words, first, last, grads, group=GROUP):
+def scatter_call(words, first, trips, grads, group=GROUP):
     rows = PAIR * VOC
     return pl.pallas_call(
         scatter_kernel,
@@ -444,32 +443,39 @@
         ),
         compiler_params=pltpu.CompilerParams(vmem_limit_bytes=VMEM),
         name="scatter",
-    )(first, last, words, grads)
-
-
-def finish_kernel(order_ref, *refs):
-    parts, rows_ref = refs[:REPS], refs[REPS]
-    source = order_ref[pl.program_id(0)]
+    )(first, trips, words, grads)
+
+
+def finish_kernel(place_ref, *refs):
+    parts, out, wide, sems = refs[:REPS], refs[REPS], refs[REPS + 1], refs[REPS + 2]
+    copies = []
     for k in range(REPS):
-
-        @pl.when(source // PAIR == k)
-        def _():
-            rows_ref[...] = parts[k][lax.rem(source, PAIR)].astype(F32)
-
-
-def finish_call(order, parts):
+        for f in range(PAIR):
+            n = k * PAIR + f
+            wide[n] = parts[k][f].astype(F32)
+            to = pl.multiple_of(place_ref[n] * VOC, VOC)
+            copies.append(
+                pltpu.make_async_copy(wide.at[n], out.at[pl.ds(to, VOC), :], sems.at[n])
+            )
+            copies[-1].start()
+    for copy in copies:
+        copy.wait()
+
+
+def finish_call(places, parts):
     return pl.pallas_call(
         finish_kernel,
         out_shape=jax.ShapeDtypeStruct((ROWS, EMB), F32),
-        grid_spec=pltpu.PrefetchScalarGridSpec(
-            num_scalar_prefetch=1,
-            grid=(FEATS,),
-            in_specs=[pl.BlockSpec((PAIR, VOC, EMB), lambda i, o: (0, 0, 0)) for _ in parts],
-            out_specs=pl.BlockSpec((VOC, EMB), lambda i, o: (i, 0)),
-        ),
-        compiler_params=pltpu.CompilerParams(vmem_limit_bytes=VMEM),
+        in_specs=[pl.BlockSpec(memory_space=pltpu.SMEM)]
+        + [pl.BlockSpec(memory_space=pltpu.VMEM) for _ in parts],
+        out_specs=pl.BlockSpec(memory_space=pl.ANY),
+        scratch_shapes=[
+            pltpu.VMEM((FEATS, VOC, EMB), F32),
+            pltpu.SemaphoreType.DMA((FEATS,)),
+        ],
+        compiler_params=pltpu.CompilerParams(vmem_limit_bytes=16 * 1024 * 1024),
         name="finish",
-    )(order, *parts)
+    )(places, *parts)
 
 
 def from_before(x, axis, k):
@@ -549,11 +555,16 @@
         ((0, 0), (0, 0), (0, 0), (0, LISTED - CAP)),
         constant_values=(PAIR * VOC) << SHIFT,
     ).reshape(-1)
-    first_word = jnp.sum((valid & (within < 0)).astype(I32), axis=3).reshape(-1)
-    last_word = jnp.sum((valid & (within < PAIR)).astype(I32), axis=3).reshape(-1)
+    below = jnp.sum((valid & (within < 0)).astype(I32), axis=3)
+    upto = jnp.sum((valid & (within < PAIR)).astype(I32), axis=3)
+    places = lax.broadcasted_iota(I32, below.shape, 1) * REPS + lax.broadcasted_iota(
+        I32, below.shape, 2
+    )
+    first_word = (places * LISTED + below).reshape(-1)
+    trips = ((upto - below + ACCS - 1) >> (ACCS.bit_length() - 1)).reshape(-1)
     sums_early = pool_call(got_early, packed, 0)
-    got_late, sums_early, words, first_word, last_word = lax.optimization_barrier(
-        (got_late, sums_early, words, first_word, last_word)
+    got_late, sums_early, words, first_word, trips = lax.optimization_barrier(
+        (got_late, sums_early, words, first_word, trips)
     )
 
     logits, grads, first_local = tower_call(
@@ -582,14 +593,12 @@
         in_order(eight, "rep", rep), "shard", axis=0, tiled=True
     ).astype(F32)
 
-    part = scatter_call(words, first_word, last_word, all_grads).reshape(PAIR, VOC, EMB)
+    part = scatter_call(words, first_word, trips, all_grads).reshape(PAIR, VOC, EMB)
     parts = [part] + [from_before(part, "rep", k) for k in range(1, REPS)]
     slots = feature_slot[lax.axis_index("shard")]
-    feature_of = jnp.argmax(
-        slots[None, :] == jnp.arange(FEATS, dtype=I32)[:, None], axis=1
-    ).astype(I32)
-    order = ((rep - feature_of // PAIR) & (REPS - 1)) * PAIR + feature_of % PAIR
-    row_grad = finish_call(order, parts)
+    holder = (rep - jnp.arange(REPS, dtype=I32)) % REPS
+    features = holder[:, None] * PAIR + jnp.arange(PAIR, dtype=I32)[None, :]
+    row_grad = finish_call(slots[features.reshape(-1)], parts)
     return (row_grad, first_grad, logits.reshape(SAMPLES))
 
 

time: 287 us -> 272 us (0.948)
  the two profiles are of different devices: /device:TPU:96 before, /device:TPU:1 now
where the time goes in v3:
time: 272 us; the launch traced here: 271 us
  Pallas kernels  101 us (37%)
  blocking collectives  68.3 us (25%)
  waiting for transfers between devices  46 us (17%)
  starting transfers between devices  24.1 us (9%)
  between operations  14.3 us (5%)
  local copies, waits for them, and re-layouts  9.09 us (3%)
  other arithmetic  7.62 us (3%)
    all_to_all x2, blocking collectives, exchange(): return lax.all_to_all(x, axis, split_axis=0, concat_axis=0, tiled=True)  51.7 us
    pallas_call x1, Pallas kernels, scatter_call(): pl.pallas_call(scatter_kernel, out_shape=jax.ShapeDtypeStruct((rows, EMB)...  41.9 us
    all_to_all x2, waiting for transfers between devices, exchange(): return lax.all_to_all(x, axis, split_axis=0, concat_axis=0, tiled=True)  25.5 us
    pallas_call x2, Pallas kernels, gather_call(): pl.pallas_call(gather_kernel, out_shape=jax.ShapeDtypeStruct((OWNERS, dep...  23.7 us
    ppermute x12, waiting for transfers between devices, from_before(): return lax.ppermute(x, axis, [(i, (i + k) % n) for i in range(n)])  20.5 us
    pallas_call x1, Pallas kernels, tower_call(): pl.pallas_call(functools.partial(tower_kernel, CAP - got.shape[1]), grid=...  17.4 us
    all_to_all x1, blocking collectives, body(): lax.all_to_all(packed.reshape(OWNERS, 4, 128), 'shard', split_axis=0, con...  16.6 us
    ppermute x12, starting transfers between devices, from_before(): return lax.ppermute(x, axis, [(i, (i + k) % n) for i in range(n)])  14 us
  transfers between devices with their start and end apart: 16, of which 12 were waited for; matrix products, arithmetic and copies ran while one was open for 4% of the time, Pallas kernels for 22%

profile of v3, /device:TPU:1, one launch (start us, length us, event | category | flops | bytes accessed | tf_op | source)
XLA Modules:
  0.0 270.6 jit_solution(11665073578130606437)
XLA Ops:
  8.5 10.0 %index.1.packed_ref = s32[32,512]{1,0:T(8,128)} custom-call(s32[1,8192]{1,0:T(1,128)} %ids_in.1, s32[1,8192]{1,0:T(1,128)} %bitcast.49, s32[1,1024]{1,0:T(1,128)} %len_in.1, s32[32,8]{1,0:T(8,128)} %copy.21.slot_ref), custom_call_target="tpu_custom_call" | custom-call | tf_op jit(solution)/shard_map/index/pallas_call | solution.py:143
  19.4 16.6 %all_to_all.25 = s32[32,4,128]{2,1,0:T(4,128)S(1)} all-to-all(s32[32,4,128]{2,1,0:T(4,128)S(1)} %reshape.104), channel_id=1, replica_groups=mesh['rep'=4,'shard'=32] {'shard'}, dimensions={0} | all-to-all | bytes 131072 | tf_op jit(solution)/shard_map/all_to_all | solution.py:519
  36.7 11.9 %gather.9 = bf16[32,256,128]{2,1,0:T(8,128)(2,1)} custom-call(s32[8192]{0:T(1024)} %bitcast.41, bf16[8192,128]{1,0:T(8,128)(2,1)} %table_ref.3), custom_call_target="tpu_custom_call" | custom-call | tf_op jit(solution)/shard_map/gather/pallas_call | solution.py:182
  48.5 4.7 %all-to-all-start.2 = ((bf16[32,256,128]{2,1,0:T(8,128)(2,1)}), bf16[32,256,128]{2,1,0:T(8,128)(2,1)}, u32[]{:S(2)}, u32[]{:S(2)}) async-start(bf16[32,256,128]{2,1,0:T(8,128)(2,1)} %gather.9), calls=%async_computation.2 | async-start | bytes 4194304 | tf_op jit(solution)/shard_map/all_to_all | solution.py:525
  53.9 11.9 %gather.8 = bf16[32,256,128]{2,1,0:T(8,128)(2,1)} custom-call(s32[8192]{0:T(1024)} %bitcast.42, bf16[8192,128]{1,0:T(8,128)(2,1)} %table_ref.3), custom_call_target="tpu_custom_call" | custom-call | tf_op jit(solution)/shard_map/gather/pallas_call | solution.py:182
  65.8 15.9 %all-to-all-done.2.got_ref = bf16[32,256,128]{2,1,0:T(8,128)(2,1)} async-done(((bf16[32,256,128]{2,1,0:T(8,128)(2,1)}), bf16[32,256,128]{2,1,0:T(8,128)(2,1)}, u32[]{:S(2)}, u32[]{:S(2)}) %all-to-all-start.2) | async-done | bytes 2097184 | tf_op jit(solution)/shard_map/all_to_all | solution.py:525
  81.7 5.2 %all-to-all-start.1 = ((bf16[32,256,128]{2,1,0:T(8,128)(2,1)}), bf16[32,256,128]{2,1,0:T(8,128)(2,1)}, u32[]{:S(2)}, u32[]{:S(2)}) async-start(bf16[32,256,128]{2,1,0:T(8,128)(2,1)} %gather.8), calls=%async_computation.1 | async-start | bytes 4194304 | tf_op jit(solution)/shard_map/all_to_all | solution.py:525
  87.8 2.7 %collective-permute-start.2 = (s32[32,4,128]{2,1,0:T(4,128)S(1)}, s32[32,4,128]{2,1,0:T(4,128)S(1)}, u32[]{:S(2)}, u32[]{:S(2)}) collective-permute-start(s32[32,4,128]{2,1,0:T(4,128)S(1)} %all_to_all.25), channel_id=1, source_target_pairs={{0,96},{32,0},{64,32},{96,64},{1,97},{33,1},{65,33},{97,65},{2,98}... | collective-permute-start | bytes 196616 | tf_op jit(solution)/shard_map/ppermute | solution.py:485
  91.9 3.7 %collective-permute-done.1 = s32[32,4,128]{2,1,0:T(4,128)S(1)} collective-permute-done((s32[32,4,128]{2,1,0:T(4,128)S(1)}, s32[32,4,128]{2,1,0:T(4,128)S(1)}, u32[]{:S(2)}, u32[]{:S(2)}) %collective-permute-start.1) | collective-permute-done | bytes 65568 | tf_op jit(solution)/shard_map/ppermute | solution.py:485
  96.5 1.4 convert_reduce_fusion
  100.3 5.5 %pool.1.earlier_ref = f32[128,1024]{1,0:T(8,128)} custom-call(bf16[32,256,128]{2,1,0:T(8,128)(2,1)} %all-to-all-done.2.got_ref, s32[32,512]{1,0:T(8,128)} %index.1.packed_ref), custom_call_target="tpu_custom_call" | custom-call | tf_op jit(solution)/shard_map/pool/pallas_call | solution.py:230
  105.8 9.6 %all-to-all-done.1.got_ref = bf16[32,256,128]{2,1,0:T(8,128)(2,1)} async-done(((bf16[32,256,128]{2,1,0:T(8,128)(2,1)}), bf16[32,256,128]{2,1,0:T(8,128)(2,1)}, u32[]{:S(2)}, u32[]{:S(2)}) %all-to-all-start.1) | async-done | bytes 2097184 | tf_op jit(solution)/shard_map/all_to_all | solution.py:525
  115.4 17.4 %tower.1 = (f32[128,1]{1,0:T(8,128)}, bf16[4,128,256]{2,1,0:T(8,128)(2,1)}, bf16[4,256,1024]{2,1,0:T(8,128)(2,1)}) custom-call(bf16[32,256,128]{2,1,0:T(8,128)(2,1)} %all-to-all-done.1.got_ref, s32[32,512]{1,0:T(8,128)} %index.1.packed_ref, f32[128,1024]{1,0:T(8,128)} %pool.1.earlier_ref, s32[128,1]{1,0:T(8,128)} %copy.22.labels_ref, f32[1,1024]{1,0:T(1,128)} %bitcast.50, ...), custom_call_target="tpu_custom_call" | custom-call | tf_op jit(solution)/shard_map/tower/pallas_call | solution.py:340
  133.8 2.8 %collective-permute-start.5 = (bf16[128,256]{1,0:T(8,128)(2,1)S(1)}, bf16[128,256]{1,0:T(8,128)(2,1)S(1)}, u32[]{:S(2)}, u32[]{:S(2)}) collective-permute-start(bf16[128,256]{1,0:T(8,128)(2,1)S(1)} %get-tuple-element.34), channel_id=1, source_target_pairs={{0,96},{32,0},{64,32},{96,64},{1,97},{33,1},{65,33},{97,65},{2,98}... | collective-permute-start | bytes 196616 | tf_op jit(solution)/shard_map/ppermute | solution.py:485
  137.9 3.4 %collective-permute-done.4 = bf16[128,256]{1,0:T(8,128)(2,1)S(1)} collective-permute-done((bf16[128,256]{1,0:T(8,128)(2,1)S(1)}, bf16[128,256]{1,0:T(8,128)(2,1)S(1)}, u32[]{:S(2)}, u32[]{:S(2)}) %collective-permute-start.4) | collective-permute-done | bytes 65568 | tf_op jit(solution)/shard_map/ppermute | solution.py:485
  142.7 27.7 %all_to_all.26 = bf16[4,256,1024]{2,1,0:T(8,128)(2,1)S(1)} all-to-all(bf16[4,256,1024]{2,1,0:T(8,128)(2,1)} %get-tuple-element.29), channel_id=1, replica_groups=mesh['rep'=4,'shard'=32] {'rep'}, dimensions={0} | all-to-all | bytes 4194304 | tf_op jit(solution)/shard_map/all_to_all | solution.py:525
  170.8 24.1 %all_to_all.27 = bf16[32,8,1024]{2,1,0:T(8,128)(2,1)S(1)} all-to-all(bf16[32,8,1024]{2,1,0:T(8,128)(2,1)S(1)} %bitcast.37), channel_id=1, replica_groups=mesh['rep'=4,'shard'=32] {'shard'}, dimensions={0} | all-to-all | bytes 1048576 | tf_op jit(solution)/shard_map/all_to_all | solution.py:525
  197.9 2.9 %collective-permute-done.10 = bf16[8,1024]{1,0:T(8,128)(2,1)S(1)} collective-permute-done((bf16[8,1024]{1,0:T(8,128)(2,1)S(1)}, bf16[8,1024]{1,0:T(8,128)(2,1)S(1)}, u32[]{:S(2)}, u32[]{:S(2)}) %collective-permute-start.10) | collective-permute-done | bytes 16416 | tf_op jit(solution)/shard_map/ppermute | solution.py:485
  201.8 41.9 %scatter.1 = bf16[2048,128]{1,0:T(8,128)(2,1)} custom-call(s32[128]{0:T(128)} %add.132.first_ref, s32[128]{0:T(128)} %reshape.116.trips_ref, s32[73728]{0:T(1024)} %reshape.108.word_ref, bf16[32,4,128,256]{3,2,1,0:T(8,128)(2,1)} %bitcast.36), custom_call_target="tpu_custom_call" | custom-call | tf_op jit(solution)/shard_map/scatter/pallas_call | solution.py:426
  243.7 2.1 collective-permute-start.8
  249.1 4.1 %convert_element_type.15 = f32[1024,1024]{1,0:T(8,128)} convert(bf16[1024,1024]{1,0:T(8,128)(2,1)} %all-gather.4.cloned.1.call-done) | non-fusion elementwise | flops 1048576 | bytes 6291456 | tf_op jit(solution)/shard_map/convert_element_type | solution.py:594
  253.2 4.6 %collective-permute-done.8.refs_3_ = bf16[2,1024,128]{2,1,0:T(8,128)(2,1)S(1)} collective-permute-done((bf16[2,1024,128]{2,1,0:T(8,128)(2,1)}, bf16[2,1024,128]{2,1,0:T(8,128)(2,1)S(1)}, u32[]{:S(2)}, u32[]{:S(2)}) %collective-permute-start.8) | collective-permute-done | bytes 524320 | tf_op jit(solution)/shard_map/ppermute | solution.py:485
  257.9 3.3 %collective-permute-done.6.refs_1_ = bf16[2,1024,128]{2,1,0:T(8,128)(2,1)S(1)} collective-permute-done((bf16[2,1024,128]{2,1,0:T(8,128)(2,1)}, bf16[2,1024,128]{2,1,0:T(8,128)(2,1)S(1)}, u32[]{:S(2)}, u32[]{:S(2)}) %collective-permute-start.6) | collective-permute-done | bytes 524320 | tf_op jit(solution)/shard_map/ppermute | solution.py:485
  261.1 2.6 finish.1
  (64 shorter events, 20.3 us)
Async XLA Ops:
  48.5 33.2 %all-to-all-start.2 = ((bf16[32,256,128]{2,1,0:T(8,128)(2,1)}), bf16[32,256,128]{2,1,0:T(8,128)(2,1)}, u32[]{:S(2)}, u32[]{:S(2)}) async-start(bf16[32,256,128]{2,1,0:T(8,128)(2,1)} %gather.9), calls=%async_computation.2 | async-start | bytes 4194304 | tf_op jit(solution)/shard_map/all_to_all | solution.py:525
  65.8 21.3 %copy-start.3 = (s32[128]{0:T(128)S(1)}, s32[128]{0:T(128)}, u32[]{:S(2)}) copy-start(s32[128]{0:T(128)} %param.17) | copy-start | bytes 1540
  81.7 33.6 %all-to-all-start.1 = ((bf16[32,256,128]{2,1,0:T(8,128)(2,1)}), bf16[32,256,128]{2,1,0:T(8,128)(2,1)}, u32[]{:S(2)}, u32[]{:S(2)}) async-start(bf16[32,256,128]{2,1,0:T(8,128)(2,1)} %gather.8), calls=%async_computation.1 | async-start | bytes 4194304 | tf_op jit(solution)/shard_map/all_to_all | solution.py:525
  86.9 114.8 %all-gather.6.cloned.1.call-start = ((), (), s32[]{:S(2)}) async-start(), calls=%async_computation.6 | async-start | bytes 8650752 | tf_op jit(solution)/shard_map/all_gather | solution.py:589
  87.8 4.1 %collective-permute-start.2 = (s32[32,4,128]{2,1,0:T(4,128)S(1)}, s32[32,4,128]{2,1,0:T(4,128)S(1)}, u32[]{:S(2)}, u32[]{:S(2)}) collective-permute-start(s32[32,4,128]{2,1,0:T(4,128)S(1)} %all_to_all.25), channel_id=1, source_target_pairs={{0,96},{32,0},{64,32},{96,64},{1,97},{33,1},{65,33},{97,65},{2,98}... | collective-permute-start | bytes 196616 | tf_op jit(solution)/shard_map/ppermute | solution.py:485
  90.5 5.0 %collective-permute-start.1 = (s32[32,4,128]{2,1,0:T(4,128)S(1)}, s32[32,4,128]{2,1,0:T(4,128)S(1)}, u32[]{:S(2)}, u32[]{:S(2)}) collective-permute-start(s32[32,4,128]{2,1,0:T(4,128)S(1)} %all_to_all.25), channel_id=1, source_target_pairs={{0,64},{32,96},{64,0},{96,32},{1,65},{33,97},{65,1},{97,33},{2,66}... | collective-permute-start | bytes 196616 | tf_op jit(solution)/shard_map/ppermute | solution.py:485
  90.9 5.6 %collective-permute-start = (s32[32,4,128]{2,1,0:T(4,128)S(1)}, s32[32,4,128]{2,1,0:T(4,128)S(1)}, u32[]{:S(2)}, u32[]{:S(2)}) collective-permute-start(s32[32,4,128]{2,1,0:T(4,128)S(1)} %all_to_all.25), channel_id=1, source_target_pairs={{0,32},{32,64},{64,96},{96,0},{1,33},{33,65},{65,97},{97,1},{2,34}... | collective-permute-start | bytes 196616 | tf_op jit(solution)/shard_map/ppermute | solution.py:485
  133.8 4.1 %collective-permute-start.5 = (bf16[128,256]{1,0:T(8,128)(2,1)S(1)}, bf16[128,256]{1,0:T(8,128)(2,1)S(1)}, u32[]{:S(2)}, u32[]{:S(2)}) collective-permute-start(bf16[128,256]{1,0:T(8,128)(2,1)S(1)} %get-tuple-element.34), channel_id=1, source_target_pairs={{0,96},{32,0},{64,32},{96,64},{1,97},{33,1},{65,33},{97,65},{2,98}... | collective-permute-start | bytes 196616 | tf_op jit(solution)/shard_map/ppermute | solution.py:485
  136.6 4.7 %collective-permute-start.4 = (bf16[128,256]{1,0:T(8,128)(2,1)S(1)}, bf16[128,256]{1,0:T(8,128)(2,1)S(1)}, u32[]{:S(2)}, u32[]{:S(2)}) collective-permute-start(bf16[128,256]{1,0:T(8,128)(2,1)S(1)} %get-tuple-element.35), channel_id=1, source_target_pairs={{0,64},{32,96},{64,0},{96,32},{1,65},{33,97},{65,1},{97,33},{2,66}... | collective-permute-start | bytes 196616 | tf_op jit(solution)/shard_map/ppermute | solution.py:485
  136.9 5.0 %collective-permute-start.3 = (bf16[128,256]{1,0:T(8,128)(2,1)S(1)}, bf16[128,256]{1,0:T(8,128)(2,1)S(1)}, u32[]{:S(2)}, u32[]{:S(2)}) collective-permute-start(bf16[128,256]{1,0:T(8,128)(2,1)S(1)} %get-tuple-element.36), channel_id=1, source_target_pairs={{0,32},{32,64},{64,96},{96,0},{1,33},{33,65},{65,97},{97,1},{2,34}... | collective-permute-start | bytes 196616 | tf_op jit(solution)/shard_map/ppermute | solution.py:485
  142.7 106.5 %all-gather.4.cloned.1.call-start = ((), (), s32[]{:S(2)}) async-start(), calls=%async_computation.5 | async-start | bytes 2162688 | tf_op jit(solution)/shard_map/all_gather | solution.py:592
  170.4 31.2 %copy-start.2 = (s32[32,8]{0,1:T(8,128)S(1)}, s32[32,8]{0,1:T(8,128)}, u32[]{:S(2)}) copy-start(s32[32,8]{0,1:T(8,128)} %param.16) | copy-start | bytes 3076
  194.9 2.9 %collective-permute-start.9 = (bf16[8,1024]{1,0:T(8,128)(2,1)S(1)}, bf16[8,1024]{1,0:T(8,128)(2,1)S(1)}, u32[]{:S(2)}, u32[]{:S(2)}) collective-permute-start(bf16[8,1024]{1,0:T(8,128)(2,1)S(1)} %reduce_sum.45), channel_id=1, source_target_pairs={{0,96},{32,0},{64,32},{96,64},{1,97},{33,1},{65,33},{97,65},{2,98}... | collective-permute-start | bytes 49160 | tf_op jit(solution)/shard_map/ppermute | solution.py:485
  196.1 4.7 %collective-permute-start.11 = (bf16[8,1024]{1,0:T(8,128)(2,1)S(1)}, bf16[8,1024]{1,0:T(8,128)(2,1)S(1)}, u32[]{:S(2)}, u32[]{:S(2)}) collective-permute-start(bf16[8,1024]{1,0:T(8,128)(2,1)S(1)} %reduce_sum.45), channel_id=1, source_target_pairs={{0,32},{32,64},{64,96},{96,0},{1,33},{33,65},{65,97},{97,1},{2,34}... | collective-permute-start | bytes 49160 | tf_op jit(solution)/shard_map/ppermute | solution.py:485
  196.7 4.1 %collective-permute-start.10 = (bf16[8,1024]{1,0:T(8,128)(2,1)S(1)}, bf16[8,1024]{1,0:T(8,128)(2,1)S(1)}, u32[]{:S(2)}, u32[]{:S(2)}) collective-permute-start(bf16[8,1024]{1,0:T(8,128)(2,1)S(1)} %reduce_sum.45), channel_id=1, source_target_pairs={{0,64},{32,96},{64,0},{96,32},{1,65},{33,97},{65,1},{97,33},{2,66}... | collective-permute-start | bytes 49160 | tf_op jit(solution)/shard_map/ppermute | solution.py:485
  201.8 46.7 %copy-start.1 = (f32[128,1]{1,0:T(8,128)S(1)}, f32[128,1]{1,0:T(8,128)}, u32[]{:S(2)}) copy-start(f32[128,1]{1,0:T(8,128)} %get-tuple-element.30) | copy-start | bytes 1540
  243.7 14.2 %collective-permute-start.8 = (bf16[2,1024,128]{2,1,0:T(8,128)(2,1)}, bf16[2,1024,128]{2,1,0:T(8,128)(2,1)S(1)}, u32[]{:S(2)}, u32[]{:S(2)}) collective-permute-start(bf16[2,1024,128]{2,1,0:T(8,128)(2,1)} %bitcast.32), channel_id=1, source_target_pairs={{0,96},{32,0},{64,32},{96,64},{1,97},{33,1},{65,33},{97,65},{2,98}... | collective-permute-start | bytes 1572872 | tf_op jit(solution)/shard_map/ppermute | solution.py:485
  245.8 12.1 %collective-permute-start.7 = (bf16[2,1024,128]{2,1,0:T(8,128)(2,1)}, bf16[2,1024,128]{2,1,0:T(8,128)(2,1)S(1)}, u32[]{:S(2)}, u32[]{:S(2)}) collective-permute-start(bf16[2,1024,128]{2,1,0:T(8,128)(2,1)} %bitcast.33), channel_id=1, source_target_pairs={{0,64},{32,96},{64,0},{96,32},{1,65},{33,97},{65,1},{97,33},{2,66}... | collective-permute-start | bytes 1572872 | tf_op jit(solution)/shard_map/ppermute | solution.py:485
  246.8 14.3 %collective-permute-start.6 = (bf16[2,1024,128]{2,1,0:T(8,128)(2,1)}, bf16[2,1024,128]{2,1,0:T(8,128)(2,1)S(1)}, u32[]{:S(2)}, u32[]{:S(2)}) collective-permute-start(bf16[2,1024,128]{2,1,0:T(8,128)(2,1)} %bitcast.34), channel_id=1, source_target_pairs={{0,32},{32,64},{64,96},{96,0},{1,33},{33,65},{65,97},{97,1},{2,34}... | collective-permute-start | bytes 1572872 | tf_op jit(solution)/shard_map/ppermute | solution.py:485
  249.1 12.0 %copy-start = (bf16[2048,128]{1,0:T(8,128)(2,1)S(1)}, bf16[2048,128]{1,0:T(8,128)(2,1)}, u32[]{:S(2)}) copy-start(bf16[2048,128]{1,0:T(8,128)(2,1)} %scatter.1) | copy-start | bytes 1572868
Sparse Core Ops, SparseCore 0:
  142.8 56.2 all-gather.5
  201.9 43.3 all-gather.3

commit v4 on v3

--- a/solution.py
+++ b/solution.py
@@ -33,7 +33,7 @@
 LISTS = 4
 SOURCES = GROUP * REPS * PAIR * SAMPLES
 SHIFT = 13
-EARLY = 256
+EARLY = 128
 VMEM = 62 * 1024 * 1024
 
 NT = (((1,), (1,)), ((), ()))
@@ -53,7 +53,7 @@
 
 
 def index_kernel(
-    ids_in, owner_in, len_in, slot_ref, out_ref, ids_ref, owner_ref, len_ref, bag_ref, key_ref
+    ids_in, owner_in, len_in, slot_ref, out_ref, send_ref, ids_ref, owner_ref, len_ref, bag_ref, key_ref
 ):
     for r in range(IDROWS):
         ids_ref[r : r + 1, :] = ids_in[:, r * LANES : (r + 1) * LANES]
@@ -102,7 +102,7 @@
     owner_iota = iota((OWNERS, LANES), 0)
 
     of_owner = onehot(iota((KEYS, OWNERS), 0) // FEATS == iota((KEYS, OWNERS), 1))
-    by_owner = dot(of_owner, slot_ref[...].astype(F32).astype(BF))
+    by_owner = dot(of_owner, slot_ref[...].astype(F32).astype(BF), NT)
     is_feature = (iota((KEYS, FEATS), 0) & (FEATS - 1)) == iota((KEYS, FEATS), 1)
     slots = jnp.sum(jnp.where(is_feature, by_owner, 0.0), axis=1, keepdims=True)
     carry0 = carry0 + jnp.broadcast_to(slots, (KEYS, LANES)) * VOC
@@ -134,15 +134,19 @@
         0, IDROWS, place, (carry0, jnp.zeros((6 * OWNERS, CAP // 2), F32)), unroll=8
     )
     acc = jnp.concatenate([acc[: 3 * OWNERS], acc[3 * OWNERS :]], axis=1).astype(I32)
-    out_ref[...] = (
-        acc[:OWNERS] + (acc[OWNERS : 2 * OWNERS] << 8) + (acc[2 * OWNERS :] << 16)
-    )
+    packed = acc[:OWNERS] + (acc[OWNERS : 2 * OWNERS] << 8) + (acc[2 * OWNERS :] << 16)
+    out_ref[...] = packed
+    for c in range(CAP // 128):
+        send_ref[:, c, :] = packed[:, c * 128 : (c + 1) * 128]
 
 
 def index_call(ids, owners, lengths, slots):
     return pl.pallas_call(
         index_kernel,
-        out_shape=jax.ShapeDtypeStruct((OWNERS, CAP), I32),
+        out_shape=[
+            jax.ShapeDtypeStruct((OWNERS, CAP), I32),
+            jax.ShapeDtypeStruct((OWNERS, CAP // 128, 128), I32),
+        ],
         scratch_shapes=[
             pltpu.VMEM((IDROWS, LANES), I32),
             pltpu.VMEM((IDROWS, LANES), I32),
@@ -155,7 +159,7 @@
     )(ids, owners, lengths, slots)
 
 
-def gather_kernel(row_ref, table_ref, out_ref, wide, picked):
+def gather_kernel(offset, row_ref, table_ref, out_ref, wide, picked):
     step = pl.program_id(0)
     depth = out_ref.shape[1]
 
@@ -164,7 +168,7 @@
         wide[...] = table_ref[...].astype(F32)
 
     for part in range(LISTS):
-        base = (step * LISTS + part) * depth
+        base = (step * LISTS + part) * CAP + offset
 
         def some(i, _):
             at = i * 32
@@ -177,10 +181,9 @@
         out_ref[part] = picked[part * depth : (part + 1) * depth, :].astype(BF)
 
 
-def gather_call(rows, table):
-    depth = rows.shape[1]
+def gather_call(rows, table, offset, depth):
     return pl.pallas_call(
-        gather_kernel,
+        functools.partial(gather_kernel, offset),
         out_shape=jax.ShapeDtypeStruct((OWNERS, depth, EMB), BF),
         grid_spec=pltpu.PrefetchScalarGridSpec(
             num_scalar_prefetch=1,
@@ -191,14 +194,15 @@
         ),
         compiler_params=pltpu.CompilerParams(vmem_limit_bytes=VMEM),
         name="gather",
-    )(rows.reshape(-1), table)
+    )(rows, table)
 
 
 def sums_of(packed_ref, got_ref, step, at):
     rows, masked = [], []
     depth = got_ref.shape[1]
+    group = packed_ref[pl.ds(pl.multiple_of(step * POOLED, POOLED), POOLED), at : at + depth]
     for i in range(POOLED):
-        packed = packed_ref[pl.ds(step * POOLED + i, 1), at : at + depth]
+        packed = group[i : i + 1, :]
         bag = packed & (BAGS - 1)
         sample = jnp.where(packed > 0, bag >> 3, -1)
         rows.append(onehot(iota((SAMPLES, depth), 0) == sample))
@@ -247,6 +251,7 @@
 
 def tower_kernel(
     at,
+    rep_ref,
     got_ref,
     packed_ref,
     earlier_ref,
@@ -258,17 +263,11 @@
     cross_hbm,
     deep_hbm,
     logits_ref,
-    grads_ref,
     first_ref,
-    pooled_ref,
-    cross_w,
-    deep_w,
-    start_ref,
-    cross_t,
-    deep_t,
-    gx_ref,
-    sems,
+    *refs,
 ):
+    grad_refs = refs[:REPS]
+    pooled_ref, cross_w, deep_w, start_ref, cross_t, deep_t, gx_ref, sems, result_ref = refs[REPS:]
     step = pl.program_id(0)
 
     def cross_copy(layer):
@@ -329,11 +328,14 @@
         inverse = lax.rsqrt(jnp.mean(pooled * pooled, axis=1, keepdims=True) + 1e-06)
         mean = jnp.mean(scaled * pooled, axis=1, keepdims=True)
         result = (inverse * scaled - pooled * (inverse * inverse * inverse) * mean).astype(BF)
-        for r in range(REPS):
-            grads_ref[r] = result[:, r * PAIR * EMB : (r + 1) * PAIR * EMB]
-
-
-def tower_call(got, packed, earlier, labels, gain, cross, cbias, deep, dbias, out_w):
+        result_ref[...] = result
+        for k in range(REPS):
+            block = (rep_ref[0] + k) & (REPS - 1)
+            columns = pl.ds(pl.multiple_of(block * (PAIR * EMB), PAIR * EMB), PAIR * EMB)
+            grad_refs[k][...] = result_ref[:, columns]
+
+
+def tower_call(rep, got, packed, earlier, labels, gain, cross, cbias, deep, dbias, out_w):
     def whole(shape):
         return pl.BlockSpec(shape, lambda i: (0,) * len(shape))
 
@@ -341,6 +343,7 @@
         functools.partial(tower_kernel, CAP - got.shape[1]),
         grid=(OWNERS // POOLED,),
         in_specs=[
+            pl.BlockSpec(memory_space=pltpu.SMEM),
             pl.BlockSpec((POOLED, got.shape[1], EMB), lambda i: (i, 0, 0)),
             whole((OWNERS, CAP)),
             whole((SAMPLES, WIDTH)),
@@ -354,14 +357,14 @@
         ],
         out_specs=[
             whole((SAMPLES, 1)),
-            whole((REPS, SAMPLES, PAIR * EMB)),
             whole((REPS, OWNERS * 8, WIDTH)),
-        ],
+        ]
+        + [whole((SAMPLES, PAIR * EMB))] * REPS,
         out_shape=[
             jax.ShapeDtypeStruct((SAMPLES, 1), F32),
-            jax.ShapeDtypeStruct((REPS, SAMPLES, PAIR * EMB), BF),
             jax.ShapeDtypeStruct((REPS, OWNERS * 8, WIDTH), BF),
-        ],
+        ]
+        + [jax.ShapeDtypeStruct((SAMPLES, PAIR * EMB), BF)] * REPS,
         scratch_shapes=[
             pltpu.VMEM((SAMPLES, WIDTH), F32),
             pltpu.VMEM((3, WIDTH, WIDTH), BF),
@@ -371,10 +374,11 @@
             pltpu.VMEM((3, SAMPLES, WIDTH), F32),
             pltpu.VMEM((SAMPLES, WIDTH), F32),
             pltpu.SemaphoreType.DMA((6,)),
+            pltpu.VMEM((SAMPLES, WIDTH), BF),
         ],
         compiler_params=pltpu.CompilerParams(vmem_limit_bytes=VMEM),
         name="tower",
-    )(got, packed, earlier, labels, gain, cbias, dbias, out_w, cross, deep)
+    )(rep, got, packed, earlier, labels, gain, cbias, dbias, out_w, cross, deep)
 
 
 def scatter_kernel(first_ref, trips_ref, word_ref, grads_ref, out_ref, wide, *accs):
@@ -510,25 +514,23 @@
     deep_bias,
     out_weight,
 ):
-    packed = index_call(
+    packed, sent = index_call(
         row_ids,
         row_owner.reshape(1, IDS),
         lengths,
-        feature_slot,
-    )
-    asked = lax.all_to_all(
-        packed.reshape(OWNERS, 4, 128), "shard", split_axis=0, concat_axis=0, tiled=True
-    )
-    rows = ((asked >> 10) & (ROWS - 1)).reshape(OWNERS, CAP)
+        feature_slot.T,
+    )
+    asked = lax.all_to_all(sent, "shard", split_axis=0, concat_axis=0, tiled=True)
+    rows = ((asked >> 10) & (ROWS - 1)).reshape(-1)
 
     def exchange(x, axis):
         return lax.all_to_all(x, axis, split_axis=0, concat_axis=0, tiled=True)
 
-    picked_early = gather_call(rows[:, :EARLY], embed_table)
+    picked_early = gather_call(rows, embed_table, 0, EARLY)
     picked_early, lists = lax.optimization_barrier((picked_early, asked))
     got_early = exchange(picked_early, "shard")
     picked_late, lists = lax.optimization_barrier(
-        (gather_call(rows[:, EARLY:], embed_table), lists)
+        (gather_call(rows, embed_table, EARLY, CAP - EARLY), lists)
     )
     got_late = exchange(picked_late, "shard")
 
@@ -567,7 +569,8 @@
         (got_late, sums_early, words, first_word, trips)
     )
 
-    logits, grads, first_local = tower_call(
+    logits, first_local, *grads = tower_call(
+        rep.reshape(1),
         got_late,
         packed,
         sums_early,
@@ -579,12 +582,7 @@
         deep_bias,
         out_weight.reshape(1, WIDTH),
     )
-    mine = jnp.stack(
-        [
-            from_before(lax.dynamic_index_in_dim(grads, (rep + k) % REPS, 0, False), "rep", k)
-            for k in range(REPS)
-        ]
-    )
+    mine = jnp.stack([from_before(grads[k], "rep", k) for k in range(REPS)])
     mine, first_local = lax.optimization_barrier((mine, first_local))
     all_grads = lax.all_gather(mine, "shard", axis=0)
     quarter = summed(exchange(first_local, "rep"))

time: 272 us -> 272 us (level)
  the two profiles are of different devices: /device:TPU:1 before, /device:TPU:65 now
where the time goes in v4:
time: 272 us; the launch traced here: 271 us
  Pallas kernels  103 us (38%)
  blocking collectives  64.8 us (24%)
  waiting for transfers between devices  47.6 us (18%)
  starting transfers between devices  28 us (10%)
  between operations  14.2 us (5%)
  other arithmetic  9.08 us (3%)
  local copies, waits for them, and re-layouts  4.65 us (2%)
    all_to_all x2, blocking collectives, exchange(): return lax.all_to_all(x, axis, split_axis=0, concat_axis=0, tiled=True)  51.7 us
    pallas_call x1, Pallas kernels, scatter_call(): pl.pallas_call(scatter_kernel, out_shape=jax.ShapeDtypeStruct((rows, EMB)...  42.1 us
    ppermute x12, waiting for transfers between devices, from_before(): return lax.ppermute(x, axis, [(i, (i + k) % n) for i in range(n)])  27.1 us
    pallas_call x2, Pallas kernels, gather_call(): pl.pallas_call(functools.partial(gather_kernel, offset), out_shape=jax.Sh...  25.5 us
    all_to_all x2, waiting for transfers between devices, exchange(): return lax.all_to_all(x, axis, split_axis=0, concat_axis=0, tiled=True)  19.4 us
    pallas_call x1, Pallas kernels, tower_call(): pl.pallas_call(functools.partial(tower_kernel, CAP - got.shape[1]), grid=...  18.2 us
    ppermute x12, starting transfers between devices, from_before(): return lax.ppermute(x, axis, [(i, (i + k) % n) for i in range(n)])  14.3 us
    all_to_all x2, starting transfers between devices, exchange(): return lax.all_to_all(x, axis, split_axis=0, concat_axis=0, tiled=True)  13.6 us
  transfers between devices with their start and end apart: 16, of which 11 were waited for; matrix products, arithmetic and copies ran while one was open for 4% of the time, Pallas kernels for 23%

profile of v4, /device:TPU:65, one launch (start us, length us, event | category | flops | bytes accessed | tf_op | source)
XLA Modules:
  0.0 271.4 jit_solution(1249395851810270905)
XLA Ops:
  7.2 10.1 %index.1 = (s32[32,512]{1,0:T(8,128)}, s32[32,4,128]{2,1,0:T(4,128)}) custom-call(s32[1,8192]{1,0:T(1,128)} %ids_in.1, s32[1,8192]{1,0:T(1,128)} %bitcast.36, s32[1,1024]{1,0:T(1,128)} %len_in.1, s32[8,32]{1,0:T(8,128)} %bitcast.37), custom_call_target="tpu_custom_call" | custom-call | tf_op jit(solution)/shard_map/index/pallas_call | solution.py:144
  17.2 13.2 %all_to_all.25 = s32[32,4,128]{2,1,0:T(4,128)S(1)} all-to-all(s32[32,4,128]{2,1,0:T(4,128)} %get-tuple-element.22), channel_id=1, replica_groups=mesh['rep'=4,'shard'=32] {'shard'}, dimensions={0} | all-to-all | bytes 131072 | tf_op jit(solution)/shard_map/all_to_all | solution.py:523
  31.0 8.7 %gather.9 = bf16[32,128,128]{2,1,0:T(8,128)(2,1)} custom-call(s32[16384]{0:T(1024)} %bitcast.27, bf16[8192,128]{1,0:T(8,128)(2,1)} %table_ref.3), custom_call_target="tpu_custom_call" | custom-call | tf_op jit(solution)/shard_map/gather/pallas_call | solution.py:185
  39.8 6.1 %all-to-all-start.2 = ((bf16[32,128,128]{2,1,0:T(8,128)(2,1)}), bf16[32,128,128]{2,1,0:T(8,128)(2,1)S(1)}, u32[]{:S(2)}, u32[]{:S(2)}) async-start(bf16[32,128,128]{2,1,0:T(8,128)(2,1)} %gather.9), calls=%async_computation.2 | async-start | bytes 2097152 | tf_op jit(solution)/shard_map/all_to_all | solution.py:527
  45.9 16.8 %gather.8 = bf16[32,384,128]{2,1,0:T(8,128)(2,1)} custom-call(s32[16384]{0:T(1024)} %bitcast.28, bf16[8192,128]{1,0:T(8,128)(2,1)} %table_ref.3), custom_call_target="tpu_custom_call" | custom-call | tf_op jit(solution)/shard_map/gather/pallas_call | solution.py:185
  62.7 7.5 %all-to-all-start.1 = ((bf16[32,384,128]{2,1,0:T(8,128)(2,1)}), bf16[32,384,128]{2,1,0:T(8,128)(2,1)}, u32[]{:S(2)}, u32[]{:S(2)}) async-start(bf16[32,384,128]{2,1,0:T(8,128)(2,1)} %gather.8), calls=%async_computation.1 | async-start | bytes 6291456 | tf_op jit(solution)/shard_map/all_to_all | solution.py:527
  71.0 2.7 %collective-permute-start.2 = (s32[32,4,128]{2,1,0:T(4,128)S(1)}, s32[32,4,128]{2,1,0:T(4,128)S(1)}, u32[]{:S(2)}, u32[]{:S(2)}) collective-permute-start(s32[32,4,128]{2,1,0:T(4,128)S(1)} %all_to_all.25), channel_id=1, source_target_pairs={{0,96},{32,0},{64,32},{96,64},{1,97},{33,1},{65,33},{97,65},{2,98}... | collective-permute-start | bytes 196616 | tf_op jit(solution)/shard_map/ppermute | solution.py:489
  75.1 3.7 %collective-permute-done.1 = s32[32,4,128]{2,1,0:T(4,128)S(1)} collective-permute-done((s32[32,4,128]{2,1,0:T(4,128)S(1)}, s32[32,4,128]{2,1,0:T(4,128)S(1)}, u32[]{:S(2)}, u32[]{:S(2)}) %collective-permute-start.1) | collective-permute-done | bytes 65568 | tf_op jit(solution)/shard_map/ppermute | solution.py:489
  78.8 1.5 collective-permute-done
  84.1 4.5 %pool.1.earlier_ref = f32[128,1024]{1,0:T(8,128)} custom-call(bf16[32,128,128]{2,1,0:T(8,128)(2,1)} %copy-done.1, s32[32,512]{1,0:T(8,128)} %get-tuple-element.26.packed_ref), custom_call_target="tpu_custom_call" | custom-call | tf_op jit(solution)/shard_map/pool/pallas_call | solution.py:234
  88.6 19.4 %all-to-all-done.1.got_ref = bf16[32,384,128]{2,1,0:T(8,128)(2,1)} async-done(((bf16[32,384,128]{2,1,0:T(8,128)(2,1)}), bf16[32,384,128]{2,1,0:T(8,128)(2,1)}, u32[]{:S(2)}, u32[]{:S(2)}) %all-to-all-start.1) | async-done | bytes 3145760 | tf_op jit(solution)/shard_map/all_to_all | solution.py:527
  108.0 18.2 %tower.1 = (f32[128,1]{1,0:T(8,128)}, bf16[4,256,1024]{2,1,0:T(8,128)(2,1)}, bf16[128,256]{1,0:T(8,128)(2,1)}, bf16[128,256]{1,0:T(8,128)(2,1)}, bf16[128,256]{1,0:T(8,128)(2,1)}, /*index=5*/bf16[128,256]{1,0:T(8,128)(2,1)}) custom-call(s32[1]{0:T(128)} %bitcast.8.rep_ref, bf16[32,384,128]{2,1,0:T(8,128)(2,1)} %all-to-all-done.1.got_ref, ...), custom_call_target="tpu_custom_call" | custom-call | tf_op jit(solution)/shard_map/tower/pallas_call | solution.py:342
  127.6 2.6 collective-permute-start.4
  131.3 1.6 collective-permute-done.4
  134.0 1.6 pad_maximum_fusion
  135.7 27.6 %all_to_all.26 = bf16[4,256,1024]{2,1,0:T(8,128)(2,1)S(1)} all-to-all(bf16[4,256,1024]{2,1,0:T(8,128)(2,1)} %get-tuple-element.39), channel_id=1, replica_groups=mesh['rep'=4,'shard'=32] {'rep'}, dimensions={0} | all-to-all | bytes 4194304 | tf_op jit(solution)/shard_map/all_to_all | solution.py:527
  163.7 24.1 %all_to_all.27 = bf16[32,8,1024]{2,1,0:T(8,128)(2,1)S(1)} all-to-all(bf16[32,8,1024]{2,1,0:T(8,128)(2,1)S(1)} %bitcast.25), channel_id=1, replica_groups=mesh['rep'=4,'shard'=32] {'shard'}, dimensions={0} | all-to-all | bytes 1048576 | tf_op jit(solution)/shard_map/all_to_all | solution.py:527
  191.1 2.6 collective-permute-done.10
  195.8 42.1 %scatter.1 = bf16[2048,128]{1,0:T(8,128)(2,1)} custom-call(s32[128]{0:T(128)} %add.97.first_ref, s32[128]{0:T(128)} %reshape.108.trips_ref, s32[73728]{0:T(1024)} %reshape.99.word_ref, bf16[32,4,128,256]{3,2,1,0:T(8,128)(2,1)} %bitcast.24), custom_call_target="tpu_custom_call" | custom-call | tf_op jit(solution)/shard_map/scatter/pallas_call | solution.py:430
  237.9 2.4 collective-permute-start.8
  242.4 4.1 %convert_element_type.15 = f32[1024,1024]{1,0:T(8,128)} convert(bf16[1024,1024]{1,0:T(8,128)(2,1)} %all-gather.4.cloned.1.call-done) | non-fusion elementwise | flops 1048576 | bytes 6291456 | tf_op jit(solution)/shard_map/convert_element_type | solution.py:592
  246.5 12.2 %collective-permute-done.8.refs_3_ = bf16[2,1024,128]{2,1,0:T(8,128)(2,1)S(1)} collective-permute-done((bf16[2,1024,128]{2,1,0:T(8,128)(2,1)}, bf16[2,1024,128]{2,1,0:T(8,128)(2,1)S(1)}, u32[]{:S(2)}, u32[]{:S(2)}) %collective-permute-start.8) | collective-permute-done | bytes 524320 | tf_op jit(solution)/shard_map/ppermute | solution.py:489
  258.7 3.3 %collective-permute-done.6.refs_1_ = bf16[2,1024,128]{2,1,0:T(8,128)(2,1)S(1)} collective-permute-done((bf16[2,1024,128]{2,1,0:T(8,128)(2,1)}, bf16[2,1024,128]{2,1,0:T(8,128)(2,1)S(1)}, u32[]{:S(2)}, u32[]{:S(2)}) %collective-permute-start.6) | collective-permute-done | bytes 524320 | tf_op jit(solution)/shard_map/ppermute | solution.py:489
  261.9 2.6 finish.1
  (59 shorter events, 18.1 us)
Async XLA Ops:
  39.8 22.9 %all-to-all-start.2 = ((bf16[32,128,128]{2,1,0:T(8,128)(2,1)}), bf16[32,128,128]{2,1,0:T(8,128)(2,1)S(1)}, u32[]{:S(2)}, u32[]{:S(2)}) async-start(bf16[32,128,128]{2,1,0:T(8,128)(2,1)} %gather.9), calls=%async_computation.2 | async-start | bytes 2097152 | tf_op jit(solution)/shard_map/all_to_all | solution.py:527
  62.7 7.6 %copy-start.4 = (s32[128]{0:T(128)S(1)}, s32[128]{0:T(128)}, u32[]{:S(2)}) copy-start(s32[128]{0:T(128)} %param.17) | copy-start | bytes 1540
  62.7 7.6 %copy-start.1 = (bf16[32,128,128]{2,1,0:T(8,128)(2,1)}, bf16[32,128,128]{2,1,0:T(8,128)(2,1)S(1)}, u32[]{:S(2)}) copy-start(bf16[32,128,128]{2,1,0:T(8,128)(2,1)S(1)} %all-to-all-done.2.got_ref) | copy-start | bytes 3145732
  62.7 45.3 %all-to-all-start.1 = ((bf16[32,384,128]{2,1,0:T(8,128)(2,1)}), bf16[32,384,128]{2,1,0:T(8,128)(2,1)}, u32[]{:S(2)}, u32[]{:S(2)}) async-start(bf16[32,384,128]{2,1,0:T(8,128)(2,1)} %gather.8), calls=%async_computation.1 | async-start | bytes 6291456 | tf_op jit(solution)/shard_map/all_to_all | solution.py:527
  70.2 125.6 %all-gather.6.cloned.1.call-start = ((), (), s32[]{:S(2)}) async-start(), calls=%async_computation.6 | async-start | bytes 8650752 | tf_op jit(solution)/shard_map/all_gather | solution.py:587
  71.0 4.1 %collective-permute-start.2 = (s32[32,4,128]{2,1,0:T(4,128)S(1)}, s32[32,4,128]{2,1,0:T(4,128)S(1)}, u32[]{:S(2)}, u32[]{:S(2)}) collective-permute-start(s32[32,4,128]{2,1,0:T(4,128)S(1)} %all_to_all.25), channel_id=1, source_target_pairs={{0,96},{32,0},{64,32},{96,64},{1,97},{33,1},{65,33},{97,65},{2,98}... | collective-permute-start | bytes 196616 | tf_op jit(solution)/shard_map/ppermute | solution.py:489
  73.8 5.0 %collective-permute-start.1 = (s32[32,4,128]{2,1,0:T(4,128)S(1)}, s32[32,4,128]{2,1,0:T(4,128)S(1)}, u32[]{:S(2)}, u32[]{:S(2)}) collective-permute-start(s32[32,4,128]{2,1,0:T(4,128)S(1)} %all_to_all.25), channel_id=1, source_target_pairs={{0,64},{32,96},{64,0},{96,32},{1,65},{33,97},{65,1},{97,33},{2,66}... | collective-permute-start | bytes 196616 | tf_op jit(solution)/shard_map/ppermute | solution.py:489
  74.1 6.2 %collective-permute-start = (s32[32,4,128]{2,1,0:T(4,128)S(1)}, s32[32,4,128]{2,1,0:T(4,128)S(1)}, u32[]{:S(2)}, u32[]{:S(2)}) collective-permute-start(s32[32,4,128]{2,1,0:T(4,128)S(1)} %all_to_all.25), channel_id=1, source_target_pairs={{0,32},{32,64},{64,96},{96,0},{1,33},{33,65},{65,97},{97,1},{2,34}... | collective-permute-start | bytes 196616 | tf_op jit(solution)/shard_map/ppermute | solution.py:489
  126.2 5.1 %collective-permute-start.3 = (bf16[128,256]{1,0:T(8,128)(2,1)}, bf16[128,256]{1,0:T(8,128)(2,1)S(1)}, u32[]{:S(2)}, u32[]{:S(2)}) collective-permute-start(bf16[128,256]{1,0:T(8,128)(2,1)} %get-tuple-element.34), channel_id=1, source_target_pairs={{0,32},{32,64},{64,96},{96,0},{1,33},{33,65},{65,97},{97,1},{2,34}... | collective-permute-start | bytes 196616 | tf_op jit(solution)/shard_map/ppermute | solution.py:489
  127.6 5.3 %collective-permute-start.4 = (bf16[128,256]{1,0:T(8,128)(2,1)}, bf16[128,256]{1,0:T(8,128)(2,1)S(1)}, u32[]{:S(2)}, u32[]{:S(2)}) collective-permute-start(bf16[128,256]{1,0:T(8,128)(2,1)} %get-tuple-element.35), channel_id=1, source_target_pairs={{0,64},{32,96},{64,0},{96,32},{1,65},{33,97},{65,1},{97,33},{2,66}... | collective-permute-start | bytes 196616 | tf_op jit(solution)/shard_map/ppermute | solution.py:489
  130.2 3.8 %collective-permute-start.5 = (bf16[128,256]{1,0:T(8,128)(2,1)}, bf16[128,256]{1,0:T(8,128)(2,1)S(1)}, u32[]{:S(2)}, u32[]{:S(2)}) collective-permute-start(bf16[128,256]{1,0:T(8,128)(2,1)} %get-tuple-element.36), channel_id=1, source_target_pairs={{0,96},{32,0},{64,32},{96,64},{1,97},{33,1},{65,33},{97,65},{2,98}... | collective-permute-start | bytes 196616 | tf_op jit(solution)/shard_map/ppermute | solution.py:489
  135.6 106.8 %all-gather.4.cloned.1.call-start = ((), (), s32[]{:S(2)}) async-start(), calls=%async_computation.5 | async-start | bytes 2162688 | tf_op jit(solution)/shard_map/all_gather | solution.py:590
  163.2 31.2 %copy-start.3 = (s32[32,8]{0,1:T(8,128)S(1)}, s32[32,8]{0,1:T(8,128)}, u32[]{:S(2)}) copy-start(s32[32,8]{0,1:T(8,128)} %param.16) | copy-start | bytes 3076
  187.8 3.3 %collective-permute-start.9 = (bf16[8,1024]{1,0:T(8,128)(2,1)S(1)}, bf16[8,1024]{1,0:T(8,128)(2,1)S(1)}, u32[]{:S(2)}, u32[]{:S(2)}) collective-permute-start(bf16[8,1024]{1,0:T(8,128)(2,1)S(1)} %reduce_sum.45), channel_id=1, source_target_pairs={{0,96},{32,0},{64,32},{96,64},{1,97},{33,1},{65,33},{97,65},{2,98}... | collective-permute-start | bytes 49160 | tf_op jit(solution)/shard_map/ppermute | solution.py:489
  189.0 4.7 %collective-permute-start.11 = (bf16[8,1024]{1,0:T(8,128)(2,1)S(1)}, bf16[8,1024]{1,0:T(8,128)(2,1)S(1)}, u32[]{:S(2)}, u32[]{:S(2)}) collective-permute-start(bf16[8,1024]{1,0:T(8,128)(2,1)S(1)} %reduce_sum.45), channel_id=1, source_target_pairs={{0,32},{32,64},{64,96},{96,0},{1,33},{33,65},{65,97},{97,1},{2,34}... | collective-permute-start | bytes 49160 | tf_op jit(solution)/shard_map/ppermute | solution.py:489
  189.6 4.1 %collective-permute-start.10 = (bf16[8,1024]{1,0:T(8,128)(2,1)S(1)}, bf16[8,1024]{1,0:T(8,128)(2,1)S(1)}, u32[]{:S(2)}, u32[]{:S(2)}) collective-permute-start(bf16[8,1024]{1,0:T(8,128)(2,1)S(1)} %reduce_sum.45), channel_id=1, source_target_pairs={{0,64},{32,96},{64,0},{96,32},{1,65},{33,97},{65,1},{97,33},{2,66}... | collective-permute-start | bytes 49160 | tf_op jit(solution)/shard_map/ppermute | solution.py:489
  195.8 45.9 %copy-start.2 = (f32[128,1]{1,0:T(8,128)S(1)}, f32[128,1]{1,0:T(8,128)}, u32[]{:S(2)}) copy-start(f32[128,1]{1,0:T(8,128)} %get-tuple-element.40) | copy-start | bytes 1540
  237.9 20.8 %collective-permute-start.8 = (bf16[2,1024,128]{2,1,0:T(8,128)(2,1)}, bf16[2,1024,128]{2,1,0:T(8,128)(2,1)S(1)}, u32[]{:S(2)}, u32[]{:S(2)}) collective-permute-start(bf16[2,1024,128]{2,1,0:T(8,128)(2,1)} %bitcast.20), channel_id=1, source_target_pairs={{0,96},{32,0},{64,32},{96,64},{1,97},{33,1},{65,33},{97,65},{2,98}... | collective-permute-start | bytes 1572872 | tf_op jit(solution)/shard_map/ppermute | solution.py:489
  240.3 18.4 %collective-permute-start.7 = (bf16[2,1024,128]{2,1,0:T(8,128)(2,1)}, bf16[2,1024,128]{2,1,0:T(8,128)(2,1)S(1)}, u32[]{:S(2)}, u32[]{:S(2)}) collective-permute-start(bf16[2,1024,128]{2,1,0:T(8,128)(2,1)} %bitcast.21), channel_id=1, source_target_pairs={{0,64},{32,96},{64,0},{96,32},{1,65},{33,97},{65,1},{97,33},{2,66}... | collective-permute-start | bytes 1572872 | tf_op jit(solution)/shard_map/ppermute | solution.py:489
  240.3 21.6 %collective-permute-start.6 = (bf16[2,1024,128]{2,1,0:T(8,128)(2,1)}, bf16[2,1024,128]{2,1,0:T(8,128)(2,1)S(1)}, u32[]{:S(2)}, u32[]{:S(2)}) collective-permute-start(bf16[2,1024,128]{2,1,0:T(8,128)(2,1)} %bitcast.22), channel_id=1, source_target_pairs={{0,32},{32,64},{64,96},{96,0},{1,33},{33,65},{65,97},{97,1},{2,34}... | collective-permute-start | bytes 1572872 | tf_op jit(solution)/shard_map/ppermute | solution.py:489
  242.4 19.6 %copy-start = (bf16[2048,128]{1,0:T(8,128)(2,1)S(1)}, bf16[2048,128]{1,0:T(8,128)(2,1)}, u32[]{:S(2)}) copy-start(bf16[2048,128]{1,0:T(8,128)(2,1)} %scatter.1) | copy-start | bytes 1572868
Sparse Core Ops, SparseCore 0:
  135.7 60.0 all-gather.5
  198.6 43.0 all-gather.3

commit v5 on v4

--- a/solution.py
+++ b/solution.py
@@ -27,10 +27,10 @@
 LANES = 256
 IDROWS = IDS // LANES
 ACCS = 16
-POOLED = 8
+POOLED = 16
 GROUP = 4
 LISTED = CAP + 64
-LISTS = 4
+LISTS = 8
 SOURCES = GROUP * REPS * PAIR * SAMPLES
 SHIFT = 13
 EARLY = 128
@@ -131,7 +131,7 @@
         return carry, acc
 
     _, acc = lax.fori_loop(
-        0, IDROWS, place, (carry0, jnp.zeros((6 * OWNERS, CAP // 2), F32)), unroll=8
+        0, IDROWS, place, (carry0, jnp.zeros((6 * OWNERS, CAP // 2), F32)), unroll=IDROWS
     )
     acc = jnp.concatenate([acc[: 3 * OWNERS], acc[3 * OWNERS :]], axis=1).astype(I32)
     packed = acc[:OWNERS] + (acc[OWNERS : 2 * OWNERS] << 8) + (acc[2 * OWNERS :] << 16)
@@ -168,7 +168,7 @@
         wide[...] = table_ref[...].astype(F32)
 
     for part in range(LISTS):
-        base = (step * LISTS + part) * CAP + offset
+        base = part * CAP + offset
 
         def some(i, _):
             at = i * 32
@@ -185,13 +185,13 @@
     return pl.pallas_call(
         functools.partial(gather_kernel, offset),
         out_shape=jax.ShapeDtypeStruct((OWNERS, depth, EMB), BF),
-        grid_spec=pltpu.PrefetchScalarGridSpec(
-            num_scalar_prefetch=1,
-            grid=(OWNERS // LISTS,),
-            in_specs=[pl.BlockSpec((ROWS, EMB), lambda i, r: (0, 0))],
-            out_specs=pl.BlockSpec((LISTS, depth, EMB), lambda i, r: (i, 0, 0)),
-            scratch_shapes=[pltpu.VMEM((ROWS, EMB), F32), pltpu.VMEM((LISTS * depth, EMB), F32)],
-        ),
+        grid=(OWNERS // LISTS,),
+        in_specs=[
+            pl.BlockSpec((LISTS * CAP,), lambda i: (i,), memory_space=pltpu.SMEM),
+            pl.BlockSpec((ROWS, EMB), lambda i: (0, 0)),
+        ],
+        out_specs=pl.BlockSpec((LISTS, depth, EMB), lambda i: (i, 0, 0)),
+        scratch_shapes=[pltpu.VMEM((ROWS, EMB), F32), pltpu.VMEM((LISTS * depth, EMB), F32)],
         compiler_params=pltpu.CompilerParams(vmem_limit_bytes=VMEM),
         name="gather",
     )(rows, table)

time: 272 us -> 268 us (0.985)
  the two profiles are of different devices: /device:TPU:65 before, /device:TPU:71 now
where the time goes in v5:
time: 268 us; the launch traced here: 267 us
  Pallas kernels  93.9 us (35%)
  blocking collectives  62.3 us (23%)
  waiting for transfers between devices  52.8 us (20%)
  starting transfers between devices  30 us (11%)
  between operations  14.2 us (5%)
  other arithmetic  9.08 us (3%)
  local copies, waits for them, and re-layouts  4.65 us (2%)
    all_to_all x2, blocking collectives, exchange(): return lax.all_to_all(x, axis, split_axis=0, concat_axis=0, tiled=True)  50.7 us
    pallas_call x1, Pallas kernels, scatter_call(): pl.pallas_call(scatter_kernel, out_shape=jax.ShapeDtypeStruct((rows, EMB)...  42.3 us
    ppermute x12, waiting for transfers between devices, from_before(): return lax.ppermute(x, axis, [(i, (i + k) % n) for i in range(n)])  31.5 us
    pallas_call x2, Pallas kernels, gather_call(): pl.pallas_call(functools.partial(gather_kernel, offset), out_shape=jax.Sh...  21.2 us
    all_to_all x2, waiting for transfers between devices, exchange(): return lax.all_to_all(x, axis, split_axis=0, concat_axis=0, tiled=True)  19.7 us
    all_to_all x2, starting transfers between devices, exchange(): return lax.all_to_all(x, axis, split_axis=0, concat_axis=0, tiled=True)  15.2 us
    pallas_call x1, Pallas kernels, tower_call(): pl.pallas_call(functools.partial(tower_kernel, CAP - got.shape[1]), grid=...  15.1 us
    ppermute x12, starting transfers between devices, from_before(): return lax.ppermute(x, axis, [(i, (i + k) % n) for i in range(n)])  14.7 us
  transfers between devices with their start and end apart: 16, of which 12 were waited for; matrix products, arithmetic and copies ran while one was open for 4% of the time, Pallas kernels for 23%

profile of v5, /device:TPU:71, one launch (start us, length us, event | category | flops | bytes accessed | tf_op | source)
XLA Modules:
  0.0 266.9 jit_solution(7812619143683824800)
XLA Ops:
  7.2 9.1 %index.1 = (s32[32,512]{1,0:T(8,128)}, s32[32,4,128]{2,1,0:T(4,128)}) custom-call(s32[1,8192]{1,0:T(1,128)} %ids_in.1, s32[1,8192]{1,0:T(1,128)} %bitcast.36, s32[1,1024]{1,0:T(1,128)} %len_in.1, s32[8,32]{1,0:T(8,128)} %bitcast.37), custom_call_target="tpu_custom_call" | custom-call | tf_op jit(solution)/shard_map/index/pallas_call | solution.py:144
  16.3 11.6 %all_to_all.25 = s32[32,4,128]{2,1,0:T(4,128)S(1)} all-to-all(s32[32,4,128]{2,1,0:T(4,128)} %get-tuple-element.22), channel_id=1, replica_groups=mesh['rep'=4,'shard'=32] {'shard'}, dimensions={0} | all-to-all | bytes 131072 | tf_op jit(solution)/shard_map/all_to_all | solution.py:523
  28.5 6.6 %gather.9 = bf16[32,128,128]{2,1,0:T(8,128)(2,1)} custom-call(s32[16384]{0:T(1024)} %bitcast.27, bf16[8192,128]{1,0:T(8,128)(2,1)} %table_ref.3), custom_call_target="tpu_custom_call" | custom-call | tf_op jit(solution)/shard_map/gather/pallas_call | solution.py:185
  35.1 7.8 %all-to-all-start.2 = ((bf16[32,128,128]{2,1,0:T(8,128)(2,1)}), bf16[32,128,128]{2,1,0:T(8,128)(2,1)S(1)}, u32[]{:S(2)}, u32[]{:S(2)}) async-start(bf16[32,128,128]{2,1,0:T(8,128)(2,1)} %gather.9), calls=%async_computation.2 | async-start | bytes 2097152 | tf_op jit(solution)/shard_map/all_to_all | solution.py:527
  42.9 14.6 %gather.8 = bf16[32,384,128]{2,1,0:T(8,128)(2,1)} custom-call(s32[16384]{0:T(1024)} %bitcast.28, bf16[8192,128]{1,0:T(8,128)(2,1)} %table_ref.3), custom_call_target="tpu_custom_call" | custom-call | tf_op jit(solution)/shard_map/gather/pallas_call | solution.py:185
  57.5 7.4 %all-to-all-start.1 = ((bf16[32,384,128]{2,1,0:T(8,128)(2,1)}), bf16[32,384,128]{2,1,0:T(8,128)(2,1)}, u32[]{:S(2)}, u32[]{:S(2)}) async-start(bf16[32,384,128]{2,1,0:T(8,128)(2,1)} %gather.8), calls=%async_computation.1 | async-start | bytes 6291456 | tf_op jit(solution)/shard_map/all_to_all | solution.py:527
  65.7 2.7 %collective-permute-start.2 = (s32[32,4,128]{2,1,0:T(4,128)S(1)}, s32[32,4,128]{2,1,0:T(4,128)S(1)}, u32[]{:S(2)}, u32[]{:S(2)}) collective-permute-start(s32[32,4,128]{2,1,0:T(4,128)S(1)} %all_to_all.25), channel_id=1, source_target_pairs={{0,96},{32,0},{64,32},{96,64},{1,97},{33,1},{65,33},{97,65},{2,98}... | collective-permute-start | bytes 196616 | tf_op jit(solution)/shard_map/ppermute | solution.py:489
  69.8 3.7 %collective-permute-done.1 = s32[32,4,128]{2,1,0:T(4,128)S(1)} collective-permute-done((s32[32,4,128]{2,1,0:T(4,128)S(1)}, s32[32,4,128]{2,1,0:T(4,128)S(1)}, u32[]{:S(2)}, u32[]{:S(2)}) %collective-permute-start.1) | collective-permute-done | bytes 65568 | tf_op jit(solution)/shard_map/ppermute | solution.py:489
  78.8 3.6 %pool.1.earlier_ref = f32[128,1024]{1,0:T(8,128)} custom-call(bf16[32,128,128]{2,1,0:T(8,128)(2,1)} %copy-done.1, s32[32,512]{1,0:T(8,128)} %get-tuple-element.26.packed_ref), custom_call_target="tpu_custom_call" | custom-call | tf_op jit(solution)/shard_map/pool/pallas_call | solution.py:234
  82.4 19.7 %all-to-all-done.1.got_ref = bf16[32,384,128]{2,1,0:T(8,128)(2,1)} async-done(((bf16[32,384,128]{2,1,0:T(8,128)(2,1)}), bf16[32,384,128]{2,1,0:T(8,128)(2,1)}, u32[]{:S(2)}, u32[]{:S(2)}) %all-to-all-start.1) | async-done | bytes 3145760 | tf_op jit(solution)/shard_map/all_to_all | solution.py:527
  102.1 15.1 %tower.1 = (f32[128,1]{1,0:T(8,128)}, bf16[4,256,1024]{2,1,0:T(8,128)(2,1)}, bf16[128,256]{1,0:T(8,128)(2,1)}, bf16[128,256]{1,0:T(8,128)(2,1)}, bf16[128,256]{1,0:T(8,128)(2,1)}, /*index=5*/bf16[128,256]{1,0:T(8,128)(2,1)}) custom-call(s32[1]{0:T(128)} %bitcast.8.rep_ref, bf16[32,384,128]{2,1,0:T(8,128)(2,1)} %all-to-all-done.1.got_ref, ...), custom_call_target="tpu_custom_call" | custom-call | tf_op jit(solution)/shard_map/tower/pallas_call | solution.py:342
  118.5 2.6 collective-permute-start.4
  122.2 1.6 collective-permute-done.4
  125.0 1.6 pad_maximum_fusion
  126.6 27.6 %all_to_all.26 = bf16[4,256,1024]{2,1,0:T(8,128)(2,1)S(1)} all-to-all(bf16[4,256,1024]{2,1,0:T(8,128)(2,1)} %get-tuple-element.39), channel_id=1, replica_groups=mesh['rep'=4,'shard'=32] {'rep'}, dimensions={0} | all-to-all | bytes 4194304 | tf_op jit(solution)/shard_map/all_to_all | solution.py:527
  154.6 23.1 %all_to_all.27 = bf16[32,8,1024]{2,1,0:T(8,128)(2,1)S(1)} all-to-all(bf16[32,8,1024]{2,1,0:T(8,128)(2,1)S(1)} %bitcast.25), channel_id=1, replica_groups=mesh['rep'=4,'shard'=32] {'shard'}, dimensions={0} | all-to-all | bytes 1048576 | tf_op jit(solution)/shard_map/all_to_all | solution.py:527
  180.9 2.6 collective-permute-done.10
  186.0 42.3 %scatter.1 = bf16[2048,128]{1,0:T(8,128)(2,1)} custom-call(s32[128]{0:T(128)} %add.97.first_ref, s32[128]{0:T(128)} %reshape.108.trips_ref, s32[73728]{0:T(1024)} %reshape.99.word_ref, bf16[32,4,128,256]{3,2,1,0:T(8,128)(2,1)} %bitcast.24), custom_call_target="tpu_custom_call" | custom-call | tf_op jit(solution)/shard_map/scatter/pallas_call | solution.py:430
  228.3 2.3 collective-permute-start.8
  233.4 4.1 %convert_element_type.15 = f32[1024,1024]{1,0:T(8,128)} convert(bf16[1024,1024]{1,0:T(8,128)(2,1)} %all-gather.4.cloned.1.call-done) | non-fusion elementwise | flops 1048576 | bytes 6291456 | tf_op jit(solution)/shard_map/convert_element_type | solution.py:592
  237.6 5.5 %collective-permute-done.8.refs_3_ = bf16[2,1024,128]{2,1,0:T(8,128)(2,1)S(1)} collective-permute-done((bf16[2,1024,128]{2,1,0:T(8,128)(2,1)}, bf16[2,1024,128]{2,1,0:T(8,128)(2,1)S(1)}, u32[]{:S(2)}, u32[]{:S(2)}) %collective-permute-start.8) | collective-permute-done | bytes 524320 | tf_op jit(solution)/shard_map/ppermute | solution.py:489
  243.1 2.0 collective-permute-done.7.refs_2_
  245.1 12.3 %collective-permute-done.6.refs_1_ = bf16[2,1024,128]{2,1,0:T(8,128)(2,1)S(1)} collective-permute-done((bf16[2,1024,128]{2,1,0:T(8,128)(2,1)}, bf16[2,1024,128]{2,1,0:T(8,128)(2,1)S(1)}, u32[]{:S(2)}, u32[]{:S(2)}) %collective-permute-start.6) | collective-permute-done | bytes 524320 | tf_op jit(solution)/shard_map/ppermute | solution.py:489
  257.4 2.6 finish.1
  (59 shorter events, 20.5 us)
Async XLA Ops:
  35.1 22.4 %all-to-all-start.2 = ((bf16[32,128,128]{2,1,0:T(8,128)(2,1)}), bf16[32,128,128]{2,1,0:T(8,128)(2,1)S(1)}, u32[]{:S(2)}, u32[]{:S(2)}) async-start(bf16[32,128,128]{2,1,0:T(8,128)(2,1)} %gather.9), calls=%async_computation.2 | async-start | bytes 2097152 | tf_op jit(solution)/shard_map/all_to_all | solution.py:527
  57.5 7.5 %copy-start.4 = (s32[128]{0:T(128)S(1)}, s32[128]{0:T(128)}, u32[]{:S(2)}) copy-start(s32[128]{0:T(128)} %param.17) | copy-start | bytes 1540
  57.5 7.5 %copy-start.1 = (bf16[32,128,128]{2,1,0:T(8,128)(2,1)}, bf16[32,128,128]{2,1,0:T(8,128)(2,1)S(1)}, u32[]{:S(2)}) copy-start(bf16[32,128,128]{2,1,0:T(8,128)(2,1)S(1)} %all-to-all-done.2.got_ref) | copy-start | bytes 3145732
  57.5 44.6 %all-to-all-start.1 = ((bf16[32,384,128]{2,1,0:T(8,128)(2,1)}), bf16[32,384,128]{2,1,0:T(8,128)(2,1)}, u32[]{:S(2)}, u32[]{:S(2)}) async-start(bf16[32,384,128]{2,1,0:T(8,128)(2,1)} %gather.8), calls=%async_computation.1 | async-start | bytes 6291456 | tf_op jit(solution)/shard_map/all_to_all | solution.py:527
  64.9 121.0 %all-gather.6.cloned.1.call-start = ((), (), s32[]{:S(2)}) async-start(), calls=%async_computation.6 | async-start | bytes 8650752 | tf_op jit(solution)/shard_map/all_gather | solution.py:587
  65.7 4.1 %collective-permute-start.2 = (s32[32,4,128]{2,1,0:T(4,128)S(1)}, s32[32,4,128]{2,1,0:T(4,128)S(1)}, u32[]{:S(2)}, u32[]{:S(2)}) collective-permute-start(s32[32,4,128]{2,1,0:T(4,128)S(1)} %all_to_all.25), channel_id=1, source_target_pairs={{0,96},{32,0},{64,32},{96,64},{1,97},{33,1},{65,33},{97,65},{2,98}... | collective-permute-start | bytes 196616 | tf_op jit(solution)/shard_map/ppermute | solution.py:489
  68.5 5.0 %collective-permute-start.1 = (s32[32,4,128]{2,1,0:T(4,128)S(1)}, s32[32,4,128]{2,1,0:T(4,128)S(1)}, u32[]{:S(2)}, u32[]{:S(2)}) collective-permute-start(s32[32,4,128]{2,1,0:T(4,128)S(1)} %all_to_all.25), channel_id=1, source_target_pairs={{0,64},{32,96},{64,0},{96,32},{1,65},{33,97},{65,1},{97,33},{2,66}... | collective-permute-start | bytes 196616 | tf_op jit(solution)/shard_map/ppermute | solution.py:489
  68.8 6.1 %collective-permute-start = (s32[32,4,128]{2,1,0:T(4,128)S(1)}, s32[32,4,128]{2,1,0:T(4,128)S(1)}, u32[]{:S(2)}, u32[]{:S(2)}) collective-permute-start(s32[32,4,128]{2,1,0:T(4,128)S(1)} %all_to_all.25), channel_id=1, source_target_pairs={{0,32},{32,64},{64,96},{96,0},{1,33},{33,65},{65,97},{97,1},{2,34}... | collective-permute-start | bytes 196616 | tf_op jit(solution)/shard_map/ppermute | solution.py:489
  117.2 5.1 %collective-permute-start.3 = (bf16[128,256]{1,0:T(8,128)(2,1)}, bf16[128,256]{1,0:T(8,128)(2,1)S(1)}, u32[]{:S(2)}, u32[]{:S(2)}) collective-permute-start(bf16[128,256]{1,0:T(8,128)(2,1)} %get-tuple-element.34), channel_id=1, source_target_pairs={{0,32},{32,64},{64,96},{96,0},{1,33},{33,65},{65,97},{97,1},{2,34}... | collective-permute-start | bytes 196616 | tf_op jit(solution)/shard_map/ppermute | solution.py:489
  118.5 5.3 %collective-permute-start.4 = (bf16[128,256]{1,0:T(8,128)(2,1)}, bf16[128,256]{1,0:T(8,128)(2,1)S(1)}, u32[]{:S(2)}, u32[]{:S(2)}) collective-permute-start(bf16[128,256]{1,0:T(8,128)(2,1)} %get-tuple-element.35), channel_id=1, source_target_pairs={{0,64},{32,96},{64,0},{96,32},{1,65},{33,97},{65,1},{97,33},{2,66}... | collective-permute-start | bytes 196616 | tf_op jit(solution)/shard_map/ppermute | solution.py:489
  121.2 3.8 %collective-permute-start.5 = (bf16[128,256]{1,0:T(8,128)(2,1)}, bf16[128,256]{1,0:T(8,128)(2,1)S(1)}, u32[]{:S(2)}, u32[]{:S(2)}) collective-permute-start(bf16[128,256]{1,0:T(8,128)(2,1)} %get-tuple-element.36), channel_id=1, source_target_pairs={{0,96},{32,0},{64,32},{96,64},{1,97},{33,1},{65,33},{97,65},{2,98}... | collective-permute-start | bytes 196616 | tf_op jit(solution)/shard_map/ppermute | solution.py:489
  126.6 106.9 %all-gather.4.cloned.1.call-start = ((), (), s32[]{:S(2)}) async-start(), calls=%async_computation.5 | async-start | bytes 2162688 | tf_op jit(solution)/shard_map/all_gather | solution.py:590
  154.2 30.0 %copy-start.3 = (s32[32,8]{0,1:T(8,128)S(1)}, s32[32,8]{0,1:T(8,128)}, u32[]{:S(2)}) copy-start(s32[32,8]{0,1:T(8,128)} %param.16) | copy-start | bytes 3076
  177.8 3.1 %collective-permute-start.9 = (bf16[8,1024]{1,0:T(8,128)(2,1)S(1)}, bf16[8,1024]{1,0:T(8,128)(2,1)S(1)}, u32[]{:S(2)}, u32[]{:S(2)}) collective-permute-start(bf16[8,1024]{1,0:T(8,128)(2,1)S(1)} %reduce_sum.45), channel_id=1, source_target_pairs={{0,96},{32,0},{64,32},{96,64},{1,97},{33,1},{65,33},{97,65},{2,98}... | collective-permute-start | bytes 49160 | tf_op jit(solution)/shard_map/ppermute | solution.py:489
  178.8 4.7 %collective-permute-start.11 = (bf16[8,1024]{1,0:T(8,128)(2,1)S(1)}, bf16[8,1024]{1,0:T(8,128)(2,1)S(1)}, u32[]{:S(2)}, u32[]{:S(2)}) collective-permute-start(bf16[8,1024]{1,0:T(8,128)(2,1)S(1)} %reduce_sum.45), channel_id=1, source_target_pairs={{0,32},{32,64},{64,96},{96,0},{1,33},{33,65},{65,97},{97,1},{2,34}... | collective-permute-start | bytes 49160 | tf_op jit(solution)/shard_map/ppermute | solution.py:489
  179.3 4.1 %collective-permute-start.10 = (bf16[8,1024]{1,0:T(8,128)(2,1)S(1)}, bf16[8,1024]{1,0:T(8,128)(2,1)S(1)}, u32[]{:S(2)}, u32[]{:S(2)}) collective-permute-start(bf16[8,1024]{1,0:T(8,128)(2,1)S(1)} %reduce_sum.45), channel_id=1, source_target_pairs={{0,64},{32,96},{64,0},{96,32},{1,65},{33,97},{65,1},{97,33},{2,66}... | collective-permute-start | bytes 49160 | tf_op jit(solution)/shard_map/ppermute | solution.py:489
  186.0 46.8 %copy-start.2 = (f32[128,1]{1,0:T(8,128)S(1)}, f32[128,1]{1,0:T(8,128)}, u32[]{:S(2)}) copy-start(f32[128,1]{1,0:T(8,128)} %get-tuple-element.40) | copy-start | bytes 1540
  228.3 14.8 %collective-permute-start.8 = (bf16[2,1024,128]{2,1,0:T(8,128)(2,1)}, bf16[2,1024,128]{2,1,0:T(8,128)(2,1)S(1)}, u32[]{:S(2)}, u32[]{:S(2)}) collective-permute-start(bf16[2,1024,128]{2,1,0:T(8,128)(2,1)} %bitcast.20), channel_id=1, source_target_pairs={{0,96},{32,0},{64,32},{96,64},{1,97},{33,1},{65,33},{97,65},{2,98}... | collective-permute-start | bytes 1572872 | tf_op jit(solution)/shard_map/ppermute | solution.py:489
  230.6 14.5 %collective-permute-start.7 = (bf16[2,1024,128]{2,1,0:T(8,128)(2,1)}, bf16[2,1024,128]{2,1,0:T(8,128)(2,1)S(1)}, u32[]{:S(2)}, u32[]{:S(2)}) collective-permute-start(bf16[2,1024,128]{2,1,0:T(8,128)(2,1)} %bitcast.21), channel_id=1, source_target_pairs={{0,64},{32,96},{64,0},{96,32},{1,65},{33,97},{65,1},{97,33},{2,66}... | collective-permute-start | bytes 1572872 | tf_op jit(solution)/shard_map/ppermute | solution.py:489
  231.3 26.1 %collective-permute-start.6 = (bf16[2,1024,128]{2,1,0:T(8,128)(2,1)}, bf16[2,1024,128]{2,1,0:T(8,128)(2,1)S(1)}, u32[]{:S(2)}, u32[]{:S(2)}) collective-permute-start(bf16[2,1024,128]{2,1,0:T(8,128)(2,1)} %bitcast.22), channel_id=1, source_target_pairs={{0,32},{32,64},{64,96},{96,0},{1,33},{33,65},{65,97},{97,1},{2,34}... | collective-permute-start | bytes 1572872 | tf_op jit(solution)/shard_map/ppermute | solution.py:489
  233.4 24.0 %copy-start = (bf16[2048,128]{1,0:T(8,128)(2,1)S(1)}, bf16[2048,128]{1,0:T(8,128)(2,1)}, u32[]{:S(2)}) copy-start(bf16[2048,128]{1,0:T(8,128)(2,1)} %scatter.1) | copy-start | bytes 1572868
Sparse Core Ops, SparseCore 0:
  126.7 59.2 all-gather.5
  188.8 43.0 all-gather.3

commit v6 on v5

--- a/solution.py
+++ b/solution.py
@@ -267,7 +267,9 @@
     *refs,
 ):
     grad_refs = refs[:REPS]
-    pooled_ref, cross_w, deep_w, start_ref, cross_t, deep_t, gx_ref, sems, result_ref = refs[REPS:]
+    pooled_ref, cross_w, deep_w, start_ref, cross_t, deep_t, deep_s, gx_ref, sems, result_ref = refs[
+        REPS:
+    ]
     step = pl.program_id(0)
 
     def cross_copy(layer):
@@ -303,7 +305,9 @@
             deep_copy(layer).wait()
             product = dot(current, deep_w[layer]) + dbias_ref[layer : layer + 1, :]
             deep_t[layer] = product
-            current = (product * sigmoid(product)).astype(BF)
+            sig = sigmoid(product)
+            deep_s[layer] = sig
+            current = (product * sig).astype(BF)
         out_w = out_w_ref[...]
         logits = jnp.sum(current.astype(F32) * out_w, axis=1, keepdims=True)
         logits_ref[...] = logits
@@ -311,7 +315,7 @@
         grad = error * out_w
         for layer in (2, 1, 0):
             product = deep_t[layer]
-            sig = sigmoid(product)
+            sig = deep_s[layer]
             masked = (grad * sig * (1.0 + product * (1.0 - sig))).astype(BF)
             grad = dot(masked, deep_w[layer], NT)
         gx_ref[...] = jnp.zeros_like(gx_ref)
@@ -370,6 +374,7 @@
             pltpu.VMEM((3, WIDTH, WIDTH), BF),
             pltpu.VMEM((3, WIDTH, WIDTH), BF),
             pltpu.VMEM((SAMPLES, WIDTH), BF),
+            pltpu.VMEM((3, SAMPLES, WIDTH), F32),
             pltpu.VMEM((3, SAMPLES, WIDTH), F32),
             pltpu.VMEM((3, SAMPLES, WIDTH), F32),
             pltpu.VMEM((SAMPLES, WIDTH), F32),
@@ -450,36 +455,41 @@
     )(first, trips, words, grads)
 
 
-def finish_kernel(place_ref, *refs):
-    parts, out, wide, sems = refs[:REPS], refs[REPS], refs[REPS + 1], refs[REPS + 2]
+def finish_kernel(count, place_ref, *refs):
+    blocks, (out, wide, sems) = refs[:count], refs[-3:]
     copies = []
-    for k in range(REPS):
-        for f in range(PAIR):
-            n = k * PAIR + f
-            wide[n] = parts[k][f].astype(F32)
+    n = 0
+    for block in blocks:
+        for f in range(block.shape[0]):
+            wide[n] = block[f].astype(F32)
             to = pl.multiple_of(place_ref[n] * VOC, VOC)
             copies.append(
                 pltpu.make_async_copy(wide.at[n], out.at[pl.ds(to, VOC), :], sems.at[n])
             )
             copies[-1].start()
+            n += 1
     for copy in copies:
         copy.wait()
 
 
-def finish_call(places, parts):
+def finish_call(places, blocks, earlier=None):
+    more = [] if earlier is None else [earlier]
+    total = sum(block.shape[0] for block in blocks)
     return pl.pallas_call(
-        finish_kernel,
+        functools.partial(finish_kernel, len(blocks)),
         out_shape=jax.ShapeDtypeStruct((ROWS, EMB), F32),
         in_specs=[pl.BlockSpec(memory_space=pltpu.SMEM)]
-        + [pl.BlockSpec(memory_space=pltpu.VMEM) for _ in parts],
+        + [pl.BlockSpec(memory_space=pltpu.VMEM) for _ in blocks]
+        + [pl.BlockSpec(memory_space=pl.ANY) for _ in more],
         out_specs=pl.BlockSpec(memory_space=pl.ANY),
         scratch_shapes=[
-            pltpu.VMEM((FEATS, VOC, EMB), F32),
-            pltpu.SemaphoreType.DMA((FEATS,)),
-        ],
+            pltpu.VMEM((total, VOC, EMB), F32),
+            pltpu.SemaphoreType.DMA((total,)),
+        ],
+        input_output_aliases={1 + len(blocks): 0} if more else {},
         compiler_params=pltpu.CompilerParams(vmem_limit_bytes=16 * 1024 * 1024),
         name="finish",
-    )(places, *parts)
+    )(places, *blocks, *more)
 
 
 def from_before(x, axis, k):
@@ -592,11 +602,19 @@
     ).astype(F32)
 
     part = scatter_call(words, first_word, trips, all_grads).reshape(PAIR, VOC, EMB)
-    parts = [part] + [from_before(part, "rep", k) for k in range(1, REPS)]
+    before = from_before(part, "rep", 1)
+    after = from_before(part, "rep", REPS - 1)
+    across = [
+        from_before(before[:1], "rep", 1),
+        from_before(after[1:], "rep", REPS - 1),
+    ]
     slots = feature_slot[lax.axis_index("shard")]
-    holder = (rep - jnp.arange(REPS, dtype=I32)) % REPS
+    holder = (rep - jnp.array([0, 1, 3, 2], I32)) % REPS
     features = holder[:, None] * PAIR + jnp.arange(PAIR, dtype=I32)[None, :]
-    row_grad = finish_call(slots[features.reshape(-1)], parts)
+    places = slots[features.reshape(-1)]
+    near, far = places[: 3 * PAIR], places[3 * PAIR :]
+    row_grad = finish_call(near, [part, before, after])
+    row_grad = finish_call(far, across, row_grad)
     return (row_grad, first_grad, logits.reshape(SAMPLES))
 
 

time: 268 us -> 265 us (0.989)
  the two profiles are of different devices: /device:TPU:71 before, /device:TPU:38 now
where the time goes in v6:
time: 265 us; the launch traced here: 260 us
  Pallas kernels  94.7 us (36%)
  blocking collectives  63.5 us (24%)
  waiting for transfers between devices  41.1 us (16%)
  starting transfers between devices  32.9 us (12%)
  between operations  14.2 us (5%)
  other arithmetic  9.01 us (3%)
  local copies, waits for them, and re-layouts  4.76 us (2%)
    all_to_all x2, blocking collectives, exchange(): return lax.all_to_all(x, axis, split_axis=0, concat_axis=0, tiled=True)  50.8 us
    pallas_call x1, Pallas kernels, scatter_call(): pl.pallas_call(scatter_kernel, out_shape=jax.ShapeDtypeStruct((rows, EMB)...  41.9 us
    ppermute x13, waiting for transfers between devices, from_before(): return lax.ppermute(x, axis, [(i, (i + k) % n) for i in range(n)])  22.5 us
    pallas_call x2, Pallas kernels, gather_call(): pl.pallas_call(functools.partial(gather_kernel, offset), out_shape=jax.Sh...  21.2 us
    ppermute x13, starting transfers between devices, from_before(): return lax.ppermute(x, axis, [(i, (i + k) % n) for i in range(n)])  18.6 us
    all_to_all x2, waiting for transfers between devices, exchange(): return lax.all_to_all(x, axis, split_axis=0, concat_axis=0, tiled=True)  18.5 us
    pallas_call x1, Pallas kernels, tower_call(): pl.pallas_call(functools.partial(tower_kernel, CAP - got.shape[1]), grid=...  15.1 us
    all_to_all x2, starting transfers between devices, exchange(): return lax.all_to_all(x, axis, split_axis=0, concat_axis=0, tiled=True)  14.2 us
  transfers between devices with their start and end apart: 17, of which 11 were waited for; matrix products, arithmetic and copies ran while one was open for 4% of the time, Pallas kernels for 24%

profile of v6, /device:TPU:38, one launch (start us, length us, event | category | flops | bytes accessed | tf_op | source)
XLA Modules:
  0.0 260.1 jit_solution(7036986689893415300)
XLA Ops:
  7.2 9.1 %index.1 = (s32[32,512]{1,0:T(8,128)}, s32[32,4,128]{2,1,0:T(4,128)}) custom-call(s32[1,8192]{1,0:T(1,128)} %ids_in.1, s32[1,8192]{1,0:T(1,128)} %bitcast.37, s32[1,1024]{1,0:T(1,128)} %len_in.1, s32[8,32]{1,0:T(8,128)} %bitcast.38), custom_call_target="tpu_custom_call" | custom-call | tf_op jit(solution)/shard_map/index/pallas_call | solution.py:144
  16.3 12.7 %all_to_all.25 = s32[32,4,128]{2,1,0:T(4,128)S(1)} all-to-all(s32[32,4,128]{2,1,0:T(4,128)} %get-tuple-element.22), channel_id=1, replica_groups=mesh['rep'=4,'shard'=32] {'shard'}, dimensions={0} | all-to-all | bytes 131072 | tf_op jit(solution)/shard_map/all_to_all | solution.py:533
  29.6 6.6 %gather.9 = bf16[32,128,128]{2,1,0:T(8,128)(2,1)} custom-call(s32[16384]{0:T(1024)} %bitcast.28, bf16[8192,128]{1,0:T(8,128)(2,1)} %table_ref.3), custom_call_target="tpu_custom_call" | custom-call | tf_op jit(solution)/shard_map/gather/pallas_call | solution.py:185
  36.2 6.8 %all-to-all-start.2 = ((bf16[32,128,128]{2,1,0:T(8,128)(2,1)}), bf16[32,128,128]{2,1,0:T(8,128)(2,1)S(1)}, u32[]{:S(2)}, u32[]{:S(2)}) async-start(bf16[32,128,128]{2,1,0:T(8,128)(2,1)} %gather.9), calls=%async_computation.2 | async-start | bytes 2097152 | tf_op jit(solution)/shard_map/all_to_all | solution.py:537
  43.0 14.6 %gather.8 = bf16[32,384,128]{2,1,0:T(8,128)(2,1)} custom-call(s32[16384]{0:T(1024)} %bitcast.29, bf16[8192,128]{1,0:T(8,128)(2,1)} %table_ref.3), custom_call_target="tpu_custom_call" | custom-call | tf_op jit(solution)/shard_map/gather/pallas_call | solution.py:185
  57.6 7.4 %all-to-all-start.1 = ((bf16[32,384,128]{2,1,0:T(8,128)(2,1)}), bf16[32,384,128]{2,1,0:T(8,128)(2,1)}, u32[]{:S(2)}, u32[]{:S(2)}) async-start(bf16[32,384,128]{2,1,0:T(8,128)(2,1)} %gather.8), calls=%async_computation.1 | async-start | bytes 6291456 | tf_op jit(solution)/shard_map/all_to_all | solution.py:537
  65.8 3.0 %collective-permute-start.2 = (s32[32,4,128]{2,1,0:T(4,128)S(1)}, s32[32,4,128]{2,1,0:T(4,128)S(1)}, u32[]{:S(2)}, u32[]{:S(2)}) collective-permute-start(s32[32,4,128]{2,1,0:T(4,128)S(1)} %all_to_all.25), channel_id=1, source_target_pairs={{0,96},{32,0},{64,32},{96,64},{1,97},{33,1},{65,33},{97,65},{2,98}... | collective-permute-start | bytes 196616 | tf_op jit(solution)/shard_map/ppermute | solution.py:499
  72.0 3.0 %collective-permute-done.1 = s32[32,4,128]{2,1,0:T(4,128)S(1)} collective-permute-done((s32[32,4,128]{2,1,0:T(4,128)S(1)}, s32[32,4,128]{2,1,0:T(4,128)S(1)}, u32[]{:S(2)}, u32[]{:S(2)}) %collective-permute-start.1) | collective-permute-done | bytes 65568 | tf_op jit(solution)/shard_map/ppermute | solution.py:499
  79.5 3.6 %pool.1.earlier_ref = f32[128,1024]{1,0:T(8,128)} custom-call(bf16[32,128,128]{2,1,0:T(8,128)(2,1)} %copy-done.1, s32[32,512]{1,0:T(8,128)} %get-tuple-element.26.packed_ref), custom_call_target="tpu_custom_call" | custom-call | tf_op jit(solution)/shard_map/pool/pallas_call | solution.py:234
  83.0 18.5 %all-to-all-done.1.got_ref = bf16[32,384,128]{2,1,0:T(8,128)(2,1)} async-done(((bf16[32,384,128]{2,1,0:T(8,128)(2,1)}), bf16[32,384,128]{2,1,0:T(8,128)(2,1)}, u32[]{:S(2)}, u32[]{:S(2)}) %all-to-all-start.1) | async-done | bytes 3145760 | tf_op jit(solution)/shard_map/all_to_all | solution.py:537
  101.6 15.1 %tower.1 = (f32[128,1]{1,0:T(8,128)}, bf16[4,256,1024]{2,1,0:T(8,128)(2,1)}, bf16[128,256]{1,0:T(8,128)(2,1)}, bf16[128,256]{1,0:T(8,128)(2,1)}, bf16[128,256]{1,0:T(8,128)(2,1)}, /*index=5*/bf16[128,256]{1,0:T(8,128)(2,1)}) custom-call(s32[1]{0:T(128)} %bitcast.8.rep_ref, bf16[32,384,128]{2,1,0:T(8,128)(2,1)} %all-to-all-done.1.got_ref, ...), custom_call_target="tpu_custom_call" | custom-call | tf_op jit(solution)/shard_map/tower/pallas_call | solution.py:346
  116.7 3.1 %collective-permute-start.5 = (bf16[128,256]{1,0:T(8,128)(2,1)}, bf16[128,256]{1,0:T(8,128)(2,1)S(1)}, u32[]{:S(2)}, u32[]{:S(2)}) collective-permute-start(bf16[128,256]{1,0:T(8,128)(2,1)} %get-tuple-element.36), channel_id=1, source_target_pairs={{0,96},{32,0},{64,32},{96,64},{1,97},{33,1},{65,33},{97,65},{2,98}... | collective-permute-start | bytes 196616 | tf_op jit(solution)/shard_map/ppermute | solution.py:499
  121.3 1.8 collective-permute-done.5
  123.2 2.9 %collective-permute-done.4 = bf16[128,256]{1,0:T(8,128)(2,1)S(1)} collective-permute-done((bf16[128,256]{1,0:T(8,128)(2,1)}, bf16[128,256]{1,0:T(8,128)(2,1)S(1)}, u32[]{:S(2)}, u32[]{:S(2)}) %collective-permute-start.4) | collective-permute-done | bytes 65568 | tf_op jit(solution)/shard_map/ppermute | solution.py:499
  126.7 1.6 pad_maximum_fusion
  128.3 29.6 %all_to_all.26 = bf16[4,256,1024]{2,1,0:T(8,128)(2,1)S(1)} all-to-all(bf16[4,256,1024]{2,1,0:T(8,128)(2,1)} %get-tuple-element.39), channel_id=1, replica_groups=mesh['rep'=4,'shard'=32] {'rep'}, dimensions={0} | all-to-all | bytes 4194304 | tf_op jit(solution)/shard_map/all_to_all | solution.py:537
  158.4 21.2 %all_to_all.27 = bf16[32,8,1024]{2,1,0:T(8,128)(2,1)S(1)} all-to-all(bf16[32,8,1024]{2,1,0:T(8,128)(2,1)S(1)} %bitcast.26), channel_id=1, replica_groups=mesh['rep'=4,'shard'=32] {'shard'}, dimensions={0} | all-to-all | bytes 1048576 | tf_op jit(solution)/shard_map/all_to_all | solution.py:537
  183.5 2.8 %collective-permute-done.11 = bf16[8,1024]{1,0:T(8,128)(2,1)S(1)} collective-permute-done((bf16[8,1024]{1,0:T(8,128)(2,1)S(1)}, bf16[8,1024]{1,0:T(8,128)(2,1)S(1)}, u32[]{:S(2)}, u32[]{:S(2)}) %collective-permute-start.11) | collective-permute-done | bytes 16416 | tf_op jit(solution)/shard_map/ppermute | solution.py:499
  188.1 41.9 %scatter.1 = bf16[2048,128]{1,0:T(8,128)(2,1)} custom-call(s32[128]{0:T(128)} %add.93.first_ref, s32[128]{0:T(128)} %reshape.93.trips_ref, s32[73728]{0:T(1024)} %reshape.84.word_ref, bf16[32,4,128,256]{3,2,1,0:T(8,128)(2,1)} %bitcast.25), custom_call_target="tpu_custom_call" | custom-call | tf_op jit(solution)/shard_map/scatter/pallas_call | solution.py:435
  230.0 3.2 %collective-permute-start.8 = (bf16[2,1024,128]{2,1,0:T(8,128)(2,1)}, bf16[2,1024,128]{2,1,0:T(8,128)(2,1)S(1)}, u32[]{:S(2)}, u32[]{:S(2)}) collective-permute-start(bf16[2,1024,128]{2,1,0:T(8,128)(2,1)} %bitcast.22), channel_id=1, source_target_pairs={{0,96},{32,0},{64,32},{96,64},{1,97},{33,1},{65,33},{97,65},{2,98}... | collective-permute-start | bytes 1572872 | tf_op jit(solution)/shard_map/ppermute | solution.py:499
  233.5 7.0 %collective-permute-done.6.refs_1_ = bf16[2,1024,128]{2,1,0:T(8,128)(2,1)S(1)} collective-permute-done((bf16[2,1024,128]{2,1,0:T(8,128)(2,1)}, bf16[2,1024,128]{2,1,0:T(8,128)(2,1)S(1)}, u32[]{:S(2)}, u32[]{:S(2)}) %collective-permute-start.6) | collective-permute-done | bytes 524320 | tf_op jit(solution)/shard_map/ppermute | solution.py:499
  240.7 3.3 %collective-permute-start.9 = (bf16[1,1024,128]{2,1,0:T(8,128)(2,1)S(1)}, bf16[1,1024,128]{2,1,0:T(8,128)(2,1)S(1)}, u32[]{:S(2)}, u32[]{:S(2)}) collective-permute-start(bf16[1,1024,128]{2,1,0:T(8,128)(2,1)S(1)} %slice.19), channel_id=1, source_target_pairs={{0,96},{32,0},{64,32},{96,64},{1,97},{33,1},{65,33},{97,65},{2,98}... | collective-permute-start | bytes 786440 | tf_op jit(solution)/shard_map/ppermute | solution.py:499
  245.3 4.1 %convert_element_type.15 = f32[1024,1024]{1,0:T(8,128)} convert(bf16[1024,1024]{1,0:T(8,128)(2,1)} %all-gather.4.cloned.1.call-done) | non-fusion elementwise | flops 1048576 | bytes 6291456 | tf_op jit(solution)/shard_map/convert_element_type | solution.py:602
  249.4 2.3 finish.2.refs_2_
  (67 shorter events, 20.8 us)
Async XLA Ops:
  36.2 21.3 %all-to-all-start.2 = ((bf16[32,128,128]{2,1,0:T(8,128)(2,1)}), bf16[32,128,128]{2,1,0:T(8,128)(2,1)S(1)}, u32[]{:S(2)}, u32[]{:S(2)}) async-start(bf16[32,128,128]{2,1,0:T(8,128)(2,1)} %gather.9), calls=%async_computation.2 | async-start | bytes 2097152 | tf_op jit(solution)/shard_map/all_to_all | solution.py:537
  57.6 7.5 %copy-start.4 = (s32[128]{0:T(128)S(1)}, s32[128]{0:T(128)}, u32[]{:S(2)}) copy-start(s32[128]{0:T(128)} %param.18) | copy-start | bytes 1540
  57.6 21.9 %copy-start.1 = (bf16[32,128,128]{2,1,0:T(8,128)(2,1)}, bf16[32,128,128]{2,1,0:T(8,128)(2,1)S(1)}, u32[]{:S(2)}) copy-start(bf16[32,128,128]{2,1,0:T(8,128)(2,1)S(1)} %all-to-all-done.2.got_ref) | copy-start | bytes 3145732
  57.6 44.0 %all-to-all-start.1 = ((bf16[32,384,128]{2,1,0:T(8,128)(2,1)}), bf16[32,384,128]{2,1,0:T(8,128)(2,1)}, u32[]{:S(2)}, u32[]{:S(2)}) async-start(bf16[32,384,128]{2,1,0:T(8,128)(2,1)} %gather.8), calls=%async_computation.1 | async-start | bytes 6291456 | tf_op jit(solution)/shard_map/all_to_all | solution.py:537
  65.0 123.0 %all-gather.6.cloned.1.call-start = ((), (), s32[]{:S(2)}) async-start(), calls=%async_computation.6 | async-start | bytes 8650752 | tf_op jit(solution)/shard_map/all_gather | solution.py:597
  65.8 6.2 %collective-permute-start.2 = (s32[32,4,128]{2,1,0:T(4,128)S(1)}, s32[32,4,128]{2,1,0:T(4,128)S(1)}, u32[]{:S(2)}, u32[]{:S(2)}) collective-permute-start(s32[32,4,128]{2,1,0:T(4,128)S(1)} %all_to_all.25), channel_id=1, source_target_pairs={{0,96},{32,0},{64,32},{96,64},{1,97},{33,1},{65,33},{97,65},{2,98}... | collective-permute-start | bytes 196616 | tf_op jit(solution)/shard_map/ppermute | solution.py:499
  68.9 6.1 %collective-permute-start.1 = (s32[32,4,128]{2,1,0:T(4,128)S(1)}, s32[32,4,128]{2,1,0:T(4,128)S(1)}, u32[]{:S(2)}, u32[]{:S(2)}) collective-permute-start(s32[32,4,128]{2,1,0:T(4,128)S(1)} %all_to_all.25), channel_id=1, source_target_pairs={{0,64},{32,96},{64,0},{96,32},{1,65},{33,97},{65,1},{97,33},{2,66}... | collective-permute-start | bytes 196616 | tf_op jit(solution)/shard_map/ppermute | solution.py:499
  69.5 6.1 %collective-permute-start = (s32[32,4,128]{2,1,0:T(4,128)S(1)}, s32[32,4,128]{2,1,0:T(4,128)S(1)}, u32[]{:S(2)}, u32[]{:S(2)}) collective-permute-start(s32[32,4,128]{2,1,0:T(4,128)S(1)} %all_to_all.25), channel_id=1, source_target_pairs={{0,32},{32,64},{64,96},{96,0},{1,33},{33,65},{65,97},{97,1},{2,34}... | collective-permute-start | bytes 196616 | tf_op jit(solution)/shard_map/ppermute | solution.py:499
  116.7 6.5 %collective-permute-start.5 = (bf16[128,256]{1,0:T(8,128)(2,1)}, bf16[128,256]{1,0:T(8,128)(2,1)S(1)}, u32[]{:S(2)}, u32[]{:S(2)}) collective-permute-start(bf16[128,256]{1,0:T(8,128)(2,1)} %get-tuple-element.36), channel_id=1, source_target_pairs={{0,96},{32,0},{64,32},{96,64},{1,97},{33,1},{65,33},{97,65},{2,98}... | collective-permute-start | bytes 196616 | tf_op jit(solution)/shard_map/ppermute | solution.py:499
  119.7 6.3 %collective-permute-start.4 = (bf16[128,256]{1,0:T(8,128)(2,1)}, bf16[128,256]{1,0:T(8,128)(2,1)S(1)}, u32[]{:S(2)}, u32[]{:S(2)}) collective-permute-start(bf16[128,256]{1,0:T(8,128)(2,1)} %get-tuple-element.35), channel_id=1, source_target_pairs={{0,64},{32,96},{64,0},{96,32},{1,65},{33,97},{65,1},{97,33},{2,66}... | collective-permute-start | bytes 196616 | tf_op jit(solution)/shard_map/ppermute | solution.py:499
  120.4 6.3 %collective-permute-start.3 = (bf16[128,256]{1,0:T(8,128)(2,1)}, bf16[128,256]{1,0:T(8,128)(2,1)S(1)}, u32[]{:S(2)}, u32[]{:S(2)}) collective-permute-start(bf16[128,256]{1,0:T(8,128)(2,1)} %get-tuple-element.34), channel_id=1, source_target_pairs={{0,32},{32,64},{64,96},{96,0},{1,33},{33,65},{65,97},{97,1},{2,34}... | collective-permute-start | bytes 196616 | tf_op jit(solution)/shard_map/ppermute | solution.py:499
  128.3 117.1 %all-gather.4.cloned.1.call-start = ((), (), s32[]{:S(2)}) async-start(), calls=%async_computation.5 | async-start | bytes 2162688 | tf_op jit(solution)/shard_map/all_gather | solution.py:600
  179.7 3.8 %collective-permute-start.10 = (bf16[8,1024]{1,0:T(8,128)(2,1)S(1)}, bf16[8,1024]{1,0:T(8,128)(2,1)S(1)}, u32[]{:S(2)}, u32[]{:S(2)}) collective-permute-start(bf16[8,1024]{1,0:T(8,128)(2,1)S(1)} %reduce_sum.45), channel_id=1, source_target_pairs={{0,96},{32,0},{64,32},{96,64},{1,97},{33,1},{65,33},{97,65},{2,98}... | collective-permute-start | bytes 49160 | tf_op jit(solution)/shard_map/ppermute | solution.py:499
  180.9 5.4 %collective-permute-start.11 = (bf16[8,1024]{1,0:T(8,128)(2,1)S(1)}, bf16[8,1024]{1,0:T(8,128)(2,1)S(1)}, u32[]{:S(2)}, u32[]{:S(2)}) collective-permute-start(bf16[8,1024]{1,0:T(8,128)(2,1)S(1)} %reduce_sum.45), channel_id=1, source_target_pairs={{0,64},{32,96},{64,0},{96,32},{1,65},{33,97},{65,1},{97,33},{2,66}... | collective-permute-start | bytes 49160 | tf_op jit(solution)/shard_map/ppermute | solution.py:499
  182.4 4.9 %collective-permute-start.12 = (bf16[8,1024]{1,0:T(8,128)(2,1)S(1)}, bf16[8,1024]{1,0:T(8,128)(2,1)S(1)}, u32[]{:S(2)}, u32[]{:S(2)}) collective-permute-start(bf16[8,1024]{1,0:T(8,128)(2,1)S(1)} %reduce_sum.45), channel_id=1, source_target_pairs={{0,32},{32,64},{64,96},{96,0},{1,33},{33,65},{65,97},{97,1},{2,34}... | collective-permute-start | bytes 49160 | tf_op jit(solution)/shard_map/ppermute | solution.py:499
  188.1 45.1 %copy-start.3 = (s32[32,8]{0,1:T(8,128)S(1)}, s32[32,8]{0,1:T(8,128)}, u32[]{:S(2)}) copy-start(s32[32,8]{0,1:T(8,128)} %param.17) | copy-start | bytes 3076
  188.1 45.3 %copy-start.5 = (s32[4]{0:T(128)S(1)}, s32[4]{0:T(128)}, u32[]{:S(2)}) copy-start(s32[4]{0:T(128)} %constant.84) | copy-start | bytes 52
  188.1 56.6 %copy-start.2 = (f32[128,1]{1,0:T(8,128)S(1)}, f32[128,1]{1,0:T(8,128)}, u32[]{:S(2)}) copy-start(f32[128,1]{1,0:T(8,128)} %get-tuple-element.40) | copy-start | bytes 1540
  229.9 19.5 %copy-start = (bf16[2048,128]{1,0:T(8,128)(2,1)S(1)}, bf16[2048,128]{1,0:T(8,128)(2,1)}, u32[]{:S(2)}) copy-start(bf16[2048,128]{1,0:T(8,128)(2,1)} %scatter.1) | copy-start | bytes 1572868
  229.9 10.6 %collective-permute-start.6 = (bf16[2,1024,128]{2,1,0:T(8,128)(2,1)}, bf16[2,1024,128]{2,1,0:T(8,128)(2,1)S(1)}, u32[]{:S(2)}, u32[]{:S(2)}) collective-permute-start(bf16[2,1024,128]{2,1,0:T(8,128)(2,1)} %bitcast.21), channel_id=1, source_target_pairs={{0,32},{32,64},{64,96},{96,0},{1,33},{33,65},{65,97},{97,1},{2,34}... | collective-permute-start | bytes 1572872 | tf_op jit(solution)/shard_map/ppermute | solution.py:499
  230.0 10.7 %collective-permute-start.8 = (bf16[2,1024,128]{2,1,0:T(8,128)(2,1)}, bf16[2,1024,128]{2,1,0:T(8,128)(2,1)S(1)}, u32[]{:S(2)}, u32[]{:S(2)}) collective-permute-start(bf16[2,1024,128]{2,1,0:T(8,128)(2,1)} %bitcast.22), channel_id=1, source_target_pairs={{0,96},{32,0},{64,32},{96,64},{1,97},{33,1},{65,33},{97,65},{2,98}... | collective-permute-start | bytes 1572872 | tf_op jit(solution)/shard_map/ppermute | solution.py:499
  240.6 11.1 %collective-permute-start.7 = (bf16[1,1024,128]{2,1,0:T(8,128)(2,1)S(1)}, bf16[1,1024,128]{2,1,0:T(8,128)(2,1)S(1)}, u32[]{:S(2)}, u32[]{:S(2)}) collective-permute-start(bf16[1,1024,128]{2,1,0:T(8,128)(2,1)S(1)} %slice.18), channel_id=1, source_target_pairs={{0,32},{32,64},{64,96},{96,0},{1,33},{33,65},{65,97},{97,1},{2,34}... | collective-permute-start | bytes 786440 | tf_op jit(solution)/shard_map/ppermute | solution.py:499
  240.7 11.0 %collective-permute-start.9 = (bf16[1,1024,128]{2,1,0:T(8,128)(2,1)S(1)}, bf16[1,1024,128]{2,1,0:T(8,128)(2,1)S(1)}, u32[]{:S(2)}, u32[]{:S(2)}) collective-permute-start(bf16[1,1024,128]{2,1,0:T(8,128)(2,1)S(1)} %slice.19), channel_id=1, source_target_pairs={{0,96},{32,0},{64,32},{96,64},{1,97},{33,1},{65,33},{97,65},{2,98}... | collective-permute-start | bytes 786440 | tf_op jit(solution)/shard_map/ppermute | solution.py:499
Sparse Core Ops, SparseCore 0:
  128.4 57.2 all-gather.5
  188.5 43.0 all-gather.3
